TPU v7x, 32 devices: a whole 2x2x4 slice. The times are simulated.
32 devices in a mesh: groups: 2 (over x), tensor: 16 (over z, y, core).
Axes of the slice: x: 2, y: 2, z: 4, core: 2. Of those that a mesh axis runs over, the one named last changes fastest.
Arguments:
- encoded_query_rows: bfloat16 [256, 16384], P('groups', 'tensor'), parts along dimension 0, may hold values from -105 to 105
- encoded_key_rows: bfloat16 [256, 1024], P(('groups', 'tensor')), parts along dimension 0, may hold values from -4 to 4
- head_value_rows: bfloat16 [256, 1024], P(('groups', 'tensor')), parts along dimension 0, may hold values from -6 to 6
- quant_codes: int32 [256, 16384], P(('groups', 'tensor')), parts along dimension 0, may hold values from -127 to 127
- exponents: int32 [256, 128], P(('groups', 'tensor')), parts along dimension 0, may hold values from -10 to -7
- out_weight: bfloat16 [16384, 16384], P('tensor'), may hold values from -0.1875 to 0.1875
Outputs:
- next_residual: bfloat16 [256, 16384], P(('groups', 'tensor')), parts along dimension 0
There are 2 independent parts, one for each index of `groups`. A program takes and returns all parts, laid end to end along the dimension named above; an argument that names none is the same for every part. Nothing has to cross between parts.
Inputs may be any that keep to these rules, and one draw needn't show every extreme that they name: `quant_codes`: codes of the residual stream in the Hadamard-rotated basis, 128 features a block. `exponents`: one exponent for each token and block of 128 features.
All inputs are finite; a program needn't handle non-finite values.
Results may differ from a plain program's by a relative error of at most 0.0046.
Values may be sent and summed in bfloat16 or wider, within the bound.
No kernel may reach another device: no remote copies, remote signals or barrier semaphores. Data moves between devices by JAX's collectives and lax.ppermute only.
A program may use at most 128 MiB of HBM per device.

v0:
```python
import math

import jax
import jax.numpy as jnp
from jax import lax
from jax.sharding import PartitionSpec as P

QUERY_HEADS = 128
KEY_VALUE_HEADS = 8
HEAD_SIZE = 128
HBLK = 128


masked_score = -1e30


def passed_along(value, axis, steps):
    count = lax.axis_size(axis)
    pairs = [(source, (source + steps) % count) for source in range(count)]
    return lax.ppermute(value, axis, pairs)


def hadamard_table(order):
    index = jnp.arange(order, dtype=jnp.int32)
    common = index[:, None] & index[None, :]
    parity = jnp.zeros((order, order), jnp.int32)
    for shift_bits in range(max(order.bit_length() - 1, 1)):
        parity = parity + (common >> shift_bits & 1)
    return (1 - 2 * (parity % 2)).astype(jnp.float32)


def attend(state, packed, key_start, query_matrix, key_value_index):
    head_count = packed.shape[1]
    total_rows = query_matrix.shape[0]
    expanded_heads = packed.astype(jnp.float32)
    key_matrix = jnp.take(
        expanded_heads[0].reshape(head_count, KEY_VALUE_HEADS, HEAD_SIZE), key_value_index, axis=1
    )
    value_matrix = jnp.take(
        expanded_heads[1].reshape(head_count, KEY_VALUE_HEADS, HEAD_SIZE), key_value_index, axis=1
    )
    scores = jnp.einsum(
        "thd,chd->htc", query_matrix, key_matrix, precision=lax.Precision.HIGHEST
    ) * (1.0 / math.sqrt(HEAD_SIZE))
    key_index = key_start + jnp.arange(head_count, dtype=jnp.int32)
    query_index = jnp.arange(total_rows, dtype=jnp.int32)
    visible = key_index[None, :] <= query_index[:, None]
    scores = jnp.where(visible, scores, masked_score)
    top_old, total, weighted = state
    top_new = jnp.maximum(top_old, jnp.max(scores, axis=-1))
    factor = jnp.exp(top_old - top_new)
    weights = jnp.where(visible, jnp.exp(scores - top_new[..., None]), 0.0)
    total = total * factor + jnp.sum(weights, axis=-1)
    weighted = weighted * factor[..., None] + jnp.einsum(
        "htc,chd->htd", weights, value_matrix, precision=lax.Precision.HIGHEST
    )
    return (top_new, total, weighted)


def body(encoded_query_rows, encoded_key_rows, head_value_rows, quant_codes, exponents, out_weight):
    total_rows = encoded_query_rows.shape[0]
    local_heads = encoded_query_rows.shape[1] // HEAD_SIZE
    kv_count = encoded_key_rows.shape[0]
    rows = quant_codes.shape[0]
    devices = lax.axis_size("tensor")
    position = lax.axis_index("tensor")
    width = quant_codes.shape[1]
    query_group = QUERY_HEADS // KEY_VALUE_HEADS
    query_matrix = encoded_query_rows.astype(jnp.float32).reshape(
        total_rows, local_heads, HEAD_SIZE
    )
    key_value_index = (
        position * local_heads + jnp.arange(local_heads, dtype=jnp.int32)
    ) // query_group
    packed = jnp.stack([encoded_key_rows, head_value_rows])
    start_state = (
        jnp.full((local_heads, total_rows), masked_score, jnp.float32),
        jnp.zeros((local_heads, total_rows), jnp.float32),
        jnp.zeros((local_heads, total_rows, HEAD_SIZE), jnp.float32),
    )

    def advance(step, carried):
        held, state = carried
        source = (position - step) % devices
        state = attend(state, held, source * kv_count, query_matrix, key_value_index)
        held = passed_along(held, "tensor", 1)
        return (held, state)

    held, state = lax.fori_loop(0, devices - 1, advance, (packed, start_state))
    state = attend(state, held, (position + 1) % devices * kv_count, query_matrix, key_value_index)
    top, total, weighted = state
    context = weighted / total[..., None]
    context = (
        jnp.transpose(context, (1, 0, 2))
        .reshape(total_rows, local_heads * HEAD_SIZE)
        .astype(jnp.bfloat16)
    )
    summed = lax.psum_scatter(
        jnp.dot(context, out_weight, preferred_element_type=jnp.float32),
        "tensor",
        scatter_dimension=0,
        tiled=True,
    )
    table = hadamard_table(HBLK)
    rotated = jnp.dot(summed.reshape(-1, HBLK), table, precision=lax.Precision.HIGHEST).reshape(
        rows, width
    ) / math.sqrt(HBLK)
    blocks = width // HBLK
    residual = (
        quant_codes.astype(jnp.float32).reshape(rows, blocks, HBLK)
        * jnp.exp2(exponents.astype(jnp.float32))[:, :, None]
    )
    return (residual.reshape(rows, width) + rotated).astype(jnp.bfloat16)


def solution(mesh):
    return jax.shard_map(
        body,
        mesh=mesh,
        in_specs=(
            P("groups", "tensor"),
            P(("groups", "tensor"), None),
            P(("groups", "tensor"), None),
            P(("groups", "tensor"), None),
            P(("groups", "tensor"), None),
            P("tensor", None),
        ),
        out_specs=P(("groups", "tensor"), None),
        check_vma=False,
    )
```

profile of v0, /device:TPU:0, one launch (start us, length us, event | category | flops | bytes accessed | tf_op | source)
XLA Modules:
  0.0 235.5 jit_solution(13614162380129853962)
XLA Ops:
  8.7 91.7 %while.22 = (s32[]{:T(128)}, bf16[2,8,1024]{2,1,0:T(8,128)(2,1)S(1)}, f32[8,128]{1,0:T(8,128)S(1)}, f32[8,128]{1,0:T(8,128)S(1)}, f32[8,128,128]{2,1,0:T(8,128)S...) while((s32[]{:T(128)}, ...), condition=%wide.region_3.5_spmd.clone, body=%wide.region_0.4_spmd.clone.sunk | while | flops 25664864 | bytes 2368026 | solution.py:89
  11.5 1.2 convolution_add_fusion.3
  12.7 3.1 %collective-permute-done = bf16[2,8,1024]{2,1,0:T(8,128)(2,1)S(1)} collective-permute-done((bf16[2,8,1024]{2,1,0:T(8,128)(2,1)S(1)}, bf16[2,8,1024]{2,1,0:T(8,128)(2,1)S(1)}, u32[]{:S(2)}, u32[]{:S(2)}) %collective-permute-start) | collective-permute-done | bytes 32800 | tf_op jit(solution)/shard_map/while/body/eval_jaxpr/ppermute | solution.py:20
  18.1 1.2 convolution_add_fusion.3
  19.3 2.5 %collective-permute-done = bf16[2,8,1024]{2,1,0:T(8,128)(2,1)S(1)} collective-permute-done((bf16[2,8,1024]{2,1,0:T(8,128)(2,1)S(1)}, bf16[2,8,1024]{2,1,0:T(8,128)(2,1)S(1)}, u32[]{:S(2)}, u32[]{:S(2)}) %collective-permute-start) | collective-permute-done | bytes 32800 | tf_op jit(solution)/shard_map/while/body/eval_jaxpr/ppermute | solution.py:20
  25.4 2.5 %collective-permute-done = bf16[2,8,1024]{2,1,0:T(8,128)(2,1)S(1)} collective-permute-done((bf16[2,8,1024]{2,1,0:T(8,128)(2,1)S(1)}, bf16[2,8,1024]{2,1,0:T(8,128)(2,1)S(1)}, u32[]{:S(2)}, u32[]{:S(2)}) %collective-permute-start) | collective-permute-done | bytes 32800 | tf_op jit(solution)/shard_map/while/body/eval_jaxpr/ppermute | solution.py:20
  30.2 1.2 convolution_add_fusion.3
  31.4 2.5 %collective-permute-done = bf16[2,8,1024]{2,1,0:T(8,128)(2,1)S(1)} collective-permute-done((bf16[2,8,1024]{2,1,0:T(8,128)(2,1)S(1)}, bf16[2,8,1024]{2,1,0:T(8,128)(2,1)S(1)}, u32[]{:S(2)}, u32[]{:S(2)}) %collective-permute-start) | collective-permute-done | bytes 32800 | tf_op jit(solution)/shard_map/while/body/eval_jaxpr/ppermute | solution.py:20
  36.3 1.2 convolution_add_fusion.3
  37.5 2.5 %collective-permute-done = bf16[2,8,1024]{2,1,0:T(8,128)(2,1)S(1)} collective-permute-done((bf16[2,8,1024]{2,1,0:T(8,128)(2,1)S(1)}, bf16[2,8,1024]{2,1,0:T(8,128)(2,1)S(1)}, u32[]{:S(2)}, u32[]{:S(2)}) %collective-permute-start) | collective-permute-done | bytes 32800 | tf_op jit(solution)/shard_map/while/body/eval_jaxpr/ppermute | solution.py:20
  43.5 2.5 %collective-permute-done = bf16[2,8,1024]{2,1,0:T(8,128)(2,1)S(1)} collective-permute-done((bf16[2,8,1024]{2,1,0:T(8,128)(2,1)S(1)}, bf16[2,8,1024]{2,1,0:T(8,128)(2,1)S(1)}, u32[]{:S(2)}, u32[]{:S(2)}) %collective-permute-start) | collective-permute-done | bytes 32800 | tf_op jit(solution)/shard_map/while/body/eval_jaxpr/ppermute | solution.py:20
  49.5 2.5 %collective-permute-done = bf16[2,8,1024]{2,1,0:T(8,128)(2,1)S(1)} collective-permute-done((bf16[2,8,1024]{2,1,0:T(8,128)(2,1)S(1)}, bf16[2,8,1024]{2,1,0:T(8,128)(2,1)S(1)}, u32[]{:S(2)}, u32[]{:S(2)}) %collective-permute-start) | collective-permute-done | bytes 32800 | tf_op jit(solution)/shard_map/while/body/eval_jaxpr/ppermute | solution.py:20
  55.6 2.5 %collective-permute-done = bf16[2,8,1024]{2,1,0:T(8,128)(2,1)S(1)} collective-permute-done((bf16[2,8,1024]{2,1,0:T(8,128)(2,1)S(1)}, bf16[2,8,1024]{2,1,0:T(8,128)(2,1)S(1)}, u32[]{:S(2)}, u32[]{:S(2)}) %collective-permute-start) | collective-permute-done | bytes 32800 | tf_op jit(solution)/shard_map/while/body/eval_jaxpr/ppermute | solution.py:20
  61.6 2.5 %collective-permute-done = bf16[2,8,1024]{2,1,0:T(8,128)(2,1)S(1)} collective-permute-done((bf16[2,8,1024]{2,1,0:T(8,128)(2,1)S(1)}, bf16[2,8,1024]{2,1,0:T(8,128)(2,1)S(1)}, u32[]{:S(2)}, u32[]{:S(2)}) %collective-permute-start) | collective-permute-done | bytes 32800 | tf_op jit(solution)/shard_map/while/body/eval_jaxpr/ppermute | solution.py:20
  66.5 1.2 convolution_add_fusion.3
  67.7 2.5 %collective-permute-done = bf16[2,8,1024]{2,1,0:T(8,128)(2,1)S(1)} collective-permute-done((bf16[2,8,1024]{2,1,0:T(8,128)(2,1)S(1)}, bf16[2,8,1024]{2,1,0:T(8,128)(2,1)S(1)}, u32[]{:S(2)}, u32[]{:S(2)}) %collective-permute-start) | collective-permute-done | bytes 32800 | tf_op jit(solution)/shard_map/while/body/eval_jaxpr/ppermute | solution.py:20
  73.7 2.5 %collective-permute-done = bf16[2,8,1024]{2,1,0:T(8,128)(2,1)S(1)} collective-permute-done((bf16[2,8,1024]{2,1,0:T(8,128)(2,1)S(1)}, bf16[2,8,1024]{2,1,0:T(8,128)(2,1)S(1)}, u32[]{:S(2)}, u32[]{:S(2)}) %collective-permute-start) | collective-permute-done | bytes 32800 | tf_op jit(solution)/shard_map/while/body/eval_jaxpr/ppermute | solution.py:20
  79.7 2.5 %collective-permute-done = bf16[2,8,1024]{2,1,0:T(8,128)(2,1)S(1)} collective-permute-done((bf16[2,8,1024]{2,1,0:T(8,128)(2,1)S(1)}, bf16[2,8,1024]{2,1,0:T(8,128)(2,1)S(1)}, u32[]{:S(2)}, u32[]{:S(2)}) %collective-permute-start) | collective-permute-done | bytes 32800 | tf_op jit(solution)/shard_map/while/body/eval_jaxpr/ppermute | solution.py:20
  84.6 1.2 convolution_add_fusion.3
  85.8 2.5 %collective-permute-done = bf16[2,8,1024]{2,1,0:T(8,128)(2,1)S(1)} collective-permute-done((bf16[2,8,1024]{2,1,0:T(8,128)(2,1)S(1)}, bf16[2,8,1024]{2,1,0:T(8,128)(2,1)S(1)}, u32[]{:S(2)}, u32[]{:S(2)}) %collective-permute-start) | collective-permute-done | bytes 32800 | tf_op jit(solution)/shard_map/while/body/eval_jaxpr/ppermute | solution.py:20
  91.8 2.5 %collective-permute-done = bf16[2,8,1024]{2,1,0:T(8,128)(2,1)S(1)} collective-permute-done((bf16[2,8,1024]{2,1,0:T(8,128)(2,1)S(1)}, bf16[2,8,1024]{2,1,0:T(8,128)(2,1)S(1)}, u32[]{:S(2)}, u32[]{:S(2)}) %collective-permute-start) | collective-permute-done | bytes 32800 | tf_op jit(solution)/shard_map/while/body/eval_jaxpr/ppermute | solution.py:20
  97.9 2.5 %collective-permute-done = bf16[2,8,1024]{2,1,0:T(8,128)(2,1)S(1)} collective-permute-done((bf16[2,8,1024]{2,1,0:T(8,128)(2,1)S(1)}, bf16[2,8,1024]{2,1,0:T(8,128)(2,1)S(1)}, u32[]{:S(2)}, u32[]{:S(2)}) %collective-permute-start) | collective-permute-done | bytes 32800 | tf_op jit(solution)/shard_map/while/body/eval_jaxpr/ppermute | solution.py:20
  103.3 18.6 %fusion.65 = f32[128,16384]{1,0:T(8,128)} fusion(bf16[128,1024]{0,1:T(8,128)(2,1)S(1)} %bitcast.59, bf16[1024,16384]{1,0:T(8,128)(2,1)} %param.15), kind=kOutput, calls=%fused_computation.108 | convolution fusion | flops 4294967296 | bytes 42205184 | tf_op jit(solution)/shard_map/dot_general | solution.py:99
  122.0 103.8 %reduce-scatter.2.cloned.1.call-done = f32[8,16384]{1,0:T(8,128)} async-done(((f32[128,16384]{1,0:T(8,128)}), f32[8,16384]{1,0:T(8,128)}) %reduce-scatter.2.cloned.1.call-update) | async-done | bytes 524304 | tf_op jit(solution)/shard_map/reduce_scatter | solution.py:98
  (282 shorter events, 52.8 us)
Async XLA Ops:
  6.5 219.3 %reduce-scatter.2.cloned.1.call-start = ((), (), s32[]{:S(2)}) async-start(), calls=%async_computation.1 | async-start | bytes 8912896 | tf_op jit(solution)/shard_map/reduce_scatter | solution.py:98
  8.7 113.2 %copy-start.1 = (s32[8,128]{1,0:T(8,128)S(1)}, s32[8,128]{1,0:T(8,128)}, u32[]{:S(2)}) copy-start(s32[8,128]{1,0:T(8,128)} %param.14) | copy-start | bytes 12292
  8.7 7.1 %collective-permute-start = (bf16[2,8,1024]{2,1,0:T(8,128)(2,1)S(1)}, bf16[2,8,1024]{2,1,0:T(8,128)(2,1)S(1)}, u32[]{:S(2)}, u32[]{:S(2)}) collective-permute-start(bf16[2,8,1024]{2,1,0:T(8,128)(2,1)S(1)} %copy.21), channel_id=1, source_target_pairs={{0,1},{1,2},{2,3},{3,4},{4,5},{5,6},{6,7},{7,8},{8,9},{9,10},{10,1... | collective-permute-start | bytes 98312 | tf_op jit(solution)/shard_map/while/body/eval_jaxpr/ppermute | solution.py:20
  15.8 6.0 %collective-permute-start = (bf16[2,8,1024]{2,1,0:T(8,128)(2,1)S(1)}, bf16[2,8,1024]{2,1,0:T(8,128)(2,1)S(1)}, u32[]{:S(2)}, u32[]{:S(2)}) collective-permute-start(bf16[2,8,1024]{2,1,0:T(8,128)(2,1)S(1)} %copy.21), channel_id=1, source_target_pairs={{0,1},{1,2},{2,3},{3,4},{4,5},{5,6},{6,7},{7,8},{8,9},{9,10},{10,1... | collective-permute-start | bytes 98312 | tf_op jit(solution)/shard_map/while/body/eval_jaxpr/ppermute | solution.py:20
  21.8 6.0 %collective-permute-start = (bf16[2,8,1024]{2,1,0:T(8,128)(2,1)S(1)}, bf16[2,8,1024]{2,1,0:T(8,128)(2,1)S(1)}, u32[]{:S(2)}, u32[]{:S(2)}) collective-permute-start(bf16[2,8,1024]{2,1,0:T(8,128)(2,1)S(1)} %copy.21), channel_id=1, source_target_pairs={{0,1},{1,2},{2,3},{3,4},{4,5},{5,6},{6,7},{7,8},{8,9},{9,10},{10,1... | collective-permute-start | bytes 98312 | tf_op jit(solution)/shard_map/while/body/eval_jaxpr/ppermute | solution.py:20
  27.9 6.0 %collective-permute-start = (bf16[2,8,1024]{2,1,0:T(8,128)(2,1)S(1)}, bf16[2,8,1024]{2,1,0:T(8,128)(2,1)S(1)}, u32[]{:S(2)}, u32[]{:S(2)}) collective-permute-start(bf16[2,8,1024]{2,1,0:T(8,128)(2,1)S(1)} %copy.21), channel_id=1, source_target_pairs={{0,1},{1,2},{2,3},{3,4},{4,5},{5,6},{6,7},{7,8},{8,9},{9,10},{10,1... | collective-permute-start | bytes 98312 | tf_op jit(solution)/shard_map/while/body/eval_jaxpr/ppermute | solution.py:20
  33.9 6.0 %collective-permute-start = (bf16[2,8,1024]{2,1,0:T(8,128)(2,1)S(1)}, bf16[2,8,1024]{2,1,0:T(8,128)(2,1)S(1)}, u32[]{:S(2)}, u32[]{:S(2)}) collective-permute-start(bf16[2,8,1024]{2,1,0:T(8,128)(2,1)S(1)} %copy.21), channel_id=1, source_target_pairs={{0,1},{1,2},{2,3},{3,4},{4,5},{5,6},{6,7},{7,8},{8,9},{9,10},{10,1... | collective-permute-start | bytes 98312 | tf_op jit(solution)/shard_map/while/body/eval_jaxpr/ppermute | solution.py:20
  40.0 6.0 %collective-permute-start = (bf16[2,8,1024]{2,1,0:T(8,128)(2,1)S(1)}, bf16[2,8,1024]{2,1,0:T(8,128)(2,1)S(1)}, u32[]{:S(2)}, u32[]{:S(2)}) collective-permute-start(bf16[2,8,1024]{2,1,0:T(8,128)(2,1)S(1)} %copy.21), channel_id=1, source_target_pairs={{0,1},{1,2},{2,3},{3,4},{4,5},{5,6},{6,7},{7,8},{8,9},{9,10},{10,1... | collective-permute-start | bytes 98312 | tf_op jit(solution)/shard_map/while/body/eval_jaxpr/ppermute | solution.py:20
  46.0 6.0 %collective-permute-start = (bf16[2,8,1024]{2,1,0:T(8,128)(2,1)S(1)}, bf16[2,8,1024]{2,1,0:T(8,128)(2,1)S(1)}, u32[]{:S(2)}, u32[]{:S(2)}) collective-permute-start(bf16[2,8,1024]{2,1,0:T(8,128)(2,1)S(1)} %copy.21), channel_id=1, source_target_pairs={{0,1},{1,2},{2,3},{3,4},{4,5},{5,6},{6,7},{7,8},{8,9},{9,10},{10,1... | collective-permute-start | bytes 98312 | tf_op jit(solution)/shard_map/while/body/eval_jaxpr/ppermute | solution.py:20
  52.0 6.0 %collective-permute-start = (bf16[2,8,1024]{2,1,0:T(8,128)(2,1)S(1)}, bf16[2,8,1024]{2,1,0:T(8,128)(2,1)S(1)}, u32[]{:S(2)}, u32[]{:S(2)}) collective-permute-start(bf16[2,8,1024]{2,1,0:T(8,128)(2,1)S(1)} %copy.21), channel_id=1, source_target_pairs={{0,1},{1,2},{2,3},{3,4},{4,5},{5,6},{6,7},{7,8},{8,9},{9,10},{10,1... | collective-permute-start | bytes 98312 | tf_op jit(solution)/shard_map/while/body/eval_jaxpr/ppermute | solution.py:20
  58.1 6.0 %collective-permute-start = (bf16[2,8,1024]{2,1,0:T(8,128)(2,1)S(1)}, bf16[2,8,1024]{2,1,0:T(8,128)(2,1)S(1)}, u32[]{:S(2)}, u32[]{:S(2)}) collective-permute-start(bf16[2,8,1024]{2,1,0:T(8,128)(2,1)S(1)} %copy.21), channel_id=1, source_target_pairs={{0,1},{1,2},{2,3},{3,4},{4,5},{5,6},{6,7},{7,8},{8,9},{9,10},{10,1... | collective-permute-start | bytes 98312 | tf_op jit(solution)/shard_map/while/body/eval_jaxpr/ppermute | solution.py:20
  64.1 6.0 %collective-permute-start = (bf16[2,8,1024]{2,1,0:T(8,128)(2,1)S(1)}, bf16[2,8,1024]{2,1,0:T(8,128)(2,1)S(1)}, u32[]{:S(2)}, u32[]{:S(2)}) collective-permute-start(bf16[2,8,1024]{2,1,0:T(8,128)(2,1)S(1)} %copy.21), channel_id=1, source_target_pairs={{0,1},{1,2},{2,3},{3,4},{4,5},{5,6},{6,7},{7,8},{8,9},{9,10},{10,1... | collective-permute-start | bytes 98312 | tf_op jit(solution)/shard_map/while/body/eval_jaxpr/ppermute | solution.py:20
  70.2 6.0 %collective-permute-start = (bf16[2,8,1024]{2,1,0:T(8,128)(2,1)S(1)}, bf16[2,8,1024]{2,1,0:T(8,128)(2,1)S(1)}, u32[]{:S(2)}, u32[]{:S(2)}) collective-permute-start(bf16[2,8,1024]{2,1,0:T(8,128)(2,1)S(1)} %copy.21), channel_id=1, source_target_pairs={{0,1},{1,2},{2,3},{3,4},{4,5},{5,6},{6,7},{7,8},{8,9},{9,10},{10,1... | collective-permute-start | bytes 98312 | tf_op jit(solution)/shard_map/while/body/eval_jaxpr/ppermute | solution.py:20
  76.2 6.0 %collective-permute-start = (bf16[2,8,1024]{2,1,0:T(8,128)(2,1)S(1)}, bf16[2,8,1024]{2,1,0:T(8,128)(2,1)S(1)}, u32[]{:S(2)}, u32[]{:S(2)}) collective-permute-start(bf16[2,8,1024]{2,1,0:T(8,128)(2,1)S(1)} %copy.21), channel_id=1, source_target_pairs={{0,1},{1,2},{2,3},{3,4},{4,5},{5,6},{6,7},{7,8},{8,9},{9,10},{10,1... | collective-permute-start | bytes 98312 | tf_op jit(solution)/shard_map/while/body/eval_jaxpr/ppermute | solution.py:20
  82.3 6.0 %collective-permute-start = (bf16[2,8,1024]{2,1,0:T(8,128)(2,1)S(1)}, bf16[2,8,1024]{2,1,0:T(8,128)(2,1)S(1)}, u32[]{:S(2)}, u32[]{:S(2)}) collective-permute-start(bf16[2,8,1024]{2,1,0:T(8,128)(2,1)S(1)} %copy.21), channel_id=1, source_target_pairs={{0,1},{1,2},{2,3},{3,4},{4,5},{5,6},{6,7},{7,8},{8,9},{9,10},{10,1... | collective-permute-start | bytes 98312 | tf_op jit(solution)/shard_map/while/body/eval_jaxpr/ppermute | solution.py:20
  88.3 6.0 %collective-permute-start = (bf16[2,8,1024]{2,1,0:T(8,128)(2,1)S(1)}, bf16[2,8,1024]{2,1,0:T(8,128)(2,1)S(1)}, u32[]{:S(2)}, u32[]{:S(2)}) collective-permute-start(bf16[2,8,1024]{2,1,0:T(8,128)(2,1)S(1)} %copy.21), channel_id=1, source_target_pairs={{0,1},{1,2},{2,3},{3,4},{4,5},{5,6},{6,7},{7,8},{8,9},{9,10},{10,1... | collective-permute-start | bytes 98312 | tf_op jit(solution)/shard_map/while/body/eval_jaxpr/ppermute | solution.py:20
  94.3 6.0 %collective-permute-start = (bf16[2,8,1024]{2,1,0:T(8,128)(2,1)S(1)}, bf16[2,8,1024]{2,1,0:T(8,128)(2,1)S(1)}, u32[]{:S(2)}, u32[]{:S(2)}) collective-permute-start(bf16[2,8,1024]{2,1,0:T(8,128)(2,1)S(1)} %copy.21), channel_id=1, source_target_pairs={{0,1},{1,2},{2,3},{3,4},{4,5},{5,6},{6,7},{7,8},{8,9},{9,10},{10,1... | collective-permute-start | bytes 98312 | tf_op jit(solution)/shard_map/while/body/eval_jaxpr/ppermute | solution.py:20
  100.4 127.4 %copy-start = (s32[8,16384]{1,0:T(8,128)S(1)}, s32[8,16384]{1,0:T(8,128)}, u32[]{:S(2)}) copy-start(s32[8,16384]{1,0:T(8,128)} %param.13) | copy-start | bytes 1572868
Sparse Core Ops, SparseCore 0:
  122.0 103.7 reduce-scatter.1
where the time goes:
time: 236 us
  waiting for transfers between devices  142 us (60%)
  matrix products  52.9 us (22%)
  local copies, waits for them, and re-layouts  20.7 us (9%)
  between operations  13.6 us (6%)
  other arithmetic  4.21 us (2%)
    reduce_scatter x1, waiting for transfers between devices, body(): lax.psum_scatter(jnp.dot(context, out_weight, preferred_element_type=jnp....  104 us
    ppermute x15, waiting for transfers between devices, passed_along(): return lax.ppermute(value, axis, pairs)  38.2 us
    dot_general x16, matrix products, attend(): jnp.einsum('htc,chd->htd', weights, value_matrix, precision=lax.Precision...  18.7 us
    dot_general x1, matrix products, body(): jnp.dot(context, out_weight, preferred_element_type=jnp.float32)  18.6 us
    dot_general x16, matrix products, attend(): jnp.einsum('thd,chd->htc', query_matrix, key_matrix, precision=lax.Precis...  15 us
    gather x16, local copies, waits for them, and re-layouts, attend(): jnp.take(expanded_heads[1].reshape(head_count, KEY_VALUE_HEADS, HEAD_SIZE...  8.88 us
    gather x16, local copies, waits for them, and re-layouts, attend(): jnp.take(expanded_heads[0].reshape(head_count, KEY_VALUE_HEADS, HEAD_SIZE...  8.88 us
  transfers between devices with their start and end apart: 16, of which 16 were waited for; matrix products, arithmetic and copies ran while one was open for 22% of the time, Pallas kernels for 0%

commit v1 on v0

v1 whole, which is shorter than its diff:
```python
import functools
import math

import jax
import jax.numpy as jnp
from jax import lax
from jax.experimental import pallas as pl
from jax.experimental.pallas import tpu as pltpu
from jax.sharding import PartitionSpec as P

QUERY_HEADS = 128
KEY_VALUE_HEADS = 8
HEAD_SIZE = 128
HBLK = 128
masked_score = -1e30

PARTS = (4, 6, 4, 2)


def reversed_bits(index, bits):
    result = 0
    for bit in range(bits):
        result = result + ((index >> bit) & 1) * (1 << (bits - 1 - bit))
    return result


def attend(token, q_ref, kv_ref, context_ref):
    total_rows = q_ref.shape[0]
    column = lax.broadcasted_iota(jnp.int32, (total_rows, total_rows), 1)
    order = jnp.where(column == token, 1.0, 0.0).astype(jnp.bfloat16)
    visible = column <= token
    queries = jnp.dot(order, q_ref[...], preferred_element_type=jnp.float32).astype(jnp.bfloat16)
    key = kv_ref[:, :HEAD_SIZE]
    value = kv_ref[:, HEAD_SIZE:]
    for head in range(q_ref.shape[1] // HEAD_SIZE):
        columns = slice(head * HEAD_SIZE, (head + 1) * HEAD_SIZE)
        scores = lax.dot_general(
            queries[:, columns], key, (((1,), (1,)), ((), ())), preferred_element_type=jnp.float32
        ) * (1.0 / math.sqrt(HEAD_SIZE))
        scores = jnp.where(visible, scores, masked_score)
        top = jnp.max(scores, axis=1, keepdims=True)
        weights = jnp.where(visible, jnp.exp(scores - top), 0.0)
        total = jnp.sum(weights, axis=1, keepdims=True)
        high = weights.astype(jnp.bfloat16)
        low = (weights - high.astype(jnp.float32)).astype(jnp.bfloat16)
        weighted = jnp.dot(high, value, preferred_element_type=jnp.float32)
        weighted = weighted + jnp.dot(low, value, preferred_element_type=jnp.float32)
        context_ref[:, columns] = (weighted / total).astype(jnp.bfloat16)


def project(start, context_ref, w_ref, keep_ref, send_ref, buffer, arrived, prologue=None):
    tiles, _, tile = buffer.shape
    half = keep_ref.shape[0]

    def copy(index):
        return pltpu.make_async_copy(
            w_ref.at[:, pl.ds(start + index * tile, tile)], buffer.at[index], arrived.at[index]
        )

    for index in range(tiles):
        copy(index).start()
    if prologue is not None:
        prologue()
    for index in range(tiles):
        copy(index).wait()
        columns = slice(index * tile, (index + 1) * tile)
        product = jnp.dot(context_ref[...], buffer[index], preferred_element_type=jnp.float32)
        keep_ref[:, columns] = product[:half]
        send_ref[:, columns] = product[half:].astype(jnp.bfloat16)


def first_kernel(start, bits, place_ref, q_ref, kv_ref, w_ref, context_ref, keep_ref, send_ref, buffer, arrived):
    total_rows = q_ref.shape[0]
    rows = total_rows >> bits
    row = lax.broadcasted_iota(jnp.int32, (total_rows, 1), 0)
    token = (place_ref[0] ^ reversed_bits(row // rows, bits)) * rows + row % rows
    project(
        start, context_ref, w_ref, keep_ref, send_ref, buffer, arrived,
        prologue=lambda: attend(token, q_ref, kv_ref, context_ref),
    )


def next_kernel(start, context_ref, w_ref, keep_ref, send_ref, buffer, arrived):
    project(start, context_ref, w_ref, keep_ref, send_ref, buffer, arrived)


def projection_call(kernel, inputs, in_specs, total_rows, depth, width, with_context):
    half = total_rows // 2
    tile = 512
    out_shape = [
        jax.ShapeDtypeStruct((half, width), jnp.float32),
        jax.ShapeDtypeStruct((half, width), jnp.bfloat16),
    ]
    if with_context:
        out_shape = [jax.ShapeDtypeStruct((total_rows, depth), jnp.bfloat16)] + out_shape
    return pl.pallas_call(
        kernel,
        in_specs=in_specs,
        out_specs=[pl.BlockSpec(memory_space=pltpu.VMEM)] * len(out_shape),
        out_shape=out_shape,
        scratch_shapes=[
            pltpu.VMEM((width // tile, depth, tile), jnp.bfloat16),
            pltpu.SemaphoreType.DMA((width // tile,)),
        ],
        compiler_params=pltpu.CompilerParams(vmem_limit_bytes=28 << 20),
        cost_estimate=pl.CostEstimate(
            flops=2 * total_rows * depth * width,
            bytes_accessed=2 * depth * width,
            transcendentals=0,
        ),
    )(*inputs)


def finish_kernel(codes_ref, exponents_ref, *refs):
    *pieces, out_ref = refs
    rows, width = out_ref.shape
    blocks = width // HBLK
    i = lax.broadcasted_iota(jnp.int32, (HBLK, HBLK), 0)
    common = i & lax.broadcasted_iota(jnp.int32, (HBLK, HBLK), 1)
    parity = jnp.zeros((HBLK, HBLK), jnp.int32)
    for bit in range(HBLK.bit_length() - 1):
        parity = parity ^ (common >> bit)
    table = (1 - 2 * (parity & 1)).astype(jnp.bfloat16)
    scale = jnp.exp2(exponents_ref[...].astype(jnp.float32))
    at = 0
    for keep_ref, got_ref in zip(pieces[::2], pieces[1::2]):
        summed = keep_ref[...] + got_ref[...].astype(jnp.float32)
        count = summed.shape[1] // HBLK
        stacked = jnp.concatenate([summed[:, b * HBLK:(b + 1) * HBLK] for b in range(count)], axis=0)
        rotated = jnp.zeros_like(stacked)
        rest = stacked
        for _ in range(3):
            piece = rest.astype(jnp.bfloat16)
            rotated = rotated + jnp.dot(piece, table, preferred_element_type=jnp.float32)
            rest = rest - piece.astype(jnp.float32)
        rotated = rotated * (1.0 / math.sqrt(HBLK))
        for b in range(count):
            block = at + b
            columns = slice(block * HBLK, (block + 1) * HBLK)
            residual = codes_ref[:, columns].astype(jnp.float32) * scale[:, block:block + 1]
            out_ref[:, columns] = (residual + rotated[b * rows:(b + 1) * rows]).astype(jnp.bfloat16)
        at += count


def finish(codes, exponents, pieces):
    rows, width = codes.shape
    padded = max(rows, 8)
    inputs = [codes, exponents, *pieces]
    if padded != rows:
        inputs = [jnp.pad(x, ((0, padded - rows), (0, 0))) for x in inputs]
    out = pl.pallas_call(
        finish_kernel,
        out_shape=jax.ShapeDtypeStruct((padded, width), jnp.bfloat16),
        in_specs=[pl.BlockSpec(memory_space=pltpu.VMEM)] * len(inputs),
        out_specs=pl.BlockSpec(memory_space=pltpu.VMEM),
        compiler_params=pltpu.CompilerParams(vmem_limit_bytes=16 << 20),
        cost_estimate=pl.CostEstimate(flops=6 * padded * width * HBLK, bytes_accessed=12 * padded * width, transcendentals=0),
    )(*inputs)
    return out[:rows]


def passed_across(value, axis, mask):
    return lax.ppermute(value, axis, [(source, source ^ mask) for source in range(lax.axis_size(axis))])


def body(encoded_query_rows, encoded_key_rows, head_value_rows, quant_codes, exponents, out_weight):
    total_rows, query_width = encoded_query_rows.shape
    depth, width = out_weight.shape
    devices = lax.axis_size("tensor")
    bits = devices.bit_length() - 1
    local_heads = query_width // HEAD_SIZE
    query_group = QUERY_HEADS // KEY_VALUE_HEADS
    kv_rows = encoded_key_rows.shape[0]

    wanted = [device * local_heads // query_group for device in range(devices)]
    packed = jnp.stack(
        [
            jnp.concatenate(
                [x[:, head * HEAD_SIZE:(head + 1) * HEAD_SIZE] for x in (encoded_key_rows, head_value_rows)], axis=1
            )
            for head in wanted
        ]
    )
    kv = lax.all_to_all(packed, "tensor", 0, 0).reshape(devices * kv_rows, 2 * HEAD_SIZE)

    place = lax.axis_index("tensor").astype(jnp.int32).reshape(1)
    vmem = pl.BlockSpec(memory_space=pltpu.VMEM)
    anywhere = pl.BlockSpec(memory_space=pl.ANY)
    unit = width // sum(PARTS)
    start = 0
    context = None
    halves = []
    for part in PARTS:
        if context is None:
            context, keep, send = projection_call(
                functools.partial(first_kernel, start, bits),
                (place, encoded_query_rows, kv, out_weight),
                [pl.BlockSpec(memory_space=pltpu.SMEM), vmem, vmem, anywhere],
                total_rows, depth, part * unit, True,
            )
        else:
            keep, send = projection_call(
                functools.partial(next_kernel, start),
                (context, out_weight), [vmem, anywhere],
                total_rows, depth, part * unit, False,
            )
        halves.append((keep, send))
        start += part * unit

    pieces = []
    for keep, send in halves:
        for bit in range(bits):
            got = passed_across(send, "tensor", 1 << bit)
            if bit == bits - 1:
                pieces += [keep, got]
            else:
                summed = keep + got.astype(jnp.float32)
                half = summed.shape[0] // 2
                keep, send = summed[:half], summed[half:].astype(jnp.bfloat16)
    return finish(quant_codes, exponents, pieces)


def solution(mesh):
    return jax.shard_map(
        body,
        mesh=mesh,
        in_specs=(
            P("groups", "tensor"),
            P(("groups", "tensor"), None),
            P(("groups", "tensor"), None),
            P(("groups", "tensor"), None),
            P(("groups", "tensor"), None),
            P("tensor", None),
        ),
        out_specs=P(("groups", "tensor"), None),
        check_vma=False,
    )
```

time: 236 us -> 83.8 us (0.36)
  waiting for transfers between devices: 142 us -> 31.3 us
  matrix products: 52.9 us -> 0 us
  starting transfers between devices: 0.54 us -> 23 us
  local copies, waits for them, and re-layouts: 20.7 us -> 2.07 us
  Pallas kernels: 0 us -> 16.7 us
  between operations: 13.6 us -> 0.27 us
  other arithmetic: 4.21 us -> 10.2 us
    reduce_scatter x1 -> x0, waiting for transfers between devices: 104 us -> none  [body(): lax.psum_scatter(jnp.dot(context, out_weight, preferred_element_type=jnp....]
    dot_general x34 -> x0, matrix products: 52.9 us -> none  [the longest x16 18.7 us: attend(): jnp.einsum('htc,chd->htd', weights, value_matrix, precision=lax.Precision...]
    gather x32 -> x0, local copies, waits for them, and re-layouts: 17.8 us -> none  [the longest x16 8.88 us: attend(): jnp.take(expanded_heads[1].reshape(head_count, KEY_VALUE_HEADS, HEAD_SIZE...]
    pallas_call x0 -> x5, Pallas kernels: none -> 16.7 us  [the longest x4 15.6 us: projection_call(): pl.pallas_call(kernel, in_specs=in_specs, out_specs=[pl.BlockSpec(memory_...]
    ppermute x15 -> x16, starting transfers between devices: 0.54 us -> 15.6 us  [passed_across(): lax.ppermute(value, axis, [(source, source ^ mask) for source in range(la...]
    ppermute x15 -> x16, waiting for transfers between devices: 38.2 us -> 24.4 us  [passed_across(): lax.ppermute(value, axis, [(source, source ^ mask) for source in range(la...]
    unnamed x3 -> x15, other arithmetic: 0.01 us -> 8.92 us
    all_to_all x0 -> x1, starting transfers between devices: none -> 7.39 us  [body(): lax.all_to_all(packed, 'tensor', 0, 0)]
  transfers between devices with their start and end apart: 16 -> 17, of which waited for: 16 -> 7; matrix products, arithmetic and copies ran while one was open for 22% -> 1% of each run, Pallas kernels for 0% -> 11%
where the time goes in v1:
time: 83.8 us; the launch traced here: 83.5 us
  waiting for transfers between devices  31.3 us (37%)
  starting transfers between devices  23 us (27%)
  Pallas kernels  16.7 us (20%)
  other arithmetic  10.2 us (12%)
  local copies, waits for them, and re-layouts  2.07 us (2%)
    ppermute x16, waiting for transfers between devices, passed_across(): lax.ppermute(value, axis, [(source, source ^ mask) for source in range(la...  24.4 us
    pallas_call x4, Pallas kernels, projection_call(): pl.pallas_call(kernel, in_specs=in_specs, out_specs=[pl.BlockSpec(memory_...  15.6 us
    ppermute x16, starting transfers between devices, passed_across(): lax.ppermute(value, axis, [(source, source ^ mask) for source in range(la...  15.6 us
    unnamed x15, other arithmetic  8.92 us
    all_to_all x1, starting transfers between devices, body(): lax.all_to_all(packed, 'tensor', 0, 0)  7.39 us
    all_to_all x1, waiting for transfers between devices, body(): lax.all_to_all(packed, 'tensor', 0, 0)  6.89 us
  transfers between devices with their start and end apart: 17, of which 7 were waited for; matrix products, arithmetic and copies ran while one was open for 1% of the time, Pallas kernels for 11%

profile of v1, /device:TPU:0, one launch (start us, length us, event | category | flops | bytes accessed | tf_op | source)
XLA Modules:
  0.0 83.5 jit_solution(11570644487581709708)
XLA Ops:
  0.0 0.8 %fusion = (bf16[8,128]{1,0:T(8,128)(2,1)S(1)}, bf16[8,128]{1,0:T(8,128)(2,1)S(1)}, bf16[8,128]{1,0:T(8,128)(2,1)S(1)}, bf16[8,128]{1,0:T(8,128)(2,1)S(1)}, bf16[...) fusion(bf16[8,1024]{1,0:T(8,128)(2,1)} %param.7, ...), kind=kLoop, calls=%fused_computation.48 | loop fusion | bytes 65536 | tf_op jit(solution)/shard_map/slice | solution.py:179
  10.4 7.4 %all-to-all-start = ((bf16[16,8,256]{2,1,0:T(8,128)(2,1)}), bf16[16,8,256]{2,1,0:T(8,128)(2,1)S(1)}, u32[]{:S(2)}, u32[]{:S(2)}) async-start(bf16[16,8,256]{2,1,0:T(8,128)(2,1)} %constant_dynamic-update-slice_fusion), calls=%async_computation | async-start | bytes 131072 | tf_op jit(solution)/shard_map/all_to_all | solution.py:184
  17.8 6.9 %all-to-all-done = bf16[16,8,256]{2,1,0:T(8,128)(2,1)S(1)} async-done(((bf16[16,8,256]{2,1,0:T(8,128)(2,1)}), bf16[16,8,256]{2,1,0:T(8,128)(2,1)S(1)}, u32[]{:S(2)}, u32[]{:S(2)}) %all-to-all-start) | async-done | bytes 65568 | tf_op jit(solution)/shard_map/all_to_all | solution.py:184
  24.7 0.9 %copy-done.1 = bf16[128,1024]{1,0:T(8,128)(2,1)S(1)} copy-done((bf16[128,1024]{1,0:T(8,128)(2,1)S(1)}, bf16[128,1024]{1,0:T(8,128)(2,1)}, u32[]{:S(2)}) %copy-start.1) | copy-done | bytes 262168
  25.6 4.0 %shard_map.64 = (bf16[128,1024]{1,0:T(8,128)(2,1)S(1)}, f32[64,4096]{1,0:T(8,128)S(1)}, bf16[64,4096]{1,0:T(8,128)(2,1)S(1)}) custom-call(s32[1]{0:T(128)} %bitcast.place_ref, bf16[128,1024]{1,0:T(8,128)(2,1)S(1)} %copy-done.1, bf16[128,256]{1,0:T(8,128)(2,1)S(1)} %bitcast.50, bf16[1024,16384]{1,0:T(8,128)(2,1)} %w_ref.7), custom_call_target="tpu_custom_call" | custom-call | flops 1073741824 | bytes 8388608 | tf_op jit(solution)/shard_map/pallas_call | solution.py:96
  29.7 2.5 %shard_map.67 = (f32[64,2048]{1,0:T(8,128)S(1)}, bf16[64,2048]{1,0:T(8,128)(2,1)S(1)}) custom-call(bf16[128,1024]{1,0:T(8,128)(2,1)S(1)} %get-tuple-element.16.context_ref, bf16[1024,16384]{1,0:T(8,128)(2,1)} %w_ref.7), custom_call_target="tpu_custom_call" | custom-call | flops 536870912 | bytes 4194304 | tf_op jit(solution)/shard_map/pallas_call | solution.py:96
  32.3 1.5 %collective-permute-done.12 = bf16[64,2048]{1,0:T(8,128)(2,1)S(1)} collective-permute-done((bf16[64,2048]{1,0:T(8,128)(2,1)S(1)}, bf16[64,2048]{1,0:T(8,128)(2,1)S(1)}, u32[]{:S(2)}, u32[]{:S(2)}) %collective-permute-start.12) | collective-permute-done | bytes 262176 | tf_op jit(solution)/shard_map/ppermute | solution.py:163
  34.1 5.2 %shard_map.65 = (f32[64,6144]{1,0:T(8,128)S(1)}, bf16[64,6144]{1,0:T(8,128)(2,1)S(1)}) custom-call(bf16[128,1024]{1,0:T(8,128)(2,1)S(1)} %get-tuple-element.16.context_ref, bf16[1024,16384]{1,0:T(8,128)(2,1)} %w_ref.7), custom_call_target="tpu_custom_call" | custom-call | flops 1610612736 | bytes 12582912 | tf_op jit(solution)/shard_map/pallas_call | solution.py:96
  39.8 3.9 %shard_map.66 = (f32[64,4096]{1,0:T(8,128)S(1)}, bf16[64,4096]{1,0:T(8,128)(2,1)S(1)}) custom-call(bf16[128,1024]{1,0:T(8,128)(2,1)S(1)} %get-tuple-element.16.context_ref, bf16[1024,16384]{1,0:T(8,128)(2,1)} %w_ref.7), custom_call_target="tpu_custom_call" | custom-call | flops 1073741824 | bytes 8388608 | tf_op jit(solution)/shard_map/pallas_call | solution.py:96
  43.9 0.7 collective-permute-start.14
  44.7 1.4 %collective-permute-start.1 = (bf16[32,4096]{1,0:T(8,128)(2,1)S(1)}, bf16[32,4096]{1,0:T(8,128)(2,1)S(1)}, u32[]{:S(2)}, u32[]{:S(2)}) collective-permute-start(bf16[32,4096]{1,0:T(8,128)(2,1)S(1)} %slice.234), channel_id=1, source_target_pairs={{0,2},{1,3},{2,0},{3,1},{4,6},{5,7},{6,4},{7,5},{8,10},{9,11},{10,... | collective-permute-start | bytes 786440 | tf_op jit(solution)/shard_map/ppermute | solution.py:163
  46.3 1.5 %collective-permute-start.9 = (bf16[32,4096]{1,0:T(8,128)(2,1)S(1)}, bf16[32,4096]{1,0:T(8,128)(2,1)S(1)}, u32[]{:S(2)}, u32[]{:S(2)}) collective-permute-start(bf16[32,4096]{1,0:T(8,128)(2,1)S(1)} %slice.233), channel_id=1, source_target_pairs={{0,2},{1,3},{2,0},{3,1},{4,6},{5,7},{6,4},{7,5},{8,10},{9,11},{10,... | collective-permute-start | bytes 786440 | tf_op jit(solution)/shard_map/ppermute | solution.py:163
  47.8 6.2 %collective-permute-done.1 = bf16[32,4096]{1,0:T(8,128)(2,1)S(1)} collective-permute-done((bf16[32,4096]{1,0:T(8,128)(2,1)S(1)}, bf16[32,4096]{1,0:T(8,128)(2,1)S(1)}, u32[]{:S(2)}, u32[]{:S(2)}) %collective-permute-start.1) | collective-permute-done | bytes 262176 | tf_op jit(solution)/shard_map/ppermute | solution.py:163
  54.0 1.4 %collective-permute-start.2 = (bf16[16,4096]{1,0:T(8,128)(2,1)S(1)}, bf16[16,4096]{1,0:T(8,128)(2,1)S(1)}, u32[]{:S(2)}, u32[]{:S(2)}) collective-permute-start(bf16[16,4096]{1,0:T(8,128)(2,1)S(1)} %slice.238), channel_id=1, source_target_pairs={{0,4},{1,5},{2,6},{3,7},{4,0},{5,1},{6,2},{7,3},{8,12},{9,13},{10,... | collective-permute-start | bytes 393224 | tf_op jit(solution)/shard_map/ppermute | solution.py:163
  55.6 2.0 %collective-permute-start.5 = (bf16[32,6144]{1,0:T(8,128)(2,1)S(1)}, bf16[32,6144]{1,0:T(8,128)(2,1)S(1)}, u32[]{:S(2)}, u32[]{:S(2)}) collective-permute-start(bf16[32,6144]{1,0:T(8,128)(2,1)S(1)} %slice.232), channel_id=1, source_target_pairs={{0,2},{1,3},{2,0},{3,1},{4,6},{5,7},{6,4},{7,5},{8,10},{9,11},{10,... | collective-permute-start | bytes 1179656 | tf_op jit(solution)/shard_map/ppermute | solution.py:163
  57.7 1.9 %collective-permute-done.9 = bf16[32,4096]{1,0:T(8,128)(2,1)S(1)} collective-permute-done((bf16[32,4096]{1,0:T(8,128)(2,1)S(1)}, bf16[32,4096]{1,0:T(8,128)(2,1)S(1)}, u32[]{:S(2)}, u32[]{:S(2)}) %collective-permute-start.9) | collective-permute-done | bytes 262176 | tf_op jit(solution)/shard_map/ppermute | solution.py:163
  59.7 1.4 %collective-permute-start.10 = (bf16[16,4096]{1,0:T(8,128)(2,1)S(1)}, bf16[16,4096]{1,0:T(8,128)(2,1)S(1)}, u32[]{:S(2)}, u32[]{:S(2)}) collective-permute-start(bf16[16,4096]{1,0:T(8,128)(2,1)S(1)} %slice.237), channel_id=1, source_target_pairs={{0,4},{1,5},{2,6},{3,7},{4,0},{5,1},{6,2},{7,3},{8,12},{9,13},{10,... | collective-permute-start | bytes 393224 | tf_op jit(solution)/shard_map/ppermute | solution.py:163
  61.1 0.8 collective-permute-start.3
  62.0 5.2 %collective-permute-done.5 = bf16[32,6144]{1,0:T(8,128)(2,1)S(1)} collective-permute-done((bf16[32,6144]{1,0:T(8,128)(2,1)S(1)}, bf16[32,6144]{1,0:T(8,128)(2,1)S(1)}, u32[]{:S(2)}, u32[]{:S(2)}) %collective-permute-start.5) | collective-permute-done | bytes 393248 | tf_op jit(solution)/shard_map/ppermute | solution.py:163
  67.4 1.6 %collective-permute-start.6 = (bf16[16,6144]{1,0:T(8,128)(2,1)S(1)}, bf16[16,6144]{1,0:T(8,128)(2,1)S(1)}, u32[]{:S(2)}, u32[]{:S(2)}) collective-permute-start(bf16[16,6144]{1,0:T(8,128)(2,1)S(1)} %slice.235), channel_id=1, source_target_pairs={{0,4},{1,5},{2,6},{3,7},{4,0},{5,1},{6,2},{7,3},{8,12},{9,13},{10,... | collective-permute-start | bytes 589832 | tf_op jit(solution)/shard_map/ppermute | solution.py:163
  69.7 5.3 %collective-permute-done.6 = bf16[16,6144]{1,0:T(8,128)(2,1)S(1)} collective-permute-done((bf16[16,6144]{1,0:T(8,128)(2,1)S(1)}, bf16[16,6144]{1,0:T(8,128)(2,1)S(1)}, u32[]{:S(2)}, u32[]{:S(2)}) %collective-permute-start.6) | collective-permute-done | bytes 196640 | tf_op jit(solution)/shard_map/ppermute | solution.py:163
  75.4 2.7 %collective-permute-start.15 = (bf16[8,2048]{1,0:T(8,128)(2,1)S(1)}, bf16[8,2048]{1,0:T(8,128)(2,1)S(1)}, u32[]{:S(2)}, u32[]{:S(2)}) collective-permute-start(bf16[8,2048]{1,0:T(8,128)(2,1)S(1)} %slice.243), channel_id=1, source_target_pairs={{0,8},{1,9},{2,10},{3,11},{4,12},{5,13},{6,14},{7,15},{8,0},{9,1},... | collective-permute-start | bytes 98312 | tf_op jit(solution)/shard_map/ppermute | solution.py:163
  78.2 4.2 %collective-permute-done.15.refs_7_ = bf16[8,2048]{1,0:T(8,128)(2,1)S(1)} collective-permute-done((bf16[8,2048]{1,0:T(8,128)(2,1)S(1)}, bf16[8,2048]{1,0:T(8,128)(2,1)S(1)}, u32[]{:S(2)}, u32[]{:S(2)}) %collective-permute-start.15) | collective-permute-done | bytes 32800 | tf_op jit(solution)/shard_map/ppermute | solution.py:163
  82.4 1.1 %shard_map.68 = bf16[8,16384]{1,0:T(8,128)(2,1)} custom-call(s32[8,16384]{1,0:T(8,128)S(1)} %copy-done, s32[8,128]{1,0:T(8,128)S(1)} %copy-done.2, f32[8,4096]{1,0:T(8,128)S(1)} %slice.192.refs_0_, bf16[8,4096]{1,0:T(8,128)(2,1)S(1)} %collective-permute-done.3.refs_1_, f32[8,6144]{1,0:T(8,128)S(1)} %slice.198.refs_2_, ...), custom_call_target="tpu_custom_call" | custom-call | flops 100663296 | bytes 1572864 | tf_op jit(solution)/shard_map/pallas_call | solution.py:151
  (66 shorter events, 12.5 us)
Async XLA Ops:
  10.4 14.3 %all-to-all-start = ((bf16[16,8,256]{2,1,0:T(8,128)(2,1)}), bf16[16,8,256]{2,1,0:T(8,128)(2,1)S(1)}, u32[]{:S(2)}, u32[]{:S(2)}) async-start(bf16[16,8,256]{2,1,0:T(8,128)(2,1)} %constant_dynamic-update-slice_fusion), calls=%async_computation | async-start | bytes 131072 | tf_op jit(solution)/shard_map/all_to_all | solution.py:184
  24.7 1.0 %copy-start.1 = (bf16[128,1024]{1,0:T(8,128)(2,1)S(1)}, bf16[128,1024]{1,0:T(8,128)(2,1)}, u32[]{:S(2)}) copy-start(bf16[128,1024]{1,0:T(8,128)(2,1)} %q_ref.1) | copy-start | bytes 786436
  32.2 1.6 %collective-permute-start.12 = (bf16[64,2048]{1,0:T(8,128)(2,1)S(1)}, bf16[64,2048]{1,0:T(8,128)(2,1)S(1)}, u32[]{:S(2)}, u32[]{:S(2)}) collective-permute-start(bf16[64,2048]{1,0:T(8,128)(2,1)S(1)} %get-tuple-element.22), channel_id=1, source_target_pairs={{0,1},{1,0},{2,3},{3,2},{4,5},{5,4},{6,7},{7,6},{8,9},{9,8},{10,11... | collective-permute-start | bytes 786440 | tf_op jit(solution)/shard_map/ppermute | solution.py:163
  33.9 9.9 %collective-permute-start.13 = (bf16[32,2048]{1,0:T(8,128)(2,1)S(1)}, bf16[32,2048]{1,0:T(8,128)(2,1)S(1)}, u32[]{:S(2)}, u32[]{:S(2)}) collective-permute-start(bf16[32,2048]{1,0:T(8,128)(2,1)S(1)} %slice.236), channel_id=1, source_target_pairs={{0,2},{1,3},{2,0},{3,1},{4,6},{5,7},{6,4},{7,5},{8,10},{9,11},{10,... | collective-permute-start | bytes 393224 | tf_op jit(solution)/shard_map/ppermute | solution.py:163
  39.3 5.4 %collective-permute-start = (bf16[64,4096]{1,0:T(8,128)(2,1)S(1)}, bf16[64,4096]{1,0:T(8,128)(2,1)S(1)}, u32[]{:S(2)}, u32[]{:S(2)}) collective-permute-start(bf16[64,4096]{1,0:T(8,128)(2,1)S(1)} %get-tuple-element.15), channel_id=1, source_target_pairs={{0,1},{1,0},{2,3},{3,2},{4,5},{5,4},{6,7},{7,6},{8,9},{9,8},{10,11... | collective-permute-start | bytes 1572872 | tf_op jit(solution)/shard_map/ppermute | solution.py:163
  39.4 16.1 %collective-permute-start.4 = (bf16[64,6144]{1,0:T(8,128)(2,1)S(1)}, bf16[64,6144]{1,0:T(8,128)(2,1)S(1)}, u32[]{:S(2)}, u32[]{:S(2)}) collective-permute-start(bf16[64,6144]{1,0:T(8,128)(2,1)S(1)} %get-tuple-element.18), channel_id=1, source_target_pairs={{0,1},{1,0},{2,3},{3,2},{4,5},{5,4},{6,7},{7,6},{8,9},{9,8},{10,11... | collective-permute-start | bytes 2359304 | tf_op jit(solution)/shard_map/ppermute | solution.py:163
  43.7 2.5 %collective-permute-start.8 = (bf16[64,4096]{1,0:T(8,128)(2,1)S(1)}, bf16[64,4096]{1,0:T(8,128)(2,1)S(1)}, u32[]{:S(2)}, u32[]{:S(2)}) collective-permute-start(bf16[64,4096]{1,0:T(8,128)(2,1)S(1)} %get-tuple-element.20), channel_id=1, source_target_pairs={{0,1},{1,0},{2,3},{3,2},{4,5},{5,4},{6,7},{7,6},{8,9},{9,8},{10,11... | collective-permute-start | bytes 1572872 | tf_op jit(solution)/shard_map/ppermute | solution.py:163
  43.9 31.5 %collective-permute-start.14 = (bf16[16,2048]{1,0:T(8,128)(2,1)S(1)}, bf16[16,2048]{1,0:T(8,128)(2,1)S(1)}, u32[]{:S(2)}, u32[]{:S(2)}) collective-permute-start(bf16[16,2048]{1,0:T(8,128)(2,1)S(1)} %slice.240), channel_id=1, source_target_pairs={{0,4},{1,5},{2,6},{3,7},{4,0},{5,1},{6,2},{7,3},{8,12},{9,13},{10,... | collective-permute-start | bytes 196616 | tf_op jit(solution)/shard_map/ppermute | solution.py:163
  44.7 9.2 %collective-permute-start.1 = (bf16[32,4096]{1,0:T(8,128)(2,1)S(1)}, bf16[32,4096]{1,0:T(8,128)(2,1)S(1)}, u32[]{:S(2)}, u32[]{:S(2)}) collective-permute-start(bf16[32,4096]{1,0:T(8,128)(2,1)S(1)} %slice.234), channel_id=1, source_target_pairs={{0,2},{1,3},{2,0},{3,1},{4,6},{5,7},{6,4},{7,5},{8,10},{9,11},{10,... | collective-permute-start | bytes 786440 | tf_op jit(solution)/shard_map/ppermute | solution.py:163
  46.3 13.3 %collective-permute-start.9 = (bf16[32,4096]{1,0:T(8,128)(2,1)S(1)}, bf16[32,4096]{1,0:T(8,128)(2,1)S(1)}, u32[]{:S(2)}, u32[]{:S(2)}) collective-permute-start(bf16[32,4096]{1,0:T(8,128)(2,1)S(1)} %slice.233), channel_id=1, source_target_pairs={{0,2},{1,3},{2,0},{3,1},{4,6},{5,7},{6,4},{7,5},{8,10},{9,11},{10,... | collective-permute-start | bytes 786440 | tf_op jit(solution)/shard_map/ppermute | solution.py:163
  54.0 7.1 %collective-permute-start.2 = (bf16[16,4096]{1,0:T(8,128)(2,1)S(1)}, bf16[16,4096]{1,0:T(8,128)(2,1)S(1)}, u32[]{:S(2)}, u32[]{:S(2)}) collective-permute-start(bf16[16,4096]{1,0:T(8,128)(2,1)S(1)} %slice.238), channel_id=1, source_target_pairs={{0,4},{1,5},{2,6},{3,7},{4,0},{5,1},{6,2},{7,3},{8,12},{9,13},{10,... | collective-permute-start | bytes 393224 | tf_op jit(solution)/shard_map/ppermute | solution.py:163
  55.6 11.6 %collective-permute-start.5 = (bf16[32,6144]{1,0:T(8,128)(2,1)S(1)}, bf16[32,6144]{1,0:T(8,128)(2,1)S(1)}, u32[]{:S(2)}, u32[]{:S(2)}) collective-permute-start(bf16[32,6144]{1,0:T(8,128)(2,1)S(1)} %slice.232), channel_id=1, source_target_pairs={{0,2},{1,3},{2,0},{3,1},{4,6},{5,7},{6,4},{7,5},{8,10},{9,11},{10,... | collective-permute-start | bytes 1179656 | tf_op jit(solution)/shard_map/ppermute | solution.py:163
  59.7 9.3 %collective-permute-start.10 = (bf16[16,4096]{1,0:T(8,128)(2,1)S(1)}, bf16[16,4096]{1,0:T(8,128)(2,1)S(1)}, u32[]{:S(2)}, u32[]{:S(2)}) collective-permute-start(bf16[16,4096]{1,0:T(8,128)(2,1)S(1)} %slice.237), channel_id=1, source_target_pairs={{0,4},{1,5},{2,6},{3,7},{4,0},{5,1},{6,2},{7,3},{8,12},{9,13},{10,... | collective-permute-start | bytes 393224 | tf_op jit(solution)/shard_map/ppermute | solution.py:163
  61.1 21.2 %collective-permute-start.3 = (bf16[8,4096]{1,0:T(8,128)(2,1)S(1)}, bf16[8,4096]{1,0:T(8,128)(2,1)S(1)}, u32[]{:S(2)}, u32[]{:S(2)}) collective-permute-start(bf16[8,4096]{1,0:T(8,128)(2,1)S(1)} %slice.242), channel_id=1, source_target_pairs={{0,8},{1,9},{2,10},{3,11},{4,12},{5,13},{6,14},{7,15},{8,0},{9,1},... | collective-permute-start | bytes 196616 | tf_op jit(solution)/shard_map/ppermute | solution.py:163
  67.3 15.0 %copy-start = (s32[8,16384]{1,0:T(8,128)S(1)}, s32[8,16384]{1,0:T(8,128)}, u32[]{:S(2)}) copy-start(s32[8,16384]{1,0:T(8,128)} %codes_ref.1) | copy-start | bytes 1572868
  67.3 15.0 %copy-start.2 = (s32[8,128]{1,0:T(8,128)S(1)}, s32[8,128]{1,0:T(8,128)}, u32[]{:S(2)}) copy-start(s32[8,128]{1,0:T(8,128)} %exponents_ref.1) | copy-start | bytes 12292
  67.4 7.6 %collective-permute-start.6 = (bf16[16,6144]{1,0:T(8,128)(2,1)S(1)}, bf16[16,6144]{1,0:T(8,128)(2,1)S(1)}, u32[]{:S(2)}, u32[]{:S(2)}) collective-permute-start(bf16[16,6144]{1,0:T(8,128)(2,1)S(1)} %slice.235), channel_id=1, source_target_pairs={{0,4},{1,5},{2,6},{3,7},{4,0},{5,1},{6,2},{7,3},{8,12},{9,13},{10,... | collective-permute-start | bytes 589832 | tf_op jit(solution)/shard_map/ppermute | solution.py:163
  69.0 13.4 %collective-permute-start.11 = (bf16[8,4096]{1,0:T(8,128)(2,1)S(1)}, bf16[8,4096]{1,0:T(8,128)(2,1)S(1)}, u32[]{:S(2)}, u32[]{:S(2)}) collective-permute-start(bf16[8,4096]{1,0:T(8,128)(2,1)S(1)} %slice.241), channel_id=1, source_target_pairs={{0,8},{1,9},{2,10},{3,11},{4,12},{5,13},{6,14},{7,15},{8,0},{9,1},... | collective-permute-start | bytes 196616 | tf_op jit(solution)/shard_map/ppermute | solution.py:163
  75.0 7.3 %collective-permute-start.7 = (bf16[8,6144]{1,0:T(8,128)(2,1)S(1)}, bf16[8,6144]{1,0:T(8,128)(2,1)S(1)}, u32[]{:S(2)}, u32[]{:S(2)}) collective-permute-start(bf16[8,6144]{1,0:T(8,128)(2,1)S(1)} %slice.239), channel_id=1, source_target_pairs={{0,8},{1,9},{2,10},{3,11},{4,12},{5,13},{6,14},{7,15},{8,0},{9,1},... | collective-permute-start | bytes 294920 | tf_op jit(solution)/shard_map/ppermute | solution.py:163
  75.4 6.9 %collective-permute-start.15 = (bf16[8,2048]{1,0:T(8,128)(2,1)S(1)}, bf16[8,2048]{1,0:T(8,128)(2,1)S(1)}, u32[]{:S(2)}, u32[]{:S(2)}) collective-permute-start(bf16[8,2048]{1,0:T(8,128)(2,1)S(1)} %slice.243), channel_id=1, source_target_pairs={{0,8},{1,9},{2,10},{3,11},{4,12},{5,13},{6,14},{7,15},{8,0},{9,1},... | collective-permute-start | bytes 98312 | tf_op jit(solution)/shard_map/ppermute | solution.py:163

commit v2 on v1

v2 whole, which is shorter than its diff:
```python
import functools
import math

import jax
import jax.numpy as jnp
from jax import lax
from jax.experimental import pallas as pl
from jax.experimental.pallas import tpu as pltpu
from jax.sharding import PartitionSpec as P

QUERY_HEADS = 128
KEY_VALUE_HEADS = 8
HEAD_SIZE = 128
HBLK = 128
masked_score = -1e30

LIMIT = 20 << 20
PARTS = ((4, 'yz', 8), (5, 'yz', 3), (5, 'yz', 3), (2, 'yz', 4))
AHEAD = (3, 3, 2)
TILE = 512
SPLIT = {}
EVENTS = ((0, 0), (1, -1), (0, 1), (1, 0), (2, -1), (0, 2), (1, 1), (2, 0), (3, -1), (1, 2), (2, 1), (0, 3), (3, 0), (2, 2), (3, 1), (1, 3), (0, 4), (3, 2), (2, 3), (1, 4), (3, 3), (2, 4), (3, 4))


def events(bits):
    if bits == 4:
        return EVENTS
    steps = range(-1, bits + 1)
    return [(part, step) for step in steps for part, (_, _, ahead) in enumerate(PARTS) if step >= 0 or (part and ahead)]


def halving_order(kind, bits):
    if kind == "yz":
        return list(range(bits))
    if kind == "zyz":
        return [0, 2, 1, *range(3, bits)]
    return [0, *range(2, bits), 1]


def reversed_bits(index, bits):
    result = 0
    for bit in range(bits):
        result = result + ((index >> bit) & 1) * (1 << (bits - 1 - bit))
    return result


def fetches(start, w_ref, buffer_ref, arrived):
    tiles, _, tile = buffer_ref.shape
    return [
        pltpu.make_async_copy(w_ref.at[:, pl.ds(start + index * tile, tile)], buffer_ref.at[index], arrived.at[index])
        for index in range(tiles)
    ]


def prepare_kernel(bits, place_ref, q_ref, queries_ref, held, arrived):
    copy = pltpu.make_async_copy(q_ref, held, arrived)
    copy.start()
    total_rows = q_ref.shape[0]
    column = lax.broadcasted_iota(jnp.int32, (total_rows, total_rows), 1)
    order = jnp.where(column == token_of_row(place_ref, total_rows, bits), 1.0, 0.0).astype(jnp.bfloat16)
    copy.wait()
    queries_ref[...] = jnp.dot(order, held[...], preferred_element_type=jnp.float32).astype(jnp.bfloat16)


def token_of_row(place_ref, total_rows, bits):
    rows = total_rows >> bits
    row = lax.broadcasted_iota(jnp.int32, (total_rows, 1), 0)
    return (place_ref[0] ^ reversed_bits(row // rows, bits)) * rows + row % rows


def attend(bits, place_ref, queries_ref, kv_ref, context_ref):
    total_rows = queries_ref.shape[0]
    visible = key_tokens(place_ref, bits, (total_rows, total_rows)) <= token_of_row(place_ref, total_rows, bits)
    key = kv_ref[:, :HEAD_SIZE]
    value = kv_ref[:, HEAD_SIZE:]
    for head in range(queries_ref.shape[1] // HEAD_SIZE):
        columns = slice(head * HEAD_SIZE, (head + 1) * HEAD_SIZE)
        scores = lax.dot_general(
            queries_ref[:, columns], key, (((1,), (1,)), ((), ())), preferred_element_type=jnp.float32
        ) * (1.0 / math.sqrt(HEAD_SIZE))
        scores = jnp.where(visible, scores, masked_score)
        top = jnp.max(scores, axis=1, keepdims=True)
        weights = jnp.where(visible, jnp.exp(scores - top), 0.0)
        total = jnp.sum(weights, axis=1, keepdims=True)
        high = weights.astype(jnp.bfloat16)
        low = (weights - high.astype(jnp.float32)).astype(jnp.bfloat16)
        weighted = jnp.dot(high, value, preferred_element_type=jnp.float32)
        weighted = weighted + jnp.dot(low, value, preferred_element_type=jnp.float32)
        context_ref[:, columns] = (weighted / total).astype(jnp.bfloat16)


def fetch_kernel(start, place_ref, w_ref, buffer_ref, arrived):
    copies = fetches(start, w_ref, buffer_ref, arrived)
    for copy in copies:
        copy.start()
    for copy in copies:
        copy.wait()


def multiply(context_ref, weight, at, keep_ref, send_ref):
    half = keep_ref.shape[0]
    columns = slice(at, at + weight.shape[1])
    product = jnp.dot(context_ref[...], weight, preferred_element_type=jnp.float32)
    keep_ref[:, columns] = product[:half]
    send_ref[:, columns] = product[half:].astype(jnp.bfloat16)


def part_kernel(bits, start, with_attention, *refs):
    if with_attention:
        place_ref, queries_ref, kv_ref, w_ref, *refs = refs
        *ahead_refs, context_ref, keep_ref, send_ref, buffer, arrived = refs
    else:
        context_ref, w_ref, *refs = refs
        *ahead_refs, keep_ref, send_ref, buffer, arrived = refs
    tiles = [(ref, index) for ref in ahead_refs for index in range(ref.shape[0])]
    missing = keep_ref.shape[1] // TILE - len(tiles)
    copies = fetches(start + len(tiles) * TILE, w_ref, buffer, arrived) if missing else []
    for copy in copies:
        copy.start()
    if with_attention:
        attend(bits, place_ref, queries_ref, kv_ref, context_ref)
    for index, (ref, tile) in enumerate(tiles):
        multiply(context_ref, ref[tile], index * TILE, keep_ref, send_ref)
    for index, copy in enumerate(copies):
        copy.wait()
        multiply(context_ref, buffer[index], (len(tiles) + index) * TILE, keep_ref, send_ref)


VMEM = pl.BlockSpec(memory_space=pltpu.VMEM)
SMEM = pl.BlockSpec(memory_space=pltpu.SMEM)
ANYWHERE = pl.BlockSpec(memory_space=pl.ANY)


def prepare(place, queries, bits):
    return pl.pallas_call(
        functools.partial(prepare_kernel, bits),
        in_specs=[SMEM, ANYWHERE],
        out_specs=VMEM,
        out_shape=jax.ShapeDtypeStruct(queries.shape, queries.dtype),
        scratch_shapes=[pltpu.VMEM(queries.shape, queries.dtype), pltpu.SemaphoreType.DMA],
        compiler_params=pltpu.CompilerParams(vmem_limit_bytes=LIMIT),
        cost_estimate=pl.CostEstimate(flops=0, bytes_accessed=4 * queries.size, transcendentals=0),
    )(place, queries)


def fetch(place, weight, start, tiles):
    return pl.pallas_call(
        functools.partial(fetch_kernel, start),
        in_specs=[SMEM, ANYWHERE],
        out_specs=VMEM,
        out_shape=jax.ShapeDtypeStruct((tiles, weight.shape[0], TILE), weight.dtype),
        scratch_shapes=[pltpu.SemaphoreType.DMA((tiles,))],
        compiler_params=pltpu.CompilerParams(vmem_limit_bytes=LIMIT),
    )(place, weight)


def project_part(bits, start, columns, context, first_inputs, weight, ahead):
    with_attention = context is None
    depth = weight.shape[0]
    total_rows = (first_inputs[1] if with_attention else context).shape[0]
    missing = max(columns // TILE - sum(array.shape[0] for array in ahead), 1)
    out_shape = [
        jax.ShapeDtypeStruct((total_rows // 2, columns), jnp.float32),
        jax.ShapeDtypeStruct((total_rows // 2, columns), jnp.bfloat16),
    ]
    inputs, in_specs = [context, weight], [VMEM, ANYWHERE]
    if with_attention:
        out_shape = [jax.ShapeDtypeStruct((total_rows, depth), jnp.bfloat16)] + out_shape
        inputs, in_specs = [*first_inputs, weight], [SMEM, VMEM, VMEM, ANYWHERE]
    return pl.pallas_call(
        functools.partial(part_kernel, bits, start, with_attention),
        in_specs=in_specs + [VMEM] * len(ahead),
        out_specs=[VMEM] * len(out_shape),
        out_shape=out_shape,
        scratch_shapes=[pltpu.VMEM((missing, depth, TILE), jnp.bfloat16), pltpu.SemaphoreType.DMA((missing,))],
        compiler_params=pltpu.CompilerParams(vmem_limit_bytes=LIMIT),
    )(*inputs, *ahead)


def finish_kernel(bounds, codes_ref, exponents_ref, *refs):
    *pieces, out_ref = refs
    rows = out_ref.shape[0]
    i = lax.broadcasted_iota(jnp.int32, (HBLK, HBLK), 0)
    common = i & lax.broadcasted_iota(jnp.int32, (HBLK, HBLK), 1)
    parity = jnp.zeros((HBLK, HBLK), jnp.int32)
    for bit in range(HBLK.bit_length() - 1):
        parity = parity ^ (common >> bit)
    table = (1 - 2 * (parity & 1)).astype(jnp.bfloat16)
    scale = jnp.exp2(exponents_ref[...].astype(jnp.float32))
    for start, keep_ref, got_ref in zip(bounds, pieces[::2], pieces[1::2]):
        summed = keep_ref[...] + got_ref[...].astype(jnp.float32)
        blocks = summed.shape[1] // HBLK
        rest = jnp.concatenate([summed[:, b * HBLK:(b + 1) * HBLK] for b in range(blocks)], axis=0)
        rotated = jnp.zeros_like(rest)
        for _ in range(3):
            piece = rest.astype(jnp.bfloat16)
            rotated = rotated + jnp.dot(piece, table, preferred_element_type=jnp.float32)
            rest = rest - piece.astype(jnp.float32)
        rotated = rotated * (1.0 / math.sqrt(HBLK))
        for b in range(blocks):
            block = start // HBLK + b
            columns = slice(block * HBLK, (block + 1) * HBLK)
            residual = codes_ref[:, columns].astype(jnp.float32) * scale[:, block:block + 1]
            out_ref[:, columns] = (residual + rotated[b * rows:(b + 1) * rows]).astype(jnp.bfloat16)


def finish(codes, exponents, pieces, bounds):
    rows, width = codes.shape
    spare = max(8 - rows, 0)
    inputs = [jnp.pad(x, ((0, spare), (0, 0))) for x in (codes, exponents, *pieces)]
    out = pl.pallas_call(
        functools.partial(finish_kernel, bounds),
        in_specs=[VMEM] * len(inputs),
        out_specs=VMEM,
        out_shape=jax.ShapeDtypeStruct((rows + spare, width), jnp.bfloat16),
        compiler_params=pltpu.CompilerParams(vmem_limit_bytes=LIMIT),
    )(*inputs)
    return out[:rows]


def passed_across(value, axis, mask):
    return lax.ppermute(value, axis, [(source, source ^ mask) for source in range(lax.axis_size(axis))])


def pack_kernel(local_heads, place_ref, key_ref, value_ref, packed_ref, held, arrived):
    copies = [
        pltpu.make_async_copy(ref, held.at[index], arrived.at[index]) for index, ref in enumerate((key_ref, value_ref))
    ]
    for copy in copies:
        copy.start()
    for copy in copies:
        copy.wait()
    query_group = QUERY_HEADS // KEY_VALUE_HEADS
    chip = place_ref[0] // 2
    for away in range(packed_ref.shape[0]):
        head = (chip ^ away) * 2 * local_heads // query_group
        columns = pl.ds(pl.multiple_of(head * HEAD_SIZE, HEAD_SIZE), HEAD_SIZE)
        for index in range(2):
            packed_ref[away, :, index * HEAD_SIZE:(index + 1) * HEAD_SIZE] = held[index, :, columns]


def shared_out(place, key_rows, value_rows, weight, bits, local_heads):
    rows = key_rows.shape[0]
    chips = 1 << (bits - 1)
    packed = pl.pallas_call(
        functools.partial(pack_kernel, local_heads),
        out_shape=jax.ShapeDtypeStruct((chips, rows, 2 * HEAD_SIZE), key_rows.dtype),
        in_specs=[SMEM, ANYWHERE, ANYWHERE],
        out_specs=VMEM,
        scratch_shapes=[pltpu.VMEM((2, *key_rows.shape), key_rows.dtype), pltpu.SemaphoreType.DMA((2,))],
        compiler_params=pltpu.CompilerParams(vmem_limit_bytes=LIMIT),
    )(place, *(pltpu.with_memory_space_constraint(x, pltpu.HBM) for x in (key_rows, value_rows)))
    held = packed[:, None]
    ahead = []
    fetched = 0
    for bit in range(bits - 1):
        halves = held.reshape(-1, 2, *held.shape[1:])
        keep, send = halves[:, 0], halves[:, 1]
        got = passed_across(send, "tensor", 2 << bit)
        if bit < len(AHEAD):
            now, _ = lax.optimization_barrier((place, send))
            ahead.append(fetch(now, weight, fetched * TILE, AHEAD[bit]))
            fetched += AHEAD[bit]
            keep, got, ahead[-1] = lax.optimization_barrier((keep, got, ahead[-1]))
        held = jnp.concatenate([keep, got], axis=1)
    held = held[0]
    got = passed_across(held, "tensor", 1)
    return jnp.concatenate([held, got], axis=0).reshape(2 * chips * rows, 2 * HEAD_SIZE), ahead


def key_tokens(place_ref, bits, shape):
    index = lax.broadcasted_iota(jnp.int32, shape, 1)
    rows = shape[1] >> bits
    block = index // rows
    chips = 1 << (bits - 1)
    away = block // chips + 2 * (block % chips)
    return (place_ref[0] ^ away) * rows + index % rows


def body(encoded_query_rows, encoded_key_rows, head_value_rows, quant_codes, exponents, out_weight):
    total_rows, query_width = encoded_query_rows.shape
    depth, width = out_weight.shape
    devices = lax.axis_size("tensor")
    bits = devices.bit_length() - 1
    local_heads = query_width // HEAD_SIZE
    rows = total_rows // devices

    place = lax.axis_index("tensor").astype(jnp.int32).reshape(1)
    weight = pltpu.with_memory_space_constraint(out_weight, pltpu.HBM)
    queries = prepare(place, encoded_query_rows, bits)
    kv, ahead = shared_out(place, encoded_key_rows, head_value_rows, weight, bits, local_heads)
    unit = width // sum(columns for columns, *_ in PARTS)
    starts = [unit * sum(columns for columns, *_ in PARTS[:part]) for part in range(len(PARTS))]

    context = token = None
    state = {}
    fetched = {0: ahead}
    for part, step in events(bits):
        columns, order, tiles = PARTS[part]
        columns *= unit
        order = halving_order(order, bits)
        if step == -2:
            left, keep, got = state[part]
            *early, token = lax.optimization_barrier((*got[:-1], token))
            state[part] = left, keep, [*early, got[-1]]
            continue
        if step == -1:
            now = place if token is None else lax.optimization_barrier((place, token))[0]
            token = fetch(now, weight, starts[part], tiles)
            fetched[part] = [token]
            continue
        if step == 0:
            if context is None:
                context, keep, send = project_part(bits, starts[part], columns, None, (place, queries, kv), weight, ahead)
            else:
                held, token = lax.optimization_barrier((context, token))
                keep, send = project_part(bits, starts[part], columns, held, None, weight, fetched.get(part, []))
            left = list(range(1, bits))
        else:
            left, keep, got = state[part]
            keep, token, *got = lax.optimization_barrier((keep, token, *got))
            if step == bits:
                state[part] = left, keep, got
                token = got[0]
                continue
            bounds = [sum(piece.shape[1] for piece in got[:i]) for i in range(len(got) + 1)]
            summed = jnp.concatenate(
                [
                    keep[:, begin:end] + piece.astype(jnp.float32)
                    for begin, end, piece in zip(bounds, bounds[1:], got)
                ],
                axis=1,
            ).reshape((2,) * len(left) + (rows, columns))
            axis = left.index(order[step])
            keep, send = (
                lax.index_in_dim(summed, side, axis, keepdims=False).reshape(-1, columns) for side in (0, 1)
            )
            send = send.astype(jnp.bfloat16)
            left = left[:axis] + left[axis + 1:]
        token = send
        cuts = [columns]
        if bits == 4 and step < 2:
            cuts = SPLIT.get((part, step), cuts)
        ends = [0, *(cut * TILE for cut in cuts if cut * TILE < columns), columns]
        pieces = [send[:, begin:end] for begin, end in zip(ends, ends[1:])]
        state[part] = left, keep, [passed_across(piece, "tensor", 1 << order[step]) for piece in pieces]
    pieces = [array for part in range(len(PARTS)) for array in (state[part][1], state[part][2][0])]
    return finish(quant_codes, exponents, pieces, starts)


def solution(mesh):
    return jax.shard_map(
        body,
        mesh=mesh,
        in_specs=(
            P("groups", "tensor"),
            P(("groups", "tensor"), None),
            P(("groups", "tensor"), None),
            P(("groups", "tensor"), None),
            P(("groups", "tensor"), None),
            P("tensor", None),
        ),
        out_specs=P(("groups", "tensor"), None),
        check_vma=False,
    )
```

time: 83.8 us -> 66.8 us (0.80)
  waiting for transfers between devices: 31.3 us -> 12.8 us
  other arithmetic: 10.2 us -> 0.76 us
  Pallas kernels: 16.7 us -> 23.4 us
  starting transfers between devices: 23 us -> 28.1 us
  local copies, waits for them, and re-layouts: 2.07 us -> 0.86 us
    ppermute x16 -> x20, starting transfers between devices: 15.6 us -> 28.1 us  [passed_across(): lax.ppermute(value, axis, [(source, source ^ mask) for source in range(la...]
    ppermute x16 -> x20, waiting for transfers between devices: 24.4 us -> 12.8 us  [passed_across(): lax.ppermute(value, axis, [(source, source ^ mask) for source in range(la...]
    unnamed x15 -> x0, other arithmetic: 8.92 us -> none
    all_to_all x1 -> x0, starting transfers between devices: 7.39 us -> none  [body(): lax.all_to_all(packed, 'tensor', 0, 0)]
    all_to_all x1 -> x0, waiting for transfers between devices: 6.89 us -> none  [body(): lax.all_to_all(packed, 'tensor', 0, 0)]
    pallas_call x5 -> x13, Pallas kernels: 16.7 us -> 23.4 us  [the longest x6 11.5 us: fetch(): pl.pallas_call(functools.partial(fetch_kernel, start), in_specs=[SMEM, AN...]
    unnamed x6 -> x18, local copies, waits for them, and re-layouts: 0.96 us -> 0.04 us
  transfers between devices with their start and end apart: 17 -> 20, of which waited for: 7 -> 8; matrix products, arithmetic and copies ran while one was open for 1% -> 1% of each run, Pallas kernels for 11% -> 30%
where the time goes in v2:
time: 66.8 us; the launch traced here: 66.5 us
  starting transfers between devices  28.1 us (42%)
  Pallas kernels  23.4 us (35%)
  waiting for transfers between devices  12.8 us (19%)
  local copies, waits for them, and re-layouts  0.86 us (1%)
  other arithmetic  0.76 us (1%)
    ppermute x20, starting transfers between devices, passed_across(): lax.ppermute(value, axis, [(source, source ^ mask) for source in range(la...  28.1 us
    ppermute x20, waiting for transfers between devices, passed_across(): lax.ppermute(value, axis, [(source, source ^ mask) for source in range(la...  12.8 us
    pallas_call x6, Pallas kernels, fetch(): pl.pallas_call(functools.partial(fetch_kernel, start), in_specs=[SMEM, AN...  11.5 us
    pallas_call x4, Pallas kernels, project_part(): pl.pallas_call(functools.partial(part_kernel, bits, start, with_attention...  9.76 us
  transfers between devices with their start and end apart: 20, of which 8 were waited for; matrix products, arithmetic and copies ran while one was open for 1% of the time, Pallas kernels for 30%

profile of v2, /device:TPU:0, one launch (start us, length us, event | category | flops | bytes accessed | tf_op | source)
XLA Modules:
  0.0 66.5 jit_solution(17781581552559323634)
XLA Ops:
  0.8 3.0 %collective-permute-start = (bf16[4,1,8,256]{3,2,1,0:T(8,128)(2,1)S(1)}, bf16[4,1,8,256]{3,2,1,0:T(8,128)(2,1)S(1)}, u32[]{:S(2)}, u32[]{:S(2)}) collective-permute-start(bf16[4,1,8,256]{3,2,1,0:T(8,128)(2,1)S(1)} %get-tuple-element.127), channel_id=1, source_target_pairs={{0,2},{1,3},{2,0},{3,1},{4,6},{5,7},{6,4},{7,5},{8,10},{9,11},{10,... | collective-permute-start | bytes 49160 | tf_op jit(solution)/shard_map/ppermute | solution.py:222
  3.8 1.9 %shard_map.66.refs_4_ = bf16[3,1024,512]{2,1,0:T(8,128)(2,1)S(1)} custom-call(s32[1]{0:T(128)} %bitcast.place_ref.refs_0_, bf16[1024,16384]{1,0:T(8,128)(2,1)} %refs_1_.5), custom_call_target="tpu_custom_call" | custom-call | tf_op jit(solution)/shard_map/pallas_call | solution.py:147
  5.8 1.9 %collective-permute-start.1 = (bf16[2,2,8,256]{3,2,1,0:T(8,128)(2,1)S(1)}, bf16[2,2,8,256]{3,2,1,0:T(8,128)(2,1)S(1)}, u32[]{:S(2)}, u32[]{:S(2)}) collective-permute-start(bf16[2,2,8,256]{3,2,1,0:T(8,128)(2,1)S(1)} %get-tuple-element.125), channel_id=1, source_target_pairs={{0,4},{1,5},{2,6},{3,7},{4,0},{5,1},{6,2},{7,3},{8,12},{9,13},{10,... | collective-permute-start | bytes 49160 | tf_op jit(solution)/shard_map/ppermute | solution.py:222
  7.7 1.9 %shard_map.67.refs_5_ = bf16[3,1024,512]{2,1,0:T(8,128)(2,1)S(1)} custom-call(s32[1]{0:T(128)} %bitcast.place_ref.refs_0_, bf16[1024,16384]{1,0:T(8,128)(2,1)} %refs_1_.5), custom_call_target="tpu_custom_call" | custom-call | tf_op jit(solution)/shard_map/pallas_call | solution.py:147
  9.6 2.9 %collective-permute-start.2 = (bf16[1,4,8,256]{3,2,1,0:T(8,128)(2,1)S(1)}, bf16[1,4,8,256]{3,2,1,0:T(8,128)(2,1)S(1)}, u32[]{:S(2)}, u32[]{:S(2)}) collective-permute-start(bf16[1,4,8,256]{3,2,1,0:T(8,128)(2,1)S(1)} %get-tuple-element.123), channel_id=1, source_target_pairs={{0,8},{1,9},{2,10},{3,11},{4,12},{5,13},{6,14},{7,15},{8,0},{9,1},... | collective-permute-start | bytes 49160 | tf_op jit(solution)/shard_map/ppermute | solution.py:222
  12.5 1.6 %shard_map.68.refs_6_ = bf16[2,1024,512]{2,1,0:T(8,128)(2,1)S(1)} custom-call(s32[1]{0:T(128)} %bitcast.place_ref.refs_0_, bf16[1024,16384]{1,0:T(8,128)(2,1)} %refs_1_.5), custom_call_target="tpu_custom_call" | custom-call | tf_op jit(solution)/shard_map/pallas_call | solution.py:147
  15.6 1.8 %shard_map.69 = (bf16[128,1024]{1,0:T(8,128)(2,1)S(1)}, f32[64,4096]{1,0:T(8,128)S(1)}, bf16[64,4096]{1,0:T(8,128)(2,1)S(1)}) custom-call(s32[1]{0:T(128)} %bitcast.place_ref.refs_0_, bf16[128,1024]{1,0:T(8,128)(2,1)S(1)} %shard_map.64.refs_1_, bf16[128,256]{1,0:T(8,128)(2,1)S(1)} %maximum_bitcast_fusion.refs_2_, bf16[1024,16384]{1,0:T(8,128)(2,1)} %refs_1_.5, ...), custom_call_target="tpu_custom_call" | custom-call | tf_op jit(solution)/shard_map/pallas_call | solution.py:170
  17.6 1.9 %shard_map.70.refs_2_ = bf16[3,1024,512]{2,1,0:T(8,128)(2,1)S(1)} custom-call(s32[1]{0:T(128)} %bitcast.place_ref.refs_0_, bf16[1024,16384]{1,0:T(8,128)(2,1)} %refs_1_.5), custom_call_target="tpu_custom_call" | custom-call | tf_op jit(solution)/shard_map/pallas_call | solution.py:147
  19.7 1.8 %collective-permute-start.5 = (bf16[32,4096]{1,0:T(8,128)(2,1)S(1)}, bf16[32,4096]{1,0:T(8,128)(2,1)S(1)}, u32[]{:S(2)}, u32[]{:S(2)}) collective-permute-start(bf16[32,4096]{1,0:T(8,128)(2,1)S(1)} %slice.206), channel_id=1, source_target_pairs={{0,2},{1,3},{2,0},{3,1},{4,6},{5,7},{6,4},{7,5},{8,10},{9,11},{10,... | collective-permute-start | bytes 786440 | tf_op jit(solution)/shard_map/ppermute | solution.py:222
  21.6 3.6 %shard_map.71 = (f32[64,5120]{1,0:T(8,128)S(1)}, bf16[64,5120]{1,0:T(8,128)(2,1)S(1)}) custom-call(bf16[128,1024]{1,0:T(8,128)(2,1)S(1)} %get-tuple-element.100.refs_0_, bf16[1024,16384]{1,0:T(8,128)(2,1)} %refs_1_.5, bf16[3,1024,512]{2,1,0:T(8,128)(2,1)S(1)} %shard_map.70.refs_2_), custom_call_target="tpu_custom_call" | custom-call | tf_op jit(solution)/shard_map/pallas_call | solution.py:170
  25.3 1.9 %shard_map.72.refs_2_ = bf16[3,1024,512]{2,1,0:T(8,128)(2,1)S(1)} custom-call(s32[1]{0:T(128)} %bitcast.place_ref.refs_0_, bf16[1024,16384]{1,0:T(8,128)(2,1)} %refs_1_.5), custom_call_target="tpu_custom_call" | custom-call | tf_op jit(solution)/shard_map/pallas_call | solution.py:147
  28.6 1.8 %collective-permute-start.7 = (bf16[32,5120]{1,0:T(8,128)(2,1)S(1)}, bf16[32,5120]{1,0:T(8,128)(2,1)S(1)}, u32[]{:S(2)}, u32[]{:S(2)}) collective-permute-start(bf16[32,5120]{1,0:T(8,128)(2,1)S(1)} %slice.205), channel_id=1, source_target_pairs={{0,2},{1,3},{2,0},{3,1},{4,6},{5,7},{6,4},{7,5},{8,10},{9,11},{10,... | collective-permute-start | bytes 983048 | tf_op jit(solution)/shard_map/ppermute | solution.py:222
  30.4 1.6 %collective-permute-start.9 = (bf16[16,4096]{1,0:T(8,128)(2,1)S(1)}, bf16[16,4096]{1,0:T(8,128)(2,1)S(1)}, u32[]{:S(2)}, u32[]{:S(2)}) collective-permute-start(bf16[16,4096]{1,0:T(8,128)(2,1)S(1)} %slice.210), channel_id=1, source_target_pairs={{0,4},{1,5},{2,6},{3,7},{4,0},{5,1},{6,2},{7,3},{8,12},{9,13},{10,... | collective-permute-start | bytes 393224 | tf_op jit(solution)/shard_map/ppermute | solution.py:222
  32.0 3.6 %shard_map.73 = (f32[64,5120]{1,0:T(8,128)S(1)}, bf16[64,5120]{1,0:T(8,128)(2,1)S(1)}) custom-call(bf16[128,1024]{1,0:T(8,128)(2,1)S(1)} %get-tuple-element.100.refs_0_, bf16[1024,16384]{1,0:T(8,128)(2,1)} %refs_1_.5, bf16[3,1024,512]{2,1,0:T(8,128)(2,1)S(1)} %shard_map.72.refs_2_), custom_call_target="tpu_custom_call" | custom-call | tf_op jit(solution)/shard_map/pallas_call | solution.py:170
  35.7 2.3 %shard_map.74.refs_2_ = bf16[4,1024,512]{2,1,0:T(8,128)(2,1)S(1)} custom-call(s32[1]{0:T(128)} %bitcast.place_ref.refs_0_, bf16[1024,16384]{1,0:T(8,128)(2,1)} %refs_1_.5), custom_call_target="tpu_custom_call" | custom-call | tf_op jit(solution)/shard_map/pallas_call | solution.py:147
  38.1 1.7 %collective-permute-start.12 = (bf16[16,5120]{1,0:T(8,128)(2,1)S(1)}, bf16[16,5120]{1,0:T(8,128)(2,1)S(1)}, u32[]{:S(2)}, u32[]{:S(2)}) collective-permute-start(bf16[16,5120]{1,0:T(8,128)(2,1)S(1)} %slice.208), channel_id=1, source_target_pairs={{0,4},{1,5},{2,6},{3,7},{4,0},{5,1},{6,2},{7,3},{8,12},{9,13},{10,... | collective-permute-start | bytes 491528 | tf_op jit(solution)/shard_map/ppermute | solution.py:222
  40.1 1.6 %collective-permute-start.10 = (bf16[32,5120]{1,0:T(8,128)(2,1)S(1)}, bf16[32,5120]{1,0:T(8,128)(2,1)S(1)}, u32[]{:S(2)}, u32[]{:S(2)}) collective-permute-start(bf16[32,5120]{1,0:T(8,128)(2,1)S(1)} %slice.204), channel_id=1, source_target_pairs={{0,2},{1,3},{2,0},{3,1},{4,6},{5,7},{6,4},{7,5},{8,10},{9,11},{10,... | collective-permute-start | bytes 983048 | tf_op jit(solution)/shard_map/ppermute | solution.py:222
  41.7 2.7 %collective-permute-start.13 = (bf16[8,4096]{1,0:T(8,128)(2,1)S(1)}, bf16[8,4096]{1,0:T(8,128)(2,1)S(1)}, u32[]{:S(2)}, u32[]{:S(2)}) collective-permute-start(bf16[8,4096]{1,0:T(8,128)(2,1)S(1)} %slice.214), channel_id=1, source_target_pairs={{0,8},{1,9},{2,10},{3,11},{4,12},{5,13},{6,14},{7,15},{8,0},{9,1},... | collective-permute-start | bytes 196616 | tf_op jit(solution)/shard_map/ppermute | solution.py:222
  45.3 3.8 %collective-permute-done.10 = bf16[32,5120]{1,0:T(8,128)(2,1)S(1)} collective-permute-done((bf16[32,5120]{1,0:T(8,128)(2,1)S(1)}, bf16[32,5120]{1,0:T(8,128)(2,1)S(1)}, u32[]{:S(2)}, u32[]{:S(2)}) %collective-permute-start.10) | collective-permute-done | bytes 327712 | tf_op jit(solution)/shard_map/ppermute | solution.py:222
  50.5 1.3 %collective-permute-start.15 = (bf16[16,5120]{1,0:T(8,128)(2,1)S(1)}, bf16[16,5120]{1,0:T(8,128)(2,1)S(1)}, u32[]{:S(2)}, u32[]{:S(2)}) collective-permute-start(bf16[16,5120]{1,0:T(8,128)(2,1)S(1)} %slice.207), channel_id=1, source_target_pairs={{0,4},{1,5},{2,6},{3,7},{4,0},{5,1},{6,2},{7,3},{8,12},{9,13},{10,... | collective-permute-start | bytes 491528 | tf_op jit(solution)/shard_map/ppermute | solution.py:222
  51.8 2.7 %collective-permute-start.16 = (bf16[8,5120]{1,0:T(8,128)(2,1)S(1)}, bf16[8,5120]{1,0:T(8,128)(2,1)S(1)}, u32[]{:S(2)}, u32[]{:S(2)}) collective-permute-start(bf16[8,5120]{1,0:T(8,128)(2,1)S(1)} %slice.212), channel_id=1, source_target_pairs={{0,8},{1,9},{2,10},{3,11},{4,12},{5,13},{6,14},{7,15},{8,0},{9,1},... | collective-permute-start | bytes 245768 | tf_op jit(solution)/shard_map/ppermute | solution.py:222
  55.7 3.6 %collective-permute-done.15 = bf16[16,5120]{1,0:T(8,128)(2,1)S(1)} collective-permute-done((bf16[16,5120]{1,0:T(8,128)(2,1)S(1)}, bf16[16,5120]{1,0:T(8,128)(2,1)S(1)}, u32[]{:S(2)}, u32[]{:S(2)}) %collective-permute-start.15) | collective-permute-done | bytes 163872 | tf_op jit(solution)/shard_map/ppermute | solution.py:222
  60.0 2.4 %collective-permute-start.19 = (bf16[8,2048]{1,0:T(8,128)(2,1)S(1)}, bf16[8,2048]{1,0:T(8,128)(2,1)S(1)}, u32[]{:S(2)}, u32[]{:S(2)}) collective-permute-start(bf16[8,2048]{1,0:T(8,128)(2,1)S(1)} %slice.215), channel_id=1, source_target_pairs={{0,8},{1,9},{2,10},{3,11},{4,12},{5,13},{6,14},{7,15},{8,0},{9,1},... | collective-permute-start | bytes 98312 | tf_op jit(solution)/shard_map/ppermute | solution.py:222
  62.4 2.6 %collective-permute-done.18.refs_5_ = bf16[8,5120]{1,0:T(8,128)(2,1)S(1)} collective-permute-done((bf16[8,5120]{1,0:T(8,128)(2,1)S(1)}, bf16[8,5120]{1,0:T(8,128)(2,1)S(1)}, u32[]{:S(2)}, u32[]{:S(2)}) %collective-permute-start.18) | collective-permute-done | bytes 81952 | tf_op jit(solution)/shard_map/ppermute | solution.py:222
  (96 shorter events, 10.1 us)
Async XLA Ops:
  0.8 4.9 %collective-permute-start = (bf16[4,1,8,256]{3,2,1,0:T(8,128)(2,1)S(1)}, bf16[4,1,8,256]{3,2,1,0:T(8,128)(2,1)S(1)}, u32[]{:S(2)}, u32[]{:S(2)}) collective-permute-start(bf16[4,1,8,256]{3,2,1,0:T(8,128)(2,1)S(1)} %get-tuple-element.127), channel_id=1, source_target_pairs={{0,2},{1,3},{2,0},{3,1},{4,6},{5,7},{6,4},{7,5},{8,10},{9,11},{10,... | collective-permute-start | bytes 49160 | tf_op jit(solution)/shard_map/ppermute | solution.py:222
  5.8 3.8 %collective-permute-start.1 = (bf16[2,2,8,256]{3,2,1,0:T(8,128)(2,1)S(1)}, bf16[2,2,8,256]{3,2,1,0:T(8,128)(2,1)S(1)}, u32[]{:S(2)}, u32[]{:S(2)}) collective-permute-start(bf16[2,2,8,256]{3,2,1,0:T(8,128)(2,1)S(1)} %get-tuple-element.125), channel_id=1, source_target_pairs={{0,4},{1,5},{2,6},{3,7},{4,0},{5,1},{6,2},{7,3},{8,12},{9,13},{10,... | collective-permute-start | bytes 49160 | tf_op jit(solution)/shard_map/ppermute | solution.py:222
  9.6 4.7 %collective-permute-start.2 = (bf16[1,4,8,256]{3,2,1,0:T(8,128)(2,1)S(1)}, bf16[1,4,8,256]{3,2,1,0:T(8,128)(2,1)S(1)}, u32[]{:S(2)}, u32[]{:S(2)}) collective-permute-start(bf16[1,4,8,256]{3,2,1,0:T(8,128)(2,1)S(1)} %get-tuple-element.123), channel_id=1, source_target_pairs={{0,8},{1,9},{2,10},{3,11},{4,12},{5,13},{6,14},{7,15},{8,0},{9,1},... | collective-permute-start | bytes 49160 | tf_op jit(solution)/shard_map/ppermute | solution.py:222
  14.4 1.2 %collective-permute-start.3 = (bf16[8,8,256]{2,1,0:T(8,128)(2,1)S(1)}, bf16[8,8,256]{2,1,0:T(8,128)(2,1)S(1)}, u32[]{:S(2)}, u32[]{:S(2)}) collective-permute-start(bf16[8,8,256]{2,1,0:T(8,128)(2,1)S(1)} %maximum_bitcast_fusion.2), channel_id=1, source_target_pairs={{0,1},{1,0},{2,3},{3,2},{4,5},{5,4},{6,7},{7,6},{8,9},{9,8},{10,11... | collective-permute-start | bytes 98312 | tf_op jit(solution)/shard_map/ppermute | solution.py:222
  17.4 2.1 %collective-permute-start.4 = (bf16[64,4096]{1,0:T(8,128)(2,1)S(1)}, bf16[64,4096]{1,0:T(8,128)(2,1)S(1)}, u32[]{:S(2)}, u32[]{:S(2)}) collective-permute-start(bf16[64,4096]{1,0:T(8,128)(2,1)S(1)} %get-tuple-element.77), channel_id=1, source_target_pairs={{0,1},{1,0},{2,3},{3,2},{4,5},{5,4},{6,7},{7,6},{8,9},{9,8},{10,11... | collective-permute-start | bytes 1572872 | tf_op jit(solution)/shard_map/ppermute | solution.py:222
  19.7 8.6 %collective-permute-start.5 = (bf16[32,4096]{1,0:T(8,128)(2,1)S(1)}, bf16[32,4096]{1,0:T(8,128)(2,1)S(1)}, u32[]{:S(2)}, u32[]{:S(2)}) collective-permute-start(bf16[32,4096]{1,0:T(8,128)(2,1)S(1)} %slice.206), channel_id=1, source_target_pairs={{0,2},{1,3},{2,0},{3,1},{4,6},{5,7},{6,4},{7,5},{8,10},{9,11},{10,... | collective-permute-start | bytes 786440 | tf_op jit(solution)/shard_map/ppermute | solution.py:222
  25.2 3.3 %collective-permute-start.6 = (bf16[64,5120]{1,0:T(8,128)(2,1)S(1)}, bf16[64,5120]{1,0:T(8,128)(2,1)S(1)}, u32[]{:S(2)}, u32[]{:S(2)}) collective-permute-start(bf16[64,5120]{1,0:T(8,128)(2,1)S(1)} %get-tuple-element.83), channel_id=1, source_target_pairs={{0,1},{1,0},{2,3},{3,2},{4,5},{5,4},{6,7},{7,6},{8,9},{9,8},{10,11... | collective-permute-start | bytes 1966088 | tf_op jit(solution)/shard_map/ppermute | solution.py:222
  28.6 9.4 %collective-permute-start.7 = (bf16[32,5120]{1,0:T(8,128)(2,1)S(1)}, bf16[32,5120]{1,0:T(8,128)(2,1)S(1)}, u32[]{:S(2)}, u32[]{:S(2)}) collective-permute-start(bf16[32,5120]{1,0:T(8,128)(2,1)S(1)} %slice.205), channel_id=1, source_target_pairs={{0,2},{1,3},{2,0},{3,1},{4,6},{5,7},{6,4},{7,5},{8,10},{9,11},{10,... | collective-permute-start | bytes 983048 | tf_op jit(solution)/shard_map/ppermute | solution.py:222
  30.4 11.2 %collective-permute-start.9 = (bf16[16,4096]{1,0:T(8,128)(2,1)S(1)}, bf16[16,4096]{1,0:T(8,128)(2,1)S(1)}, u32[]{:S(2)}, u32[]{:S(2)}) collective-permute-start(bf16[16,4096]{1,0:T(8,128)(2,1)S(1)} %slice.210), channel_id=1, source_target_pairs={{0,4},{1,5},{2,6},{3,7},{4,0},{5,1},{6,2},{7,3},{8,12},{9,13},{10,... | collective-permute-start | bytes 393224 | tf_op jit(solution)/shard_map/ppermute | solution.py:222
  35.6 4.2 %collective-permute-start.8 = (bf16[64,5120]{1,0:T(8,128)(2,1)S(1)}, bf16[64,5120]{1,0:T(8,128)(2,1)S(1)}, u32[]{:S(2)}, u32[]{:S(2)}) collective-permute-start(bf16[64,5120]{1,0:T(8,128)(2,1)S(1)} %get-tuple-element.92), channel_id=1, source_target_pairs={{0,1},{1,0},{2,3},{3,2},{4,5},{5,4},{6,7},{7,6},{8,9},{9,8},{10,11... | collective-permute-start | bytes 1966088 | tf_op jit(solution)/shard_map/ppermute | solution.py:222
  38.1 11.8 %collective-permute-start.12 = (bf16[16,5120]{1,0:T(8,128)(2,1)S(1)}, bf16[16,5120]{1,0:T(8,128)(2,1)S(1)}, u32[]{:S(2)}, u32[]{:S(2)}) collective-permute-start(bf16[16,5120]{1,0:T(8,128)(2,1)S(1)} %slice.208), channel_id=1, source_target_pairs={{0,4},{1,5},{2,6},{3,7},{4,0},{5,1},{6,2},{7,3},{8,12},{9,13},{10,... | collective-permute-start | bytes 491528 | tf_op jit(solution)/shard_map/ppermute | solution.py:222
  40.1 9.0 %collective-permute-start.10 = (bf16[32,5120]{1,0:T(8,128)(2,1)S(1)}, bf16[32,5120]{1,0:T(8,128)(2,1)S(1)}, u32[]{:S(2)}, u32[]{:S(2)}) collective-permute-start(bf16[32,5120]{1,0:T(8,128)(2,1)S(1)} %slice.204), channel_id=1, source_target_pairs={{0,2},{1,3},{2,0},{3,1},{4,6},{5,7},{6,4},{7,5},{8,10},{9,11},{10,... | collective-permute-start | bytes 983048 | tf_op jit(solution)/shard_map/ppermute | solution.py:222
  41.7 7.4 %slice-start = ((f32[64,5120]{1,0:T(8,128)}), f32[32,5120]{1,0:T(8,128)S(1)}, s32[]{:S(2)}) async-start(f32[64,5120]{1,0:T(8,128)} %copy-done.3), calls=%async_computation | async-start | bytes 1310720 | tf_op jit(solution)/shard_map/slice | solution.py:336
  41.7 12.7 %collective-permute-start.13 = (bf16[8,4096]{1,0:T(8,128)(2,1)S(1)}, bf16[8,4096]{1,0:T(8,128)(2,1)S(1)}, u32[]{:S(2)}, u32[]{:S(2)}) collective-permute-start(bf16[8,4096]{1,0:T(8,128)(2,1)S(1)} %slice.214), channel_id=1, source_target_pairs={{0,8},{1,9},{2,10},{3,11},{4,12},{5,13},{6,14},{7,15},{8,0},{9,1},... | collective-permute-start | bytes 196616 | tf_op jit(solution)/shard_map/ppermute | solution.py:222
  45.2 4.0 %collective-permute-start.11 = (bf16[64,2048]{1,0:T(8,128)(2,1)S(1)}, bf16[64,2048]{1,0:T(8,128)(2,1)S(1)}, u32[]{:S(2)}, u32[]{:S(2)}) collective-permute-start(bf16[64,2048]{1,0:T(8,128)(2,1)S(1)} %get-tuple-element.102), channel_id=1, source_target_pairs={{0,1},{1,0},{2,3},{3,2},{4,5},{5,4},{6,7},{7,6},{8,9},{9,8},{10,11... | collective-permute-start | bytes 786440 | tf_op jit(solution)/shard_map/ppermute | solution.py:222
  49.3 5.1 %collective-permute-start.14 = (bf16[32,2048]{1,0:T(8,128)(2,1)S(1)}, bf16[32,2048]{1,0:T(8,128)(2,1)S(1)}, u32[]{:S(2)}, u32[]{:S(2)}) collective-permute-start(bf16[32,2048]{1,0:T(8,128)(2,1)S(1)} %slice.209), channel_id=1, source_target_pairs={{0,2},{1,3},{2,0},{3,1},{4,6},{5,7},{6,4},{7,5},{8,10},{9,11},{10,... | collective-permute-start | bytes 393224 | tf_op jit(solution)/shard_map/ppermute | solution.py:222
  50.4 8.8 %slice-start.3 = ((f32[32,5120]{1,0:T(8,128)}), f32[16,5120]{1,0:T(8,128)S(1)}, s32[]{:S(2)}) async-start(f32[32,5120]{1,0:T(8,128)} %copy-done.6), calls=%async_computation.3 | async-start | bytes 655360 | tf_op jit(solution)/shard_map/slice | solution.py:336
  50.5 14.9 %copy-start = (s32[8,16384]{1,0:T(8,128)S(1)}, s32[8,16384]{1,0:T(8,128)}, u32[]{:S(2)}) copy-start(s32[8,16384]{1,0:T(8,128)} %codes_ref.1) | copy-start | bytes 1572868
  50.5 14.8 %copy-start.2 = (s32[8,128]{1,0:T(8,128)S(1)}, s32[8,128]{1,0:T(8,128)}, u32[]{:S(2)}) copy-start(s32[8,128]{1,0:T(8,128)} %exponents_ref.1) | copy-start | bytes 12292
  50.5 8.7 %collective-permute-start.15 = (bf16[16,5120]{1,0:T(8,128)(2,1)S(1)}, bf16[16,5120]{1,0:T(8,128)(2,1)S(1)}, u32[]{:S(2)}, u32[]{:S(2)}) collective-permute-start(bf16[16,5120]{1,0:T(8,128)(2,1)S(1)} %slice.207), channel_id=1, source_target_pairs={{0,4},{1,5},{2,6},{3,7},{4,0},{5,1},{6,2},{7,3},{8,12},{9,13},{10,... | collective-permute-start | bytes 491528 | tf_op jit(solution)/shard_map/ppermute | solution.py:222
  51.8 8.0 %collective-permute-start.16 = (bf16[8,5120]{1,0:T(8,128)(2,1)S(1)}, bf16[8,5120]{1,0:T(8,128)(2,1)S(1)}, u32[]{:S(2)}, u32[]{:S(2)}) collective-permute-start(bf16[8,5120]{1,0:T(8,128)(2,1)S(1)} %slice.212), channel_id=1, source_target_pairs={{0,8},{1,9},{2,10},{3,11},{4,12},{5,13},{6,14},{7,15},{8,0},{9,1},... | collective-permute-start | bytes 245768 | tf_op jit(solution)/shard_map/ppermute | solution.py:222
  54.5 5.4 %collective-permute-start.17 = (bf16[16,2048]{1,0:T(8,128)(2,1)S(1)}, bf16[16,2048]{1,0:T(8,128)(2,1)S(1)}, u32[]{:S(2)}, u32[]{:S(2)}) collective-permute-start(bf16[16,2048]{1,0:T(8,128)(2,1)S(1)} %slice.213), channel_id=1, source_target_pairs={{0,4},{1,5},{2,6},{3,7},{4,0},{5,1},{6,2},{7,3},{8,12},{9,13},{10,... | collective-permute-start | bytes 196616 | tf_op jit(solution)/shard_map/ppermute | solution.py:222
  59.3 5.7 %collective-permute-start.18 = (bf16[8,5120]{1,0:T(8,128)(2,1)S(1)}, bf16[8,5120]{1,0:T(8,128)(2,1)S(1)}, u32[]{:S(2)}, u32[]{:S(2)}) collective-permute-start(bf16[8,5120]{1,0:T(8,128)(2,1)S(1)} %slice.211), channel_id=1, source_target_pairs={{0,8},{1,9},{2,10},{3,11},{4,12},{5,13},{6,14},{7,15},{8,0},{9,1},... | collective-permute-start | bytes 245768 | tf_op jit(solution)/shard_map/ppermute | solution.py:222
  60.0 5.4 %collective-permute-start.19 = (bf16[8,2048]{1,0:T(8,128)(2,1)S(1)}, bf16[8,2048]{1,0:T(8,128)(2,1)S(1)}, u32[]{:S(2)}, u32[]{:S(2)}) collective-permute-start(bf16[8,2048]{1,0:T(8,128)(2,1)S(1)} %slice.215), channel_id=1, source_target_pairs={{0,8},{1,9},{2,10},{3,11},{4,12},{5,13},{6,14},{7,15},{8,0},{9,1},... | collective-permute-start | bytes 98312 | tf_op jit(solution)/shard_map/ppermute | solution.py:222
  (11 other events, 32.7 us)

commit v3 on v2

--- a/solution.py
+++ b/solution.py
@@ -14,12 +14,12 @@
 HBLK = 128
 masked_score = -1e30
 
-LIMIT = 20 << 20
-PARTS = ((4, 'yz', 8), (5, 'yz', 3), (5, 'yz', 3), (2, 'yz', 4))
-AHEAD = (3, 3, 2)
+LIMIT = 12 << 20
+PARTS = ((4, 'yz', 8), (5, 'yz', 3), (4, 'zyz', 0), (3, 'yz', 3))
+AHEAD = (4, 4)
 TILE = 512
 SPLIT = {}
-EVENTS = ((0, 0), (1, -1), (0, 1), (1, 0), (2, -1), (0, 2), (1, 1), (2, 0), (3, -1), (1, 2), (2, 1), (0, 3), (3, 0), (2, 2), (3, 1), (1, 3), (0, 4), (3, 2), (2, 3), (1, 4), (3, 3), (2, 4), (3, 4))
+EVENTS = ((0, 0), (1, -1), (0, 1), (1, 0), (2, 0), (0, 2), (1, 1), (2, 1), (3, -1), (3, 0), (1, 2), (3, 1), (2, 2), (0, 3), (1, 3), (3, 2), (2, 3), (0, 4), (1, 4), (3, 3), (2, 4), (3, 4))
 
 
 def events(bits):
@@ -178,8 +178,8 @@
 
 
 def finish_kernel(bounds, codes_ref, exponents_ref, *refs):
-    *pieces, out_ref = refs
-    rows = out_ref.shape[0]
+    pieces = refs[:2 * len(bounds)]
+    out_ref, *done_refs, stored = refs[len(refs) - len(bounds) - 2:]
     i = lax.broadcasted_iota(jnp.int32, (HBLK, HBLK), 0)
     common = i & lax.broadcasted_iota(jnp.int32, (HBLK, HBLK), 1)
     parity = jnp.zeros((HBLK, HBLK), jnp.int32)
@@ -187,9 +187,11 @@
         parity = parity ^ (common >> bit)
     table = (1 - 2 * (parity & 1)).astype(jnp.bfloat16)
     scale = jnp.exp2(exponents_ref[...].astype(jnp.float32))
-    for start, keep_ref, got_ref in zip(bounds, pieces[::2], pieces[1::2]):
+    stores = []
+    for index, (start, keep_ref, got_ref, done_ref) in enumerate(zip(bounds, pieces[::2], pieces[1::2], done_refs)):
+        rows, width = done_ref.shape
         summed = keep_ref[...] + got_ref[...].astype(jnp.float32)
-        blocks = summed.shape[1] // HBLK
+        blocks = width // HBLK
         rest = jnp.concatenate([summed[:, b * HBLK:(b + 1) * HBLK] for b in range(blocks)], axis=0)
         rotated = jnp.zeros_like(rest)
         for _ in range(3):
@@ -199,23 +201,32 @@
         rotated = rotated * (1.0 / math.sqrt(HBLK))
         for b in range(blocks):
             block = start // HBLK + b
-            columns = slice(block * HBLK, (block + 1) * HBLK)
-            residual = codes_ref[:, columns].astype(jnp.float32) * scale[:, block:block + 1]
-            out_ref[:, columns] = (residual + rotated[b * rows:(b + 1) * rows]).astype(jnp.bfloat16)
-
-
-def finish(codes, exponents, pieces, bounds):
-    rows, width = codes.shape
-    spare = max(8 - rows, 0)
-    inputs = [jnp.pad(x, ((0, spare), (0, 0))) for x in (codes, exponents, *pieces)]
-    out = pl.pallas_call(
+            codes = codes_ref[:, block * HBLK:(block + 1) * HBLK].astype(jnp.float32)
+            done_ref[:, b * HBLK:(b + 1) * HBLK] = (
+                codes * scale[:, block:block + 1] + rotated[b * rows:(b + 1) * rows]
+            ).astype(jnp.bfloat16)
+        store = pltpu.make_async_copy(done_ref, out_ref.at[:, pl.ds(start, width)], stored.at[index])
+        store.start()
+        stores.append(store)
+    for store in stores:
+        store.wait()
+
+
+def finish(codes, exponents, pieces, bounds, out):
+    inputs, in_specs, aliases = [codes, exponents, *pieces], [VMEM] * (2 + len(pieces)), {}
+    if out is not None:
+        aliases = {len(inputs): 0}
+        inputs, in_specs = [*inputs, out], [*in_specs, ANYWHERE]
+    return pl.pallas_call(
         functools.partial(finish_kernel, bounds),
-        in_specs=[VMEM] * len(inputs),
-        out_specs=VMEM,
-        out_shape=jax.ShapeDtypeStruct((rows + spare, width), jnp.bfloat16),
+        in_specs=in_specs,
+        out_specs=ANYWHERE,
+        out_shape=jax.ShapeDtypeStruct(codes.shape, jnp.bfloat16),
+        input_output_aliases=aliases,
+        scratch_shapes=[pltpu.VMEM(keep.shape, jnp.bfloat16) for keep in pieces[::2]]
+        + [pltpu.SemaphoreType.DMA((len(bounds),))],
         compiler_params=pltpu.CompilerParams(vmem_limit_bytes=LIMIT),
     )(*inputs)
-    return out[:rows]
 
 
 def passed_across(value, axis, mask):
@@ -295,14 +306,27 @@
     context = token = None
     state = {}
     fetched = {0: ahead}
-    for part, step in events(bits):
+
+    def summed_halves(part, step):
+        nonlocal token
+        left, keep, got = state.pop(part)
+        keep, got, token = lax.optimization_barrier((keep, got, token))
+        got = got[0] if len(got) == 1 else jnp.concatenate(got, axis=1)
+        if step == bits:
+            return left, keep, got
+        columns = keep.shape[1]
+        summed = (keep + got.astype(jnp.float32)).reshape((2,) * len(left) + (rows, columns))
+        axis = left.index(halving_order(PARTS[part][1], bits)[step])
+        keep, send = (lax.index_in_dim(summed, side, axis, keepdims=False).reshape(-1, columns) for side in (0, 1))
+        return left[:axis] + left[axis + 1:], keep, send.astype(jnp.bfloat16)
+
+    for part, step, *joined in events(bits):
         columns, order, tiles = PARTS[part]
         columns *= unit
-        order = halving_order(order, bits)
         if step == -2:
             left, keep, got = state[part]
-            *early, token = lax.optimization_barrier((*got[:-1], token))
-            state[part] = left, keep, [*early, got[-1]]
+            early, token = lax.optimization_barrier((got[0], token))
+            state[part] = left, keep, (early, *got[1:])
             continue
         if step == -1:
             now = place if token is None else lax.optimization_barrier((place, token))[0]
@@ -317,35 +341,27 @@
                 keep, send = project_part(bits, starts[part], columns, held, None, weight, fetched.get(part, []))
             left = list(range(1, bits))
         else:
-            left, keep, got = state[part]
-            keep, token, *got = lax.optimization_barrier((keep, token, *got))
-            if step == bits:
-                state[part] = left, keep, got
-                token = got[0]
-                continue
-            bounds = [sum(piece.shape[1] for piece in got[:i]) for i in range(len(got) + 1)]
-            summed = jnp.concatenate(
-                [
-                    keep[:, begin:end] + piece.astype(jnp.float32)
-                    for begin, end, piece in zip(bounds, bounds[1:], got)
-                ],
-                axis=1,
-            ).reshape((2,) * len(left) + (rows, columns))
-            axis = left.index(order[step])
-            keep, send = (
-                lax.index_in_dim(summed, side, axis, keepdims=False).reshape(-1, columns) for side in (0, 1)
-            )
-            send = send.astype(jnp.bfloat16)
-            left = left[:axis] + left[axis + 1:]
-        token = send
-        cuts = [columns]
-        if bits == 4 and step < 2:
-            cuts = SPLIT.get((part, step), cuts)
-        ends = [0, *(cut * TILE for cut in cuts if cut * TILE < columns), columns]
-        pieces = [send[:, begin:end] for begin, end in zip(ends, ends[1:])]
-        state[part] = left, keep, [passed_across(piece, "tensor", 1 << order[step]) for piece in pieces]
-    pieces = [array for part in range(len(PARTS)) for array in (state[part][1], state[part][2][0])]
-    return finish(quant_codes, exponents, pieces, starts)
+            left, keep, send = summed_halves(part, step)
+            for other in joined:
+                _, keep_too, send_too = summed_halves(other, step)
+                keep = jnp.concatenate([keep, keep_too], axis=1)
+                send = jnp.concatenate([send, send_too], axis=1)
+        if step == bits:
+            state[part], token = (left, keep, send), send
+            continue
+        cut = SPLIT.get(part, 0) * TILE if step == 1 else 0
+        token = (send[:, :cut], send[:, cut:]) if cut else (send,)
+        mask = 1 << halving_order(order, bits)[step]
+        state[part] = left, keep, tuple(passed_across(piece, "tensor", mask) for piece in token)
+    spare = max(8 - rows, 0)
+    codes, scales = (jnp.pad(x, ((0, spare), (0, 0))) for x in (quant_codes, exponents))
+    *early, last = state
+    out = None
+    for group in (early, [last]):
+        if group:
+            pieces = [jnp.pad(x, ((0, spare), (0, 0))) for part in group for x in state[part][1:]]
+            out = finish(codes, scales, pieces, [starts[part] for part in group], out)
+    return out[:rows]
 
 
 def solution(mesh):

time: 66.8 us -> 61.8 us (0.925)
  waiting for transfers between devices: 12.8 us -> 8.81 us
    ppermute x20, waiting for transfers between devices: 12.8 us -> 8.81 us  [passed_across(): lax.ppermute(value, axis, [(source, source ^ mask) for source in range(la...]
    pallas_call x6 -> x4, Pallas kernels: 11.5 us -> 8.25 us  [fetch(): pl.pallas_call(functools.partial(fetch_kernel, start), in_specs=[SMEM, AN...]
    pallas_call x4, Pallas kernels: 9.76 us -> 11.6 us  [project_part(): pl.pallas_call(functools.partial(part_kernel, bits, start, with_attention...]
    pallas_call x1 -> x2, Pallas kernels: 1.12 us -> 1.9 us  [finish(): pl.pallas_call(functools.partial(finish_kernel, bounds), in_specs=in_spec...]
  transfers between devices with their start and end apart: 20 -> 20, of which waited for: 8 -> 8; matrix products, arithmetic and copies ran while one was open for 1% -> 2% of each run, Pallas kernels for 30% -> 32%
where the time goes in v3:
time: 61.8 us; the launch traced here: 61.5 us
  starting transfers between devices  27.9 us (45%)
  Pallas kernels  22.8 us (37%)
  waiting for transfers between devices  8.81 us (14%)
  other arithmetic  0.82 us (1%)
  local copies, waits for them, and re-layouts  0.62 us (1%)
    ppermute x20, starting transfers between devices, passed_across(): lax.ppermute(value, axis, [(source, source ^ mask) for source in range(la...  27.9 us
    pallas_call x4, Pallas kernels, project_part(): pl.pallas_call(functools.partial(part_kernel, bits, start, with_attention...  11.6 us
    ppermute x20, waiting for transfers between devices, passed_across(): lax.ppermute(value, axis, [(source, source ^ mask) for source in range(la...  8.81 us
    pallas_call x4, Pallas kernels, fetch(): pl.pallas_call(functools.partial(fetch_kernel, start), in_specs=[SMEM, AN...  8.25 us
    pallas_call x2, Pallas kernels, finish(): pl.pallas_call(functools.partial(finish_kernel, bounds), in_specs=in_spec...  1.9 us
  transfers between devices with their start and end apart: 20, of which 8 were waited for; matrix products, arithmetic and copies ran while one was open for 2% of the time, Pallas kernels for 32%

profile of v3, /device:TPU:0, one launch (start us, length us, event | category | flops | bytes accessed | tf_op | source)
XLA Modules:
  0.0 61.5 jit_solution(1836748718048778509)
XLA Ops:
  0.8 3.0 %collective-permute-start = (bf16[4,1,8,256]{3,2,1,0:T(8,128)(2,1)S(1)}, bf16[4,1,8,256]{3,2,1,0:T(8,128)(2,1)S(1)}, u32[]{:S(2)}, u32[]{:S(2)}) collective-permute-start(bf16[4,1,8,256]{3,2,1,0:T(8,128)(2,1)S(1)} %get-tuple-element.117), channel_id=1, source_target_pairs={{0,2},{1,3},{2,0},{3,1},{4,6},{5,7},{6,4},{7,5},{8,10},{9,11},{10,... | collective-permute-start | bytes 49160 | tf_op jit(solution)/shard_map/ppermute | solution.py:233
  3.8 2.2 %shard_map.66.refs_4_ = bf16[4,1024,512]{2,1,0:T(8,128)(2,1)S(1)} custom-call(s32[1]{0:T(128)} %bitcast.place_ref.refs_0_, bf16[1024,16384]{1,0:T(8,128)(2,1)} %refs_1_.5), custom_call_target="tpu_custom_call" | custom-call | tf_op jit(solution)/shard_map/pallas_call | solution.py:147
  6.1 1.6 %collective-permute-start.1 = (bf16[2,2,8,256]{3,2,1,0:T(8,128)(2,1)S(1)}, bf16[2,2,8,256]{3,2,1,0:T(8,128)(2,1)S(1)}, u32[]{:S(2)}, u32[]{:S(2)}) collective-permute-start(bf16[2,2,8,256]{3,2,1,0:T(8,128)(2,1)S(1)} %get-tuple-element.115), channel_id=1, source_target_pairs={{0,4},{1,5},{2,6},{3,7},{4,0},{5,1},{6,2},{7,3},{8,12},{9,13},{10,... | collective-permute-start | bytes 49160 | tf_op jit(solution)/shard_map/ppermute | solution.py:233
  7.8 2.2 %shard_map.67.refs_5_ = bf16[4,1024,512]{2,1,0:T(8,128)(2,1)S(1)} custom-call(s32[1]{0:T(128)} %bitcast.place_ref.refs_0_, bf16[1024,16384]{1,0:T(8,128)(2,1)} %refs_1_.5), custom_call_target="tpu_custom_call" | custom-call | tf_op jit(solution)/shard_map/pallas_call | solution.py:147
  10.0 2.7 %collective-permute-start.2 = (bf16[1,4,8,256]{3,2,1,0:T(8,128)(2,1)S(1)}, bf16[1,4,8,256]{3,2,1,0:T(8,128)(2,1)S(1)}, u32[]{:S(2)}, u32[]{:S(2)}) collective-permute-start(bf16[1,4,8,256]{3,2,1,0:T(8,128)(2,1)S(1)} %get-tuple-element.114), channel_id=1, source_target_pairs={{0,8},{1,9},{2,10},{3,11},{4,12},{5,13},{6,14},{7,15},{8,0},{9,1},... | collective-permute-start | bytes 49160 | tf_op jit(solution)/shard_map/ppermute | solution.py:233
  12.7 2.0 %collective-permute-done.2 = bf16[1,4,8,256]{3,2,1,0:T(8,128)(2,1)S(1)} collective-permute-done((bf16[1,4,8,256]{3,2,1,0:T(8,128)(2,1)S(1)}, bf16[1,4,8,256]{3,2,1,0:T(8,128)(2,1)S(1)}, u32[]{:S(2)}, u32[]{:S(2)}) %collective-permute-start.2) | collective-permute-done | bytes 16416 | tf_op jit(solution)/shard_map/ppermute | solution.py:233
  15.1 0.9 %collective-permute-done.3 = bf16[8,8,256]{2,1,0:T(8,128)(2,1)S(1)} collective-permute-done((bf16[8,8,256]{2,1,0:T(8,128)(2,1)S(1)}, bf16[8,8,256]{2,1,0:T(8,128)(2,1)S(1)}, u32[]{:S(2)}, u32[]{:S(2)}) %collective-permute-start.3) | collective-permute-done | bytes 32800 | tf_op jit(solution)/shard_map/ppermute | solution.py:233
  16.0 1.8 %shard_map.68 = (bf16[128,1024]{1,0:T(8,128)(2,1)S(1)}, f32[64,4096]{1,0:T(8,128)S(1)}, bf16[64,4096]{1,0:T(8,128)(2,1)S(1)}) custom-call(s32[1]{0:T(128)} %bitcast.place_ref.refs_0_, bf16[128,1024]{1,0:T(8,128)(2,1)S(1)} %shard_map.64.refs_1_, bf16[128,256]{1,0:T(8,128)(2,1)S(1)} %maximum_bitcast_fusion.refs_2_, bf16[1024,16384]{1,0:T(8,128)(2,1)} %refs_1_.5, ...), custom_call_target="tpu_custom_call" | custom-call | tf_op jit(solution)/shard_map/pallas_call | solution.py:170
  18.0 1.9 %shard_map.69.refs_2_ = bf16[3,1024,512]{2,1,0:T(8,128)(2,1)S(1)} custom-call(s32[1]{0:T(128)} %bitcast.place_ref.refs_0_, bf16[1024,16384]{1,0:T(8,128)(2,1)} %refs_1_.5), custom_call_target="tpu_custom_call" | custom-call | tf_op jit(solution)/shard_map/pallas_call | solution.py:147
  20.1 1.5 %collective-permute-start.7 = (bf16[32,4096]{1,0:T(8,128)(2,1)S(1)}, bf16[32,4096]{1,0:T(8,128)(2,1)S(1)}, u32[]{:S(2)}, u32[]{:S(2)}) collective-permute-start(bf16[32,4096]{1,0:T(8,128)(2,1)S(1)} %slice.202), channel_id=1, source_target_pairs={{0,2},{1,3},{2,0},{3,1},{4,6},{5,7},{6,4},{7,5},{8,10},{9,11},{10,... | collective-permute-start | bytes 786440 | tf_op jit(solution)/shard_map/ppermute | solution.py:233
  21.6 3.6 %shard_map.70 = (f32[64,5120]{1,0:T(8,128)S(1)}, bf16[64,5120]{1,0:T(8,128)(2,1)S(1)}) custom-call(bf16[128,1024]{1,0:T(8,128)(2,1)S(1)} %get-tuple-element.86.refs_0_, bf16[1024,16384]{1,0:T(8,128)(2,1)} %refs_1_.5, bf16[3,1024,512]{2,1,0:T(8,128)(2,1)S(1)} %shard_map.69.refs_2_), custom_call_target="tpu_custom_call" | custom-call | tf_op jit(solution)/shard_map/pallas_call | solution.py:170
  25.4 3.9 %shard_map.71 = (f32[64,4096]{1,0:T(8,128)S(1)}, bf16[64,4096]{1,0:T(8,128)(2,1)S(1)}) custom-call(bf16[128,1024]{1,0:T(8,128)(2,1)S(1)} %get-tuple-element.86.refs_0_, bf16[1024,16384]{1,0:T(8,128)(2,1)} %refs_1_.5), custom_call_target="tpu_custom_call" | custom-call | tf_op jit(solution)/shard_map/pallas_call | solution.py:170
  29.9 1.6 %collective-permute-start.12 = (bf16[16,4096]{1,0:T(8,128)(2,1)S(1)}, bf16[16,4096]{1,0:T(8,128)(2,1)S(1)}, u32[]{:S(2)}, u32[]{:S(2)}) collective-permute-start(bf16[16,4096]{1,0:T(8,128)(2,1)S(1)} %slice.206), channel_id=1, source_target_pairs={{0,4},{1,5},{2,6},{3,7},{4,0},{5,1},{6,2},{7,3},{8,12},{9,13},{10,... | collective-permute-start | bytes 393224 | tf_op jit(solution)/shard_map/ppermute | solution.py:233
  33.2 1.9 %shard_map.72.refs_2_ = bf16[3,1024,512]{2,1,0:T(8,128)(2,1)S(1)} custom-call(s32[1]{0:T(128)} %bitcast.place_ref.refs_0_, bf16[1024,16384]{1,0:T(8,128)(2,1)} %refs_1_.5), custom_call_target="tpu_custom_call" | custom-call | tf_op jit(solution)/shard_map/pallas_call | solution.py:147
  35.1 2.3 %shard_map.73 = (f32[64,3072]{1,0:T(8,128)S(1)}, bf16[64,3072]{1,0:T(8,128)(2,1)S(1)}) custom-call(bf16[128,1024]{1,0:T(8,128)(2,1)S(1)} %get-tuple-element.86.refs_0_, bf16[1024,16384]{1,0:T(8,128)(2,1)} %refs_1_.5, bf16[3,1024,512]{2,1,0:T(8,128)(2,1)S(1)} %shard_map.72.refs_2_), custom_call_target="tpu_custom_call" | custom-call | tf_op jit(solution)/shard_map/pallas_call | solution.py:170
  37.5 3.6 %collective-permute-done.9 = bf16[32,5120]{1,0:T(8,128)(2,1)S(1)} collective-permute-done((bf16[32,5120]{1,0:T(8,128)(2,1)S(1)}, bf16[32,5120]{1,0:T(8,128)(2,1)S(1)}, u32[]{:S(2)}, u32[]{:S(2)}) %collective-permute-start.9) | collective-permute-done | bytes 327712 | tf_op jit(solution)/shard_map/ppermute | solution.py:233
  42.9 1.5 %collective-permute-start.10 = (bf16[32,3072]{1,0:T(8,128)(2,1)S(1)}, bf16[32,3072]{1,0:T(8,128)(2,1)S(1)}, u32[]{:S(2)}, u32[]{:S(2)}) collective-permute-start(bf16[32,3072]{1,0:T(8,128)(2,1)S(1)} %slice.203), channel_id=1, source_target_pairs={{0,2},{1,3},{2,0},{3,1},{4,6},{5,7},{6,4},{7,5},{8,10},{9,11},{10,... | collective-permute-start | bytes 589832 | tf_op jit(solution)/shard_map/ppermute | solution.py:233
  44.4 2.6 %collective-permute-start.16 = (bf16[8,4096]{1,0:T(8,128)(2,1)S(1)}, bf16[8,4096]{1,0:T(8,128)(2,1)S(1)}, u32[]{:S(2)}, u32[]{:S(2)}) collective-permute-start(bf16[8,4096]{1,0:T(8,128)(2,1)S(1)} %slice.210), channel_id=1, source_target_pairs={{0,8},{1,9},{2,10},{3,11},{4,12},{5,13},{6,14},{7,15},{8,0},{9,1},... | collective-permute-start | bytes 196616 | tf_op jit(solution)/shard_map/ppermute | solution.py:233
  47.4 2.7 %collective-permute-start.15 = (bf16[8,5120]{1,0:T(8,128)(2,1)S(1)}, bf16[8,5120]{1,0:T(8,128)(2,1)S(1)}, u32[]{:S(2)}, u32[]{:S(2)}) collective-permute-start(bf16[8,5120]{1,0:T(8,128)(2,1)S(1)} %slice.208), channel_id=1, source_target_pairs={{0,8},{1,9},{2,10},{3,11},{4,12},{5,13},{6,14},{7,15},{8,0},{9,1},... | collective-permute-start | bytes 245768 | tf_op jit(solution)/shard_map/ppermute | solution.py:233
  50.7 1.5 %collective-permute-start.14 = (bf16[16,3072]{1,0:T(8,128)(2,1)S(1)}, bf16[16,3072]{1,0:T(8,128)(2,1)S(1)}, u32[]{:S(2)}, u32[]{:S(2)}) collective-permute-start(bf16[16,3072]{1,0:T(8,128)(2,1)S(1)} %slice.207), channel_id=1, source_target_pairs={{0,4},{1,5},{2,6},{3,7},{4,0},{5,1},{6,2},{7,3},{8,12},{9,13},{10,... | collective-permute-start | bytes 294920 | tf_op jit(solution)/shard_map/ppermute | solution.py:233
  52.3 2.8 %collective-permute-start.19 = (bf16[8,4096]{1,0:T(8,128)(2,1)S(1)}, bf16[8,4096]{1,0:T(8,128)(2,1)S(1)}, u32[]{:S(2)}, u32[]{:S(2)}) collective-permute-start(bf16[8,4096]{1,0:T(8,128)(2,1)S(1)} %slice.209), channel_id=1, source_target_pairs={{0,8},{1,9},{2,10},{3,11},{4,12},{5,13},{6,14},{7,15},{8,0},{9,1},... | collective-permute-start | bytes 196616 | tf_op jit(solution)/shard_map/ppermute | solution.py:233
  55.5 3.1 %collective-permute-start.18 = (bf16[8,3072]{1,0:T(8,128)(2,1)S(1)}, bf16[8,3072]{1,0:T(8,128)(2,1)S(1)}, u32[]{:S(2)}, u32[]{:S(2)}) collective-permute-start(bf16[8,3072]{1,0:T(8,128)(2,1)S(1)} %slice.211), channel_id=1, source_target_pairs={{0,8},{1,9},{2,10},{3,11},{4,12},{5,13},{6,14},{7,15},{8,0},{9,1},... | collective-permute-start | bytes 147464 | tf_op jit(solution)/shard_map/ppermute | solution.py:233
  59.2 1.0 %shard_map.74.refs_2_ = bf16[8,16384]{1,0:T(8,128)(2,1)} custom-call(s32[8,16384]{1,0:T(8,128)S(1)} %copy-done, s32[8,128]{1,0:T(8,128)S(1)} %copy-done.2, f32[8,4096]{1,0:T(8,128)S(1)} %slice.178.refs_0_, bf16[8,4096]{1,0:T(8,128)(2,1)S(1)} %collective-permute-done.16.refs_1_, f32[8,5120]{1,0:T(8,128)S(1)} %slice.177.refs_2_, ...), custom_call_target="tpu_custom_call" | custom-call | tf_op jit(solution)/shard_map/pallas_call | solution.py:220
  60.7 0.9 %shard_map.75 = bf16[8,16384]{1,0:T(8,128)(2,1)} custom-call(s32[8,16384]{1,0:T(8,128)S(1)} %copy-done, s32[8,128]{1,0:T(8,128)S(1)} %copy-done.2, f32[8,3072]{1,0:T(8,128)S(1)} %slice.181.refs_0_, bf16[8,3072]{1,0:T(8,128)(2,1)S(1)} %collective-permute-done.18.refs_1_, bf16[8,16384]{1,0:T(8,128)(2,1)} %shard_map.74.refs_2_), custom_call_target="tpu_custom_call", output_to_operand_aliasing={{}: (4, {})} | custom-call | tf_op jit(solution)/shard_map/pallas_call | solution.py:220
  (87 shorter events, 8.0 us)
Async XLA Ops:
  0.8 5.3 %collective-permute-start = (bf16[4,1,8,256]{3,2,1,0:T(8,128)(2,1)S(1)}, bf16[4,1,8,256]{3,2,1,0:T(8,128)(2,1)S(1)}, u32[]{:S(2)}, u32[]{:S(2)}) collective-permute-start(bf16[4,1,8,256]{3,2,1,0:T(8,128)(2,1)S(1)} %get-tuple-element.117), channel_id=1, source_target_pairs={{0,2},{1,3},{2,0},{3,1},{4,6},{5,7},{6,4},{7,5},{8,10},{9,11},{10,... | collective-permute-start | bytes 49160 | tf_op jit(solution)/shard_map/ppermute | solution.py:233
  6.1 8.6 %copy-start.1 = (bf16[128,1024]{1,0:T(8,128)(2,1)S(1)}, bf16[128,1024]{1,0:T(8,128)(2,1)}, u32[]{:S(2)}) copy-start(bf16[128,1024]{1,0:T(8,128)(2,1)} %q_ref.1) | copy-start | bytes 786436
  6.1 3.9 %collective-permute-start.1 = (bf16[2,2,8,256]{3,2,1,0:T(8,128)(2,1)S(1)}, bf16[2,2,8,256]{3,2,1,0:T(8,128)(2,1)S(1)}, u32[]{:S(2)}, u32[]{:S(2)}) collective-permute-start(bf16[2,2,8,256]{3,2,1,0:T(8,128)(2,1)S(1)} %get-tuple-element.115), channel_id=1, source_target_pairs={{0,4},{1,5},{2,6},{3,7},{4,0},{5,1},{6,2},{7,3},{8,12},{9,13},{10,... | collective-permute-start | bytes 49160 | tf_op jit(solution)/shard_map/ppermute | solution.py:233
  10.0 4.7 %collective-permute-start.2 = (bf16[1,4,8,256]{3,2,1,0:T(8,128)(2,1)S(1)}, bf16[1,4,8,256]{3,2,1,0:T(8,128)(2,1)S(1)}, u32[]{:S(2)}, u32[]{:S(2)}) collective-permute-start(bf16[1,4,8,256]{3,2,1,0:T(8,128)(2,1)S(1)} %get-tuple-element.114), channel_id=1, source_target_pairs={{0,8},{1,9},{2,10},{3,11},{4,12},{5,13},{6,14},{7,15},{8,0},{9,1},... | collective-permute-start | bytes 49160 | tf_op jit(solution)/shard_map/ppermute | solution.py:233
  14.7 1.2 %collective-permute-start.3 = (bf16[8,8,256]{2,1,0:T(8,128)(2,1)S(1)}, bf16[8,8,256]{2,1,0:T(8,128)(2,1)S(1)}, u32[]{:S(2)}, u32[]{:S(2)}) collective-permute-start(bf16[8,8,256]{2,1,0:T(8,128)(2,1)S(1)} %maximum_bitcast_fusion.2), channel_id=1, source_target_pairs={{0,1},{1,0},{2,3},{3,2},{4,5},{5,4},{6,7},{7,6},{8,9},{9,8},{10,11... | collective-permute-start | bytes 98312 | tf_op jit(solution)/shard_map/ppermute | solution.py:233
  17.8 2.1 %collective-permute-start.4 = (bf16[64,4096]{1,0:T(8,128)(2,1)S(1)}, bf16[64,4096]{1,0:T(8,128)(2,1)S(1)}, u32[]{:S(2)}, u32[]{:S(2)}) collective-permute-start(bf16[64,4096]{1,0:T(8,128)(2,1)S(1)} %get-tuple-element.69), channel_id=1, source_target_pairs={{0,1},{1,0},{2,3},{3,2},{4,5},{5,4},{6,7},{7,6},{8,9},{9,8},{10,11... | collective-permute-start | bytes 1572872 | tf_op jit(solution)/shard_map/ppermute | solution.py:233
  20.1 9.7 %collective-permute-start.7 = (bf16[32,4096]{1,0:T(8,128)(2,1)S(1)}, bf16[32,4096]{1,0:T(8,128)(2,1)S(1)}, u32[]{:S(2)}, u32[]{:S(2)}) collective-permute-start(bf16[32,4096]{1,0:T(8,128)(2,1)S(1)} %slice.202), channel_id=1, source_target_pairs={{0,2},{1,3},{2,0},{3,1},{4,6},{5,7},{6,4},{7,5},{8,10},{9,11},{10,... | collective-permute-start | bytes 786440 | tf_op jit(solution)/shard_map/ppermute | solution.py:233
  25.2 6.2 %collective-permute-start.6 = (bf16[64,5120]{1,0:T(8,128)(2,1)S(1)}, bf16[64,5120]{1,0:T(8,128)(2,1)S(1)}, u32[]{:S(2)}, u32[]{:S(2)}) collective-permute-start(bf16[64,5120]{1,0:T(8,128)(2,1)S(1)} %get-tuple-element.74), channel_id=1, source_target_pairs={{0,1},{1,0},{2,3},{3,2},{4,5},{5,4},{6,7},{7,6},{8,9},{9,8},{10,11... | collective-permute-start | bytes 1966088 | tf_op jit(solution)/shard_map/ppermute | solution.py:233
  29.3 2.9 %collective-permute-start.5 = (bf16[64,4096]{1,0:T(8,128)(2,1)S(1)}, bf16[64,4096]{1,0:T(8,128)(2,1)S(1)}, u32[]{:S(2)}, u32[]{:S(2)}) collective-permute-start(bf16[64,4096]{1,0:T(8,128)(2,1)S(1)} %get-tuple-element.77), channel_id=1, source_target_pairs={{0,1},{1,0},{2,3},{3,2},{4,5},{5,4},{6,7},{7,6},{8,9},{9,8},{10,11... | collective-permute-start | bytes 1572872 | tf_op jit(solution)/shard_map/ppermute | solution.py:233
  29.9 12.2 %collective-permute-start.12 = (bf16[16,4096]{1,0:T(8,128)(2,1)S(1)}, bf16[16,4096]{1,0:T(8,128)(2,1)S(1)}, u32[]{:S(2)}, u32[]{:S(2)}) collective-permute-start(bf16[16,4096]{1,0:T(8,128)(2,1)S(1)} %slice.206), channel_id=1, source_target_pairs={{0,4},{1,5},{2,6},{3,7},{4,0},{5,1},{6,2},{7,3},{8,12},{9,13},{10,... | collective-permute-start | bytes 393224 | tf_op jit(solution)/shard_map/ppermute | solution.py:233
  31.6 9.5 %collective-permute-start.9 = (bf16[32,5120]{1,0:T(8,128)(2,1)S(1)}, bf16[32,5120]{1,0:T(8,128)(2,1)S(1)}, u32[]{:S(2)}, u32[]{:S(2)}) collective-permute-start(bf16[32,5120]{1,0:T(8,128)(2,1)S(1)} %slice.201), channel_id=1, source_target_pairs={{0,2},{1,3},{2,0},{3,1},{4,6},{5,7},{6,4},{7,5},{8,10},{9,11},{10,... | collective-permute-start | bytes 983048 | tf_op jit(solution)/shard_map/ppermute | solution.py:233
  32.7 9.3 %collective-permute-start.13 = (bf16[32,4096]{1,0:T(8,128)(2,1)S(1)}, bf16[32,4096]{1,0:T(8,128)(2,1)S(1)}, u32[]{:S(2)}, u32[]{:S(2)}) collective-permute-start(bf16[32,4096]{1,0:T(8,128)(2,1)S(1)} %bitcast.36), channel_id=1, source_target_pairs={{0,4},{1,5},{2,6},{3,7},{4,0},{5,1},{6,2},{7,3},{8,12},{9,13},{10,... | collective-permute-start | bytes 786440 | tf_op jit(solution)/shard_map/ppermute | solution.py:233
  35.1 6.0 %slice-start = ((f32[64,5120]{1,0:T(8,128)}), f32[32,5120]{1,0:T(8,128)S(1)}, s32[]{:S(2)}) async-start(f32[64,5120]{1,0:T(8,128)} %copy-done.3), calls=%async_computation | async-start | bytes 1310720 | tf_op jit(solution)/shard_map/slice | solution.py:320
  37.4 4.5 %collective-permute-start.8 = (bf16[64,3072]{1,0:T(8,128)(2,1)S(1)}, bf16[64,3072]{1,0:T(8,128)(2,1)S(1)}, u32[]{:S(2)}, u32[]{:S(2)}) collective-permute-start(bf16[64,3072]{1,0:T(8,128)(2,1)S(1)} %get-tuple-element.88), channel_id=1, source_target_pairs={{0,1},{1,0},{2,3},{3,2},{4,5},{5,4},{6,7},{7,6},{8,9},{9,8},{10,11... | collective-permute-start | bytes 1179656 | tf_op jit(solution)/shard_map/ppermute | solution.py:233
  41.3 6.1 %collective-permute-start.11 = (bf16[16,5120]{1,0:T(8,128)(2,1)S(1)}, bf16[16,5120]{1,0:T(8,128)(2,1)S(1)}, u32[]{:S(2)}, u32[]{:S(2)}) collective-permute-start(bf16[16,5120]{1,0:T(8,128)(2,1)S(1)} %slice.204), channel_id=1, source_target_pairs={{0,4},{1,5},{2,6},{3,7},{4,0},{5,1},{6,2},{7,3},{8,12},{9,13},{10,... | collective-permute-start | bytes 491528 | tf_op jit(solution)/shard_map/ppermute | solution.py:233
  42.1 17.1 %copy-start = (s32[8,16384]{1,0:T(8,128)S(1)}, s32[8,16384]{1,0:T(8,128)}, u32[]{:S(2)}) copy-start(s32[8,16384]{1,0:T(8,128)} %codes_ref.3) | copy-start | bytes 1572868
  42.2 17.1 %copy-start.2 = (s32[8,128]{1,0:T(8,128)S(1)}, s32[8,128]{1,0:T(8,128)}, u32[]{:S(2)}) copy-start(s32[8,128]{1,0:T(8,128)} %exponents_ref.3) | copy-start | bytes 12292
  42.3 10.0 %collective-permute-start.17 = (bf16[16,4096]{1,0:T(8,128)(2,1)S(1)}, bf16[16,4096]{1,0:T(8,128)(2,1)S(1)}, u32[]{:S(2)}, u32[]{:S(2)}) collective-permute-start(bf16[16,4096]{1,0:T(8,128)(2,1)S(1)} %slice.205), channel_id=1, source_target_pairs={{0,2},{1,3},{2,0},{3,1},{4,6},{5,7},{6,4},{7,5},{8,10},{9,11},{10,... | collective-permute-start | bytes 393224 | tf_op jit(solution)/shard_map/ppermute | solution.py:233
  42.9 7.7 %collective-permute-start.10 = (bf16[32,3072]{1,0:T(8,128)(2,1)S(1)}, bf16[32,3072]{1,0:T(8,128)(2,1)S(1)}, u32[]{:S(2)}, u32[]{:S(2)}) collective-permute-start(bf16[32,3072]{1,0:T(8,128)(2,1)S(1)} %slice.203), channel_id=1, source_target_pairs={{0,2},{1,3},{2,0},{3,1},{4,6},{5,7},{6,4},{7,5},{8,10},{9,11},{10,... | collective-permute-start | bytes 589832 | tf_op jit(solution)/shard_map/ppermute | solution.py:233
  44.4 10.8 %collective-permute-start.16 = (bf16[8,4096]{1,0:T(8,128)(2,1)S(1)}, bf16[8,4096]{1,0:T(8,128)(2,1)S(1)}, u32[]{:S(2)}, u32[]{:S(2)}) collective-permute-start(bf16[8,4096]{1,0:T(8,128)(2,1)S(1)} %slice.210), channel_id=1, source_target_pairs={{0,8},{1,9},{2,10},{3,11},{4,12},{5,13},{6,14},{7,15},{8,0},{9,1},... | collective-permute-start | bytes 196616 | tf_op jit(solution)/shard_map/ppermute | solution.py:233
  47.4 7.7 %collective-permute-start.15 = (bf16[8,5120]{1,0:T(8,128)(2,1)S(1)}, bf16[8,5120]{1,0:T(8,128)(2,1)S(1)}, u32[]{:S(2)}, u32[]{:S(2)}) collective-permute-start(bf16[8,5120]{1,0:T(8,128)(2,1)S(1)} %slice.208), channel_id=1, source_target_pairs={{0,8},{1,9},{2,10},{3,11},{4,12},{5,13},{6,14},{7,15},{8,0},{9,1},... | collective-permute-start | bytes 245768 | tf_op jit(solution)/shard_map/ppermute | solution.py:233
  50.7 4.8 %collective-permute-start.14 = (bf16[16,3072]{1,0:T(8,128)(2,1)S(1)}, bf16[16,3072]{1,0:T(8,128)(2,1)S(1)}, u32[]{:S(2)}, u32[]{:S(2)}) collective-permute-start(bf16[16,3072]{1,0:T(8,128)(2,1)S(1)} %slice.207), channel_id=1, source_target_pairs={{0,4},{1,5},{2,6},{3,7},{4,0},{5,1},{6,2},{7,3},{8,12},{9,13},{10,... | collective-permute-start | bytes 294920 | tf_op jit(solution)/shard_map/ppermute | solution.py:233
  52.3 6.9 %collective-permute-start.19 = (bf16[8,4096]{1,0:T(8,128)(2,1)S(1)}, bf16[8,4096]{1,0:T(8,128)(2,1)S(1)}, u32[]{:S(2)}, u32[]{:S(2)}) collective-permute-start(bf16[8,4096]{1,0:T(8,128)(2,1)S(1)} %slice.209), channel_id=1, source_target_pairs={{0,8},{1,9},{2,10},{3,11},{4,12},{5,13},{6,14},{7,15},{8,0},{9,1},... | collective-permute-start | bytes 196616 | tf_op jit(solution)/shard_map/ppermute | solution.py:233
  55.5 5.1 %collective-permute-start.18 = (bf16[8,3072]{1,0:T(8,128)(2,1)S(1)}, bf16[8,3072]{1,0:T(8,128)(2,1)S(1)}, u32[]{:S(2)}, u32[]{:S(2)}) collective-permute-start(bf16[8,3072]{1,0:T(8,128)(2,1)S(1)} %slice.211), channel_id=1, source_target_pairs={{0,8},{1,9},{2,10},{3,11},{4,12},{5,13},{6,14},{7,15},{8,0},{9,1},... | collective-permute-start | bytes 147464 | tf_op jit(solution)/shard_map/ppermute | solution.py:233
  (5 other events, 18.0 us)

commit v4 on v3

--- a/solution.py
+++ b/solution.py
@@ -15,11 +15,11 @@
 masked_score = -1e30
 
 LIMIT = 12 << 20
-PARTS = ((4, 'yz', 8), (5, 'yz', 3), (4, 'zyz', 0), (3, 'yz', 3))
-AHEAD = (4, 4)
+PARTS = ((4, 'yz', 8), (4, 'yz', 3), (5, 'zyz', 0), (3, 'yz', 3))
+AHEAD = (4, 3, 1)
 TILE = 512
 SPLIT = {}
-EVENTS = ((0, 0), (1, -1), (0, 1), (1, 0), (2, 0), (0, 2), (1, 1), (2, 1), (3, -1), (3, 0), (1, 2), (3, 1), (2, 2), (0, 3), (1, 3), (3, 2), (2, 3), (0, 4), (1, 4), (3, 3), (2, 4), (3, 4))
+EVENTS = ((0, 0), (1, -1), (0, 1), (1, 0), (2, 0), (0, 2), (1, 1), (2, 1), (3, -1), (3, 0), (1, 2), (0, 3), (3, 1), (2, 2), (1, 3), (3, 2), (2, 3), (0, 4), (1, 4), (3, 3), (2, 4), (3, 4))
 
 
 def events(bits):
@@ -177,9 +177,7 @@
     )(*inputs, *ahead)
 
 
-def finish_kernel(bounds, codes_ref, exponents_ref, *refs):
-    pieces = refs[:2 * len(bounds)]
-    out_ref, *done_refs, stored = refs[len(refs) - len(bounds) - 2:]
+def finish_kernel(bounds, is_last, codes_ref, exponents_ref, *refs):
     i = lax.broadcasted_iota(jnp.int32, (HBLK, HBLK), 0)
     common = i & lax.broadcasted_iota(jnp.int32, (HBLK, HBLK), 1)
     parity = jnp.zeros((HBLK, HBLK), jnp.int32)
@@ -187,9 +185,15 @@
         parity = parity ^ (common >> bit)
     table = (1 - 2 * (parity & 1)).astype(jnp.bfloat16)
     scale = jnp.exp2(exponents_ref[...].astype(jnp.float32))
-    stores = []
-    for index, (start, keep_ref, got_ref, done_ref) in enumerate(zip(bounds, pieces[::2], pieces[1::2], done_refs)):
-        rows, width = done_ref.shape
+    if is_last:
+        keep_ref, got_ref, *done_refs, out_ref = refs
+        for start, done_ref in zip(bounds[1:], done_refs):
+            out_ref[:, start:start + done_ref.shape[1]] = done_ref[...]
+        jobs = [(bounds[0], keep_ref, got_ref, out_ref, bounds[0])]
+    else:
+        jobs = [(start, *refs[2 * n:2 * n + 2], refs[2 * len(bounds) + n], 0) for n, start in enumerate(bounds)]
+    for start, keep_ref, got_ref, done_ref, at in jobs:
+        rows, width = keep_ref.shape
         summed = keep_ref[...] + got_ref[...].astype(jnp.float32)
         blocks = width // HBLK
         rest = jnp.concatenate([summed[:, b * HBLK:(b + 1) * HBLK] for b in range(blocks)], axis=0)
@@ -202,29 +206,21 @@
         for b in range(blocks):
             block = start // HBLK + b
             codes = codes_ref[:, block * HBLK:(block + 1) * HBLK].astype(jnp.float32)
-            done_ref[:, b * HBLK:(b + 1) * HBLK] = (
+            done_ref[:, at + b * HBLK:at + (b + 1) * HBLK] = (
                 codes * scale[:, block:block + 1] + rotated[b * rows:(b + 1) * rows]
             ).astype(jnp.bfloat16)
-        store = pltpu.make_async_copy(done_ref, out_ref.at[:, pl.ds(start, width)], stored.at[index])
-        store.start()
-        stores.append(store)
-    for store in stores:
-        store.wait()
-
-
-def finish(codes, exponents, pieces, bounds, out):
-    inputs, in_specs, aliases = [codes, exponents, *pieces], [VMEM] * (2 + len(pieces)), {}
-    if out is not None:
-        aliases = {len(inputs): 0}
-        inputs, in_specs = [*inputs, out], [*in_specs, ANYWHERE]
+
+
+def finish(codes, exponents, pieces, bounds, done=None):
+    is_last = done is not None
+    rows, width = codes.shape
+    shapes = [(rows, width)] if is_last else [keep.shape for keep in pieces[::2]]
+    inputs = [codes, exponents, *pieces, *(done or [])]
     return pl.pallas_call(
-        functools.partial(finish_kernel, bounds),
-        in_specs=in_specs,
-        out_specs=ANYWHERE,
-        out_shape=jax.ShapeDtypeStruct(codes.shape, jnp.bfloat16),
-        input_output_aliases=aliases,
-        scratch_shapes=[pltpu.VMEM(keep.shape, jnp.bfloat16) for keep in pieces[::2]]
-        + [pltpu.SemaphoreType.DMA((len(bounds),))],
+        functools.partial(finish_kernel, bounds, is_last),
+        in_specs=[VMEM] * len(inputs),
+        out_specs=[VMEM] * len(shapes),
+        out_shape=[jax.ShapeDtypeStruct(shape, jnp.bfloat16) for shape in shapes],
         compiler_params=pltpu.CompilerParams(vmem_limit_bytes=LIMIT),
     )(*inputs)
 
@@ -233,21 +229,14 @@
     return lax.ppermute(value, axis, [(source, source ^ mask) for source in range(lax.axis_size(axis))])
 
 
-def pack_kernel(local_heads, place_ref, key_ref, value_ref, packed_ref, held, arrived):
-    copies = [
-        pltpu.make_async_copy(ref, held.at[index], arrived.at[index]) for index, ref in enumerate((key_ref, value_ref))
-    ]
-    for copy in copies:
-        copy.start()
-    for copy in copies:
-        copy.wait()
+def pack_kernel(local_heads, place_ref, rows_ref, packed_ref):
     query_group = QUERY_HEADS // KEY_VALUE_HEADS
     chip = place_ref[0] // 2
     for away in range(packed_ref.shape[0]):
         head = (chip ^ away) * 2 * local_heads // query_group
         columns = pl.ds(pl.multiple_of(head * HEAD_SIZE, HEAD_SIZE), HEAD_SIZE)
         for index in range(2):
-            packed_ref[away, :, index * HEAD_SIZE:(index + 1) * HEAD_SIZE] = held[index, :, columns]
+            packed_ref[away, :, index * HEAD_SIZE:(index + 1) * HEAD_SIZE] = rows_ref[index, :, columns]
 
 
 def shared_out(place, key_rows, value_rows, weight, bits, local_heads):
@@ -256,11 +245,10 @@
     packed = pl.pallas_call(
         functools.partial(pack_kernel, local_heads),
         out_shape=jax.ShapeDtypeStruct((chips, rows, 2 * HEAD_SIZE), key_rows.dtype),
-        in_specs=[SMEM, ANYWHERE, ANYWHERE],
+        in_specs=[SMEM, VMEM],
         out_specs=VMEM,
-        scratch_shapes=[pltpu.VMEM((2, *key_rows.shape), key_rows.dtype), pltpu.SemaphoreType.DMA((2,))],
-        compiler_params=pltpu.CompilerParams(vmem_limit_bytes=LIMIT),
-    )(place, *(pltpu.with_memory_space_constraint(x, pltpu.HBM) for x in (key_rows, value_rows)))
+        compiler_params=pltpu.CompilerParams(vmem_limit_bytes=LIMIT),
+    )(place, jnp.stack([key_rows, value_rows]))
     held = packed[:, None]
     ahead = []
     fetched = 0
@@ -355,12 +343,12 @@
         state[part] = left, keep, tuple(passed_across(piece, "tensor", mask) for piece in token)
     spare = max(8 - rows, 0)
     codes, scales = (jnp.pad(x, ((0, spare), (0, 0))) for x in (quant_codes, exponents))
-    *early, last = state
-    out = None
-    for group in (early, [last]):
-        if group:
-            pieces = [jnp.pad(x, ((0, spare), (0, 0))) for part in group for x in state[part][1:]]
-            out = finish(codes, scales, pieces, [starts[part] for part in group], out)
+    *early, last = [
+        (starts[part], *(jnp.pad(x, ((0, spare), (0, 0))) for x in state[part][1:])) for part in state
+    ]
+    bounds = [start for start, _, _ in early]
+    done = finish(codes, scales, [x for _, *pair in early for x in pair], bounds) if early else []
+    (out,) = finish(codes, scales, last[1:], [last[0], *bounds], done)
     return out[:rows]
 
 

time: 61.8 us -> 61.2 us (level)
  starting transfers between devices: 27.9 us -> 24.5 us
  waiting for transfers between devices: 8.81 us -> 11.5 us
  other arithmetic: 0.82 us -> 1.57 us
    ppermute x20, starting transfers between devices: 27.9 us -> 24.5 us  [passed_across(): lax.ppermute(value, axis, [(source, source ^ mask) for source in range(la...]
    ppermute x20, waiting for transfers between devices: 8.81 us -> 11.5 us  [passed_across(): lax.ppermute(value, axis, [(source, source ^ mask) for source in range(la...]
    pallas_call x4 -> x5, Pallas kernels: 8.25 us -> 9.15 us  [fetch(): pl.pallas_call(functools.partial(fetch_kernel, start), in_specs=[SMEM, AN...]
    another operation x0 -> x1, other arithmetic: none -> 0.74 us  [shared_out(): jnp.stack([key_rows, value_rows])]
    pallas_call x1, Pallas kernels: 0.77 us -> 0.03 us  [shared_out(): pl.pallas_call(functools.partial(pack_kernel, local_heads), out_shape=jax...]
    pallas_call x2, Pallas kernels: 1.9 us -> 1.28 us  [finish(): pl.pallas_call(functools.partial(finish_kernel, bounds, is_last), in_spec...]
  transfers between devices with their start and end apart: 20 -> 20, of which waited for: 8 -> 10; matrix products, arithmetic and copies ran while one was open for 2% -> 2% of each run, Pallas kernels for 32% -> 32%
where the time goes in v4:
time: 61.2 us; the launch traced here: 60.9 us
  starting transfers between devices  24.5 us (40%)
  Pallas kernels  22.4 us (37%)
  waiting for transfers between devices  11.5 us (19%)
  other arithmetic  1.57 us (3%)
    ppermute x20, starting transfers between devices, passed_across(): lax.ppermute(value, axis, [(source, source ^ mask) for source in range(la...  24.5 us
    pallas_call x4, Pallas kernels, project_part(): pl.pallas_call(functools.partial(part_kernel, bits, start, with_attention...  11.6 us
    ppermute x20, waiting for transfers between devices, passed_across(): lax.ppermute(value, axis, [(source, source ^ mask) for source in range(la...  11.5 us
    pallas_call x5, Pallas kernels, fetch(): pl.pallas_call(functools.partial(fetch_kernel, start), in_specs=[SMEM, AN...  9.15 us
    pallas_call x2, Pallas kernels, finish(): pl.pallas_call(functools.partial(finish_kernel, bounds, is_last), in_spec...  1.28 us
  transfers between devices with their start and end apart: 20, of which 10 were waited for; matrix products, arithmetic and copies ran while one was open for 2% of the time, Pallas kernels for 32%

profile of v4, /device:TPU:0, one launch (start us, length us, event | category | flops | bytes accessed | tf_op | source)
XLA Modules:
  0.0 60.9 jit_solution(997595474156559182)
XLA Ops:
  0.8 3.0 %collective-permute-start = (bf16[4,1,8,256]{3,2,1,0:T(8,128)(2,1)S(1)}, bf16[4,1,8,256]{3,2,1,0:T(8,128)(2,1)S(1)}, u32[]{:S(2)}, u32[]{:S(2)}) collective-permute-start(bf16[4,1,8,256]{3,2,1,0:T(8,128)(2,1)S(1)} %get-tuple-element.131), channel_id=1, source_target_pairs={{0,2},{1,3},{2,0},{3,1},{4,6},{5,7},{6,4},{7,5},{8,10},{9,11},{10,... | collective-permute-start | bytes 49160 | tf_op jit(solution)/shard_map/ppermute | solution.py:229
  3.8 2.2 %shard_map.66.refs_4_ = bf16[4,1024,512]{2,1,0:T(8,128)(2,1)S(1)} custom-call(s32[1]{0:T(128)} %bitcast.place_ref.refs_0_, bf16[1024,16384]{1,0:T(8,128)(2,1)} %refs_1_.5), custom_call_target="tpu_custom_call" | custom-call | tf_op jit(solution)/shard_map/pallas_call | solution.py:147
  6.1 1.6 %collective-permute-start.1 = (bf16[2,2,8,256]{3,2,1,0:T(8,128)(2,1)S(1)}, bf16[2,2,8,256]{3,2,1,0:T(8,128)(2,1)S(1)}, u32[]{:S(2)}, u32[]{:S(2)}) collective-permute-start(bf16[2,2,8,256]{3,2,1,0:T(8,128)(2,1)S(1)} %get-tuple-element.129), channel_id=1, source_target_pairs={{0,4},{1,5},{2,6},{3,7},{4,0},{5,1},{6,2},{7,3},{8,12},{9,13},{10,... | collective-permute-start | bytes 49160 | tf_op jit(solution)/shard_map/ppermute | solution.py:229
  7.7 1.9 %shard_map.67.refs_5_ = bf16[3,1024,512]{2,1,0:T(8,128)(2,1)S(1)} custom-call(s32[1]{0:T(128)} %bitcast.place_ref.refs_0_, bf16[1024,16384]{1,0:T(8,128)(2,1)} %refs_1_.5), custom_call_target="tpu_custom_call" | custom-call | tf_op jit(solution)/shard_map/pallas_call | solution.py:147
  9.9 2.7 %collective-permute-start.2 = (bf16[1,4,8,256]{3,2,1,0:T(8,128)(2,1)S(1)}, bf16[1,4,8,256]{3,2,1,0:T(8,128)(2,1)S(1)}, u32[]{:S(2)}, u32[]{:S(2)}) collective-permute-start(bf16[1,4,8,256]{3,2,1,0:T(8,128)(2,1)S(1)} %get-tuple-element.127), channel_id=1, source_target_pairs={{0,8},{1,9},{2,10},{3,11},{4,12},{5,13},{6,14},{7,15},{8,0},{9,1},... | collective-permute-start | bytes 49160 | tf_op jit(solution)/shard_map/ppermute | solution.py:229
  12.6 1.2 %shard_map.68.refs_6_ = bf16[1,1024,512]{2,1,0:T(8,128)(2,1)S(1)} custom-call(s32[1]{0:T(128)} %bitcast.place_ref.refs_0_, bf16[1024,16384]{1,0:T(8,128)(2,1)} %refs_1_.5), custom_call_target="tpu_custom_call" | custom-call | tf_op jit(solution)/shard_map/pallas_call | solution.py:147
  15.0 0.9 %collective-permute-done.3 = bf16[8,8,256]{2,1,0:T(8,128)(2,1)S(1)} collective-permute-done((bf16[8,8,256]{2,1,0:T(8,128)(2,1)S(1)}, bf16[8,8,256]{2,1,0:T(8,128)(2,1)S(1)}, u32[]{:S(2)}, u32[]{:S(2)}) %collective-permute-start.3) | collective-permute-done | bytes 32800 | tf_op jit(solution)/shard_map/ppermute | solution.py:229
  15.9 1.8 %shard_map.69 = (bf16[128,1024]{1,0:T(8,128)(2,1)S(1)}, f32[64,4096]{1,0:T(8,128)S(1)}, bf16[64,4096]{1,0:T(8,128)(2,1)S(1)}) custom-call(s32[1]{0:T(128)} %bitcast.place_ref.refs_0_, bf16[128,1024]{1,0:T(8,128)(2,1)S(1)} %shard_map.64.refs_1_, bf16[128,256]{1,0:T(8,128)(2,1)S(1)} %maximum_bitcast_fusion.refs_2_, bf16[1024,16384]{1,0:T(8,128)(2,1)} %refs_1_.5, ...), custom_call_target="tpu_custom_call" | custom-call | tf_op jit(solution)/shard_map/pallas_call | solution.py:170
  17.9 1.9 %shard_map.70.refs_2_ = bf16[3,1024,512]{2,1,0:T(8,128)(2,1)S(1)} custom-call(s32[1]{0:T(128)} %bitcast.place_ref.refs_0_, bf16[1024,16384]{1,0:T(8,128)(2,1)} %refs_1_.5), custom_call_target="tpu_custom_call" | custom-call | tf_op jit(solution)/shard_map/pallas_call | solution.py:147
  20.0 1.5 %collective-permute-start.7 = (bf16[32,4096]{1,0:T(8,128)(2,1)S(1)}, bf16[32,4096]{1,0:T(8,128)(2,1)S(1)}, u32[]{:S(2)}, u32[]{:S(2)}) collective-permute-start(bf16[32,4096]{1,0:T(8,128)(2,1)S(1)} %slice.202), channel_id=1, source_target_pairs={{0,2},{1,3},{2,0},{3,1},{4,6},{5,7},{6,4},{7,5},{8,10},{9,11},{10,... | collective-permute-start | bytes 786440 | tf_op jit(solution)/shard_map/ppermute | solution.py:229
  21.5 2.9 %shard_map.71 = (f32[64,4096]{1,0:T(8,128)S(1)}, bf16[64,4096]{1,0:T(8,128)(2,1)S(1)}) custom-call(bf16[128,1024]{1,0:T(8,128)(2,1)S(1)} %get-tuple-element.97.refs_0_, bf16[1024,16384]{1,0:T(8,128)(2,1)} %refs_1_.5, bf16[3,1024,512]{2,1,0:T(8,128)(2,1)S(1)} %shard_map.70.refs_2_), custom_call_target="tpu_custom_call" | custom-call | tf_op jit(solution)/shard_map/pallas_call | solution.py:170
  24.6 4.6 %shard_map.72 = (f32[64,5120]{1,0:T(8,128)S(1)}, bf16[64,5120]{1,0:T(8,128)(2,1)S(1)}) custom-call(bf16[128,1024]{1,0:T(8,128)(2,1)S(1)} %get-tuple-element.97.refs_0_, bf16[1024,16384]{1,0:T(8,128)(2,1)} %refs_1_.5), custom_call_target="tpu_custom_call" | custom-call | tf_op jit(solution)/shard_map/pallas_call | solution.py:170
  29.8 1.6 %collective-permute-start.9 = (bf16[16,4096]{1,0:T(8,128)(2,1)S(1)}, bf16[16,4096]{1,0:T(8,128)(2,1)S(1)}, u32[]{:S(2)}, u32[]{:S(2)}) collective-permute-start(bf16[16,4096]{1,0:T(8,128)(2,1)S(1)} %slice.206), channel_id=1, source_target_pairs={{0,4},{1,5},{2,6},{3,7},{4,0},{5,1},{6,2},{7,3},{8,12},{9,13},{10,... | collective-permute-start | bytes 393224 | tf_op jit(solution)/shard_map/ppermute | solution.py:229
  33.4 1.9 %shard_map.73.refs_2_ = bf16[3,1024,512]{2,1,0:T(8,128)(2,1)S(1)} custom-call(s32[1]{0:T(128)} %bitcast.place_ref.refs_0_, bf16[1024,16384]{1,0:T(8,128)(2,1)} %refs_1_.5), custom_call_target="tpu_custom_call" | custom-call | tf_op jit(solution)/shard_map/pallas_call | solution.py:147
  35.3 2.3 %shard_map.74 = (f32[64,3072]{1,0:T(8,128)S(1)}, bf16[64,3072]{1,0:T(8,128)(2,1)S(1)}) custom-call(bf16[128,1024]{1,0:T(8,128)(2,1)S(1)} %get-tuple-element.97.refs_0_, bf16[1024,16384]{1,0:T(8,128)(2,1)} %refs_1_.5, bf16[3,1024,512]{2,1,0:T(8,128)(2,1)S(1)} %shard_map.73.refs_2_), custom_call_target="tpu_custom_call" | custom-call | tf_op jit(solution)/shard_map/pallas_call | solution.py:170
  37.8 1.9 %collective-permute-done.10 = bf16[32,4096]{1,0:T(8,128)(2,1)S(1)} collective-permute-done((bf16[32,4096]{1,0:T(8,128)(2,1)S(1)}, bf16[32,4096]{1,0:T(8,128)(2,1)S(1)}, u32[]{:S(2)}, u32[]{:S(2)}) %collective-permute-start.10) | collective-permute-done | bytes 262176 | tf_op jit(solution)/shard_map/ppermute | solution.py:229
  40.4 2.6 %collective-permute-start.16 = (bf16[8,4096]{1,0:T(8,128)(2,1)S(1)}, bf16[8,4096]{1,0:T(8,128)(2,1)S(1)}, u32[]{:S(2)}, u32[]{:S(2)}) collective-permute-start(bf16[8,4096]{1,0:T(8,128)(2,1)S(1)} %slice.210), channel_id=1, source_target_pairs={{0,8},{1,9},{2,10},{3,11},{4,12},{5,13},{6,14},{7,15},{8,0},{9,1},... | collective-permute-start | bytes 196616 | tf_op jit(solution)/shard_map/ppermute | solution.py:229
  44.0 2.5 %collective-permute-done.12 = bf16[16,4096]{1,0:T(8,128)(2,1)S(1)} collective-permute-done((bf16[16,4096]{1,0:T(8,128)(2,1)S(1)}, bf16[16,4096]{1,0:T(8,128)(2,1)S(1)}, u32[]{:S(2)}, u32[]{:S(2)}) %collective-permute-start.12) | collective-permute-done | bytes 131104 | tf_op jit(solution)/shard_map/ppermute | solution.py:229
  46.7 0.9 %collective-permute-start.17 = (bf16[16,5120]{1,0:T(8,128)(2,1)S(1)}, bf16[16,5120]{1,0:T(8,128)(2,1)S(1)}, u32[]{:S(2)}, u32[]{:S(2)}) collective-permute-start(bf16[16,5120]{1,0:T(8,128)(2,1)S(1)} %slice.204), channel_id=1, source_target_pairs={{0,2},{1,3},{2,0},{3,1},{4,6},{5,7},{6,4},{7,5},{8,10},{9,11},{10,... | collective-permute-start | bytes 491528 | tf_op jit(solution)/shard_map/ppermute | solution.py:229
  47.6 1.9 %collective-permute-start.15 = (bf16[8,4096]{1,0:T(8,128)(2,1)S(1)}, bf16[8,4096]{1,0:T(8,128)(2,1)S(1)}, u32[]{:S(2)}, u32[]{:S(2)}) collective-permute-start(bf16[8,4096]{1,0:T(8,128)(2,1)S(1)} %slice.209), channel_id=1, source_target_pairs={{0,8},{1,9},{2,10},{3,11},{4,12},{5,13},{6,14},{7,15},{8,0},{9,1},... | collective-permute-start | bytes 196616 | tf_op jit(solution)/shard_map/ppermute | solution.py:229
  49.6 2.4 %collective-permute-start.14 = (bf16[16,3072]{1,0:T(8,128)(2,1)S(1)}, bf16[16,3072]{1,0:T(8,128)(2,1)S(1)}, u32[]{:S(2)}, u32[]{:S(2)}) collective-permute-start(bf16[16,3072]{1,0:T(8,128)(2,1)S(1)} %slice.207), channel_id=1, source_target_pairs={{0,4},{1,5},{2,6},{3,7},{4,0},{5,1},{6,2},{7,3},{8,12},{9,13},{10,... | collective-permute-start | bytes 294920 | tf_op jit(solution)/shard_map/ppermute | solution.py:229
  52.5 1.7 %collective-permute-start.19 = (bf16[8,5120]{1,0:T(8,128)(2,1)S(1)}, bf16[8,5120]{1,0:T(8,128)(2,1)S(1)}, u32[]{:S(2)}, u32[]{:S(2)}) collective-permute-start(bf16[8,5120]{1,0:T(8,128)(2,1)S(1)} %slice.208), channel_id=1, source_target_pairs={{0,8},{1,9},{2,10},{3,11},{4,12},{5,13},{6,14},{7,15},{8,0},{9,1},... | collective-permute-start | bytes 245768 | tf_op jit(solution)/shard_map/ppermute | solution.py:229
  55.6 3.8 %collective-permute-done.19.refs_5_ = bf16[8,5120]{1,0:T(8,128)(2,1)S(1)} collective-permute-done((bf16[8,5120]{1,0:T(8,128)(2,1)S(1)}, bf16[8,5120]{1,0:T(8,128)(2,1)S(1)}, u32[]{:S(2)}, u32[]{:S(2)}) %collective-permute-start.19) | collective-permute-done | bytes 81952 | tf_op jit(solution)/shard_map/ppermute | solution.py:229
  60.0 0.9 %shard_map.76 = bf16[8,16384]{1,0:T(8,128)(2,1)} custom-call(s32[8,16384]{1,0:T(8,128)S(1)} %copy-done, s32[8,128]{1,0:T(8,128)S(1)} %copy-done.2, f32[8,3072]{1,0:T(8,128)S(1)} %slice.181.refs_0_, bf16[8,3072]{1,0:T(8,128)(2,1)S(1)} %collective-permute-done.18.refs_1_, bf16[8,4096]{1,0:T(8,128)(2,1)S(1)} %get-tuple-element.124.refs_2_, ...), custom_call_target="tpu_custom_call" | custom-call | tf_op jit(solution)/shard_map/pallas_call | solution.py:219
  (89 shorter events, 9.4 us)
Async XLA Ops:
  0.8 5.3 %collective-permute-start = (bf16[4,1,8,256]{3,2,1,0:T(8,128)(2,1)S(1)}, bf16[4,1,8,256]{3,2,1,0:T(8,128)(2,1)S(1)}, u32[]{:S(2)}, u32[]{:S(2)}) collective-permute-start(bf16[4,1,8,256]{3,2,1,0:T(8,128)(2,1)S(1)} %get-tuple-element.131), channel_id=1, source_target_pairs={{0,2},{1,3},{2,0},{3,1},{4,6},{5,7},{6,4},{7,5},{8,10},{9,11},{10,... | collective-permute-start | bytes 49160 | tf_op jit(solution)/shard_map/ppermute | solution.py:229
  6.1 3.8 %collective-permute-start.1 = (bf16[2,2,8,256]{3,2,1,0:T(8,128)(2,1)S(1)}, bf16[2,2,8,256]{3,2,1,0:T(8,128)(2,1)S(1)}, u32[]{:S(2)}, u32[]{:S(2)}) collective-permute-start(bf16[2,2,8,256]{3,2,1,0:T(8,128)(2,1)S(1)} %get-tuple-element.129), channel_id=1, source_target_pairs={{0,4},{1,5},{2,6},{3,7},{4,0},{5,1},{6,2},{7,3},{8,12},{9,13},{10,... | collective-permute-start | bytes 49160 | tf_op jit(solution)/shard_map/ppermute | solution.py:229
  9.9 4.7 %copy-start.1 = (bf16[128,1024]{1,0:T(8,128)(2,1)S(1)}, bf16[128,1024]{1,0:T(8,128)(2,1)}, u32[]{:S(2)}) copy-start(bf16[128,1024]{1,0:T(8,128)(2,1)} %q_ref.1) | copy-start | bytes 786436
  9.9 4.7 %collective-permute-start.2 = (bf16[1,4,8,256]{3,2,1,0:T(8,128)(2,1)S(1)}, bf16[1,4,8,256]{3,2,1,0:T(8,128)(2,1)S(1)}, u32[]{:S(2)}, u32[]{:S(2)}) collective-permute-start(bf16[1,4,8,256]{3,2,1,0:T(8,128)(2,1)S(1)} %get-tuple-element.127), channel_id=1, source_target_pairs={{0,8},{1,9},{2,10},{3,11},{4,12},{5,13},{6,14},{7,15},{8,0},{9,1},... | collective-permute-start | bytes 49160 | tf_op jit(solution)/shard_map/ppermute | solution.py:229
  14.6 1.2 %collective-permute-start.3 = (bf16[8,8,256]{2,1,0:T(8,128)(2,1)S(1)}, bf16[8,8,256]{2,1,0:T(8,128)(2,1)S(1)}, u32[]{:S(2)}, u32[]{:S(2)}) collective-permute-start(bf16[8,8,256]{2,1,0:T(8,128)(2,1)S(1)} %maximum_bitcast_fusion.2), channel_id=1, source_target_pairs={{0,1},{1,0},{2,3},{3,2},{4,5},{5,4},{6,7},{7,6},{8,9},{9,8},{10,11... | collective-permute-start | bytes 98312 | tf_op jit(solution)/shard_map/ppermute | solution.py:229
  17.7 2.1 %collective-permute-start.4 = (bf16[64,4096]{1,0:T(8,128)(2,1)S(1)}, bf16[64,4096]{1,0:T(8,128)(2,1)S(1)}, u32[]{:S(2)}, u32[]{:S(2)}) collective-permute-start(bf16[64,4096]{1,0:T(8,128)(2,1)S(1)} %get-tuple-element.80), channel_id=1, source_target_pairs={{0,1},{1,0},{2,3},{3,2},{4,5},{5,4},{6,7},{7,6},{8,9},{9,8},{10,11... | collective-permute-start | bytes 1572872 | tf_op jit(solution)/shard_map/ppermute | solution.py:229
  20.0 9.7 %collective-permute-start.7 = (bf16[32,4096]{1,0:T(8,128)(2,1)S(1)}, bf16[32,4096]{1,0:T(8,128)(2,1)S(1)}, u32[]{:S(2)}, u32[]{:S(2)}) collective-permute-start(bf16[32,4096]{1,0:T(8,128)(2,1)S(1)} %slice.202), channel_id=1, source_target_pairs={{0,2},{1,3},{2,0},{3,1},{4,6},{5,7},{6,4},{7,5},{8,10},{9,11},{10,... | collective-permute-start | bytes 786440 | tf_op jit(solution)/shard_map/ppermute | solution.py:229
  24.5 5.2 %slice-start = ((f32[64,4096]{1,0:T(8,128)}), f32[32,4096]{1,0:T(8,128)S(1)}, s32[]{:S(2)}) async-start(f32[64,4096]{1,0:T(8,128)} %copy-done.3), calls=%async_computation | async-start | bytes 1048576 | tf_op jit(solution)/shard_map/slice | solution.py:308
  24.5 6.9 %collective-permute-start.6 = (bf16[64,4096]{1,0:T(8,128)(2,1)S(1)}, bf16[64,4096]{1,0:T(8,128)(2,1)S(1)}, u32[]{:S(2)}, u32[]{:S(2)}) collective-permute-start(bf16[64,4096]{1,0:T(8,128)(2,1)S(1)} %get-tuple-element.85), channel_id=1, source_target_pairs={{0,1},{1,0},{2,3},{3,2},{4,5},{5,4},{6,7},{7,6},{8,9},{9,8},{10,11... | collective-permute-start | bytes 1572872 | tf_op jit(solution)/shard_map/ppermute | solution.py:229
  29.2 3.0 %collective-permute-start.5 = (bf16[64,5120]{1,0:T(8,128)(2,1)S(1)}, bf16[64,5120]{1,0:T(8,128)(2,1)S(1)}, u32[]{:S(2)}, u32[]{:S(2)}) collective-permute-start(bf16[64,5120]{1,0:T(8,128)(2,1)S(1)} %get-tuple-element.88), channel_id=1, source_target_pairs={{0,1},{1,0},{2,3},{3,2},{4,5},{5,4},{6,7},{7,6},{8,9},{9,8},{10,11... | collective-permute-start | bytes 1966088 | tf_op jit(solution)/shard_map/ppermute | solution.py:229
  29.8 10.0 %collective-permute-start.9 = (bf16[16,4096]{1,0:T(8,128)(2,1)S(1)}, bf16[16,4096]{1,0:T(8,128)(2,1)S(1)}, u32[]{:S(2)}, u32[]{:S(2)}) collective-permute-start(bf16[16,4096]{1,0:T(8,128)(2,1)S(1)} %slice.206), channel_id=1, source_target_pairs={{0,4},{1,5},{2,6},{3,7},{4,0},{5,1},{6,2},{7,3},{8,12},{9,13},{10,... | collective-permute-start | bytes 393224 | tf_op jit(solution)/shard_map/ppermute | solution.py:229
  31.6 8.1 %collective-permute-start.10 = (bf16[32,4096]{1,0:T(8,128)(2,1)S(1)}, bf16[32,4096]{1,0:T(8,128)(2,1)S(1)}, u32[]{:S(2)}, u32[]{:S(2)}) collective-permute-start(bf16[32,4096]{1,0:T(8,128)(2,1)S(1)} %slice.201), channel_id=1, source_target_pairs={{0,2},{1,3},{2,0},{3,1},{4,6},{5,7},{6,4},{7,5},{8,10},{9,11},{10,... | collective-permute-start | bytes 786440 | tf_op jit(solution)/shard_map/ppermute | solution.py:229
  32.6 11.4 %collective-permute-start.13 = (bf16[32,5120]{1,0:T(8,128)(2,1)S(1)}, bf16[32,5120]{1,0:T(8,128)(2,1)S(1)}, u32[]{:S(2)}, u32[]{:S(2)}) collective-permute-start(bf16[32,5120]{1,0:T(8,128)(2,1)S(1)} %bitcast.38), channel_id=1, source_target_pairs={{0,4},{1,5},{2,6},{3,7},{4,0},{5,1},{6,2},{7,3},{8,12},{9,13},{10,... | collective-permute-start | bytes 983048 | tf_op jit(solution)/shard_map/ppermute | solution.py:229
  37.6 5.4 %collective-permute-start.8 = (bf16[64,3072]{1,0:T(8,128)(2,1)S(1)}, bf16[64,3072]{1,0:T(8,128)(2,1)S(1)}, u32[]{:S(2)}, u32[]{:S(2)}) collective-permute-start(bf16[64,3072]{1,0:T(8,128)(2,1)S(1)} %get-tuple-element.99), channel_id=1, source_target_pairs={{0,1},{1,0},{2,3},{3,2},{4,5},{5,4},{6,7},{7,6},{8,9},{9,8},{10,11... | collective-permute-start | bytes 1179656 | tf_op jit(solution)/shard_map/ppermute | solution.py:229
  39.9 6.7 %collective-permute-start.12 = (bf16[16,4096]{1,0:T(8,128)(2,1)S(1)}, bf16[16,4096]{1,0:T(8,128)(2,1)S(1)}, u32[]{:S(2)}, u32[]{:S(2)}) collective-permute-start(bf16[16,4096]{1,0:T(8,128)(2,1)S(1)} %slice.205), channel_id=1, source_target_pairs={{0,4},{1,5},{2,6},{3,7},{4,0},{5,1},{6,2},{7,3},{8,12},{9,13},{10,... | collective-permute-start | bytes 393224 | tf_op jit(solution)/shard_map/ppermute | solution.py:229
  40.4 13.7 %collective-permute-start.16 = (bf16[8,4096]{1,0:T(8,128)(2,1)S(1)}, bf16[8,4096]{1,0:T(8,128)(2,1)S(1)}, u32[]{:S(2)}, u32[]{:S(2)}) collective-permute-start(bf16[8,4096]{1,0:T(8,128)(2,1)S(1)} %slice.210), channel_id=1, source_target_pairs={{0,8},{1,9},{2,10},{3,11},{4,12},{5,13},{6,14},{7,15},{8,0},{9,1},... | collective-permute-start | bytes 196616 | tf_op jit(solution)/shard_map/ppermute | solution.py:229
  43.1 6.4 %collective-permute-start.11 = (bf16[32,3072]{1,0:T(8,128)(2,1)S(1)}, bf16[32,3072]{1,0:T(8,128)(2,1)S(1)}, u32[]{:S(2)}, u32[]{:S(2)}) collective-permute-start(bf16[32,3072]{1,0:T(8,128)(2,1)S(1)} %slice.203), channel_id=1, source_target_pairs={{0,2},{1,3},{2,0},{3,1},{4,6},{5,7},{6,4},{7,5},{8,10},{9,11},{10,... | collective-permute-start | bytes 589832 | tf_op jit(solution)/shard_map/ppermute | solution.py:229
  44.0 15.4 %copy-start = (s32[8,16384]{1,0:T(8,128)S(1)}, s32[8,16384]{1,0:T(8,128)}, u32[]{:S(2)}) copy-start(s32[8,16384]{1,0:T(8,128)} %codes_ref.3) | copy-start | bytes 1572868
  44.0 15.4 %copy-start.2 = (s32[8,128]{1,0:T(8,128)S(1)}, s32[8,128]{1,0:T(8,128)}, u32[]{:S(2)}) copy-start(s32[8,128]{1,0:T(8,128)} %exponents_ref.3) | copy-start | bytes 12292
  46.7 5.7 %collective-permute-start.17 = (bf16[16,5120]{1,0:T(8,128)(2,1)S(1)}, bf16[16,5120]{1,0:T(8,128)(2,1)S(1)}, u32[]{:S(2)}, u32[]{:S(2)}) collective-permute-start(bf16[16,5120]{1,0:T(8,128)(2,1)S(1)} %slice.204), channel_id=1, source_target_pairs={{0,2},{1,3},{2,0},{3,1},{4,6},{5,7},{6,4},{7,5},{8,10},{9,11},{10,... | collective-permute-start | bytes 491528 | tf_op jit(solution)/shard_map/ppermute | solution.py:229
  47.6 6.5 %collective-permute-start.15 = (bf16[8,4096]{1,0:T(8,128)(2,1)S(1)}, bf16[8,4096]{1,0:T(8,128)(2,1)S(1)}, u32[]{:S(2)}, u32[]{:S(2)}) collective-permute-start(bf16[8,4096]{1,0:T(8,128)(2,1)S(1)} %slice.209), channel_id=1, source_target_pairs={{0,8},{1,9},{2,10},{3,11},{4,12},{5,13},{6,14},{7,15},{8,0},{9,1},... | collective-permute-start | bytes 196616 | tf_op jit(solution)/shard_map/ppermute | solution.py:229
  49.6 5.0 %collective-permute-start.14 = (bf16[16,3072]{1,0:T(8,128)(2,1)S(1)}, bf16[16,3072]{1,0:T(8,128)(2,1)S(1)}, u32[]{:S(2)}, u32[]{:S(2)}) collective-permute-start(bf16[16,3072]{1,0:T(8,128)(2,1)S(1)} %slice.207), channel_id=1, source_target_pairs={{0,4},{1,5},{2,6},{3,7},{4,0},{5,1},{6,2},{7,3},{8,12},{9,13},{10,... | collective-permute-start | bytes 294920 | tf_op jit(solution)/shard_map/ppermute | solution.py:229
  52.5 7.0 %collective-permute-start.19 = (bf16[8,5120]{1,0:T(8,128)(2,1)S(1)}, bf16[8,5120]{1,0:T(8,128)(2,1)S(1)}, u32[]{:S(2)}, u32[]{:S(2)}) collective-permute-start(bf16[8,5120]{1,0:T(8,128)(2,1)S(1)} %slice.208), channel_id=1, source_target_pairs={{0,8},{1,9},{2,10},{3,11},{4,12},{5,13},{6,14},{7,15},{8,0},{9,1},... | collective-permute-start | bytes 245768 | tf_op jit(solution)/shard_map/ppermute | solution.py:229
  54.7 5.2 %collective-permute-start.18 = (bf16[8,3072]{1,0:T(8,128)(2,1)S(1)}, bf16[8,3072]{1,0:T(8,128)(2,1)S(1)}, u32[]{:S(2)}, u32[]{:S(2)}) collective-permute-start(bf16[8,3072]{1,0:T(8,128)(2,1)S(1)} %slice.211), channel_id=1, source_target_pairs={{0,8},{1,9},{2,10},{3,11},{4,12},{5,13},{6,14},{7,15},{8,0},{9,1},... | collective-permute-start | bytes 147464 | tf_op jit(solution)/shard_map/ppermute | solution.py:229
  (5 other events, 17.0 us)

commit v5 on v4

--- a/solution.py
+++ b/solution.py
@@ -15,11 +15,11 @@
 masked_score = -1e30
 
 LIMIT = 12 << 20
-PARTS = ((4, 'yz', 8), (4, 'yz', 3), (5, 'zyz', 0), (3, 'yz', 3))
-AHEAD = (4, 3, 1)
+PARTS = ((4, 'yz', 0), (4, 'yz', 0), (5, 'zyz', 3), (3, 'yz', 3))
+AHEAD = (4, 4, 3)
 TILE = 512
 SPLIT = {}
-EVENTS = ((0, 0), (1, -1), (0, 1), (1, 0), (2, 0), (0, 2), (1, 1), (2, 1), (3, -1), (3, 0), (1, 2), (0, 3), (3, 1), (2, 2), (1, 3), (3, 2), (2, 3), (0, 4), (1, 4), (3, 3), (2, 4), (3, 4))
+EVENTS = ((0, 0), (2, -1), (0, 1), (1, 0), (2, 0), (0, 2), (1, 1), (2, 1), (3, -1), (3, 0), (1, 2), (3, 1), (0, 3), (2, 2), (1, 3), (3, 2), (2, 3), (0, 4), (1, 4), (3, 3), (2, 4), (3, 4))
 
 
 def events(bits):
@@ -105,14 +105,14 @@
     send_ref[:, columns] = product[half:].astype(jnp.bfloat16)
 
 
-def part_kernel(bits, start, with_attention, *refs):
+def part_kernel(bits, start, with_attention, ranges, *refs):
     if with_attention:
         place_ref, queries_ref, kv_ref, w_ref, *refs = refs
         *ahead_refs, context_ref, keep_ref, send_ref, buffer, arrived = refs
     else:
         context_ref, w_ref, *refs = refs
         *ahead_refs, keep_ref, send_ref, buffer, arrived = refs
-    tiles = [(ref, index) for ref in ahead_refs for index in range(ref.shape[0])]
+    tiles = [(ref, index) for ref, (first, last) in zip(ahead_refs, ranges) for index in range(first, last)]
     missing = keep_ref.shape[1] // TILE - len(tiles)
     copies = fetches(start + len(tiles) * TILE, w_ref, buffer, arrived) if missing else []
     for copy in copies:
@@ -158,7 +158,8 @@
     with_attention = context is None
     depth = weight.shape[0]
     total_rows = (first_inputs[1] if with_attention else context).shape[0]
-    missing = max(columns // TILE - sum(array.shape[0] for array in ahead), 1)
+    ranges = [(first, last) for _, first, last in ahead]
+    missing = max(columns // TILE - sum(last - first for first, last in ranges), 1)
     out_shape = [
         jax.ShapeDtypeStruct((total_rows // 2, columns), jnp.float32),
         jax.ShapeDtypeStruct((total_rows // 2, columns), jnp.bfloat16),
@@ -168,13 +169,13 @@
         out_shape = [jax.ShapeDtypeStruct((total_rows, depth), jnp.bfloat16)] + out_shape
         inputs, in_specs = [*first_inputs, weight], [SMEM, VMEM, VMEM, ANYWHERE]
     return pl.pallas_call(
-        functools.partial(part_kernel, bits, start, with_attention),
+        functools.partial(part_kernel, bits, start, with_attention, ranges),
         in_specs=in_specs + [VMEM] * len(ahead),
         out_specs=[VMEM] * len(out_shape),
         out_shape=out_shape,
         scratch_shapes=[pltpu.VMEM((missing, depth, TILE), jnp.bfloat16), pltpu.SemaphoreType.DMA((missing,))],
         compiler_params=pltpu.CompilerParams(vmem_limit_bytes=LIMIT),
-    )(*inputs, *ahead)
+    )(*inputs, *(array for array, _, _ in ahead))
 
 
 def finish_kernel(bounds, is_last, codes_ref, exponents_ref, *refs):
@@ -293,7 +294,15 @@
 
     context = token = None
     state = {}
-    fetched = {0: ahead}
+    fetched = {}
+    first = 0
+    for array in ahead:
+        for part, (columns, *_) in enumerate(PARTS):
+            begin, end = starts[part] // TILE, (starts[part] + columns * unit) // TILE
+            lowest, highest = max(begin, first), min(end, first + array.shape[0])
+            if lowest < highest:
+                fetched.setdefault(part, []).append((array, lowest - first, highest - first))
+        first += array.shape[0]
 
     def summed_halves(part, step):
         nonlocal token
@@ -319,11 +328,11 @@
         if step == -1:
             now = place if token is None else lax.optimization_barrier((place, token))[0]
             token = fetch(now, weight, starts[part], tiles)
-            fetched[part] = [token]
+            fetched[part] = [(token, 0, tiles)]
             continue
         if step == 0:
             if context is None:
-                context, keep, send = project_part(bits, starts[part], columns, None, (place, queries, kv), weight, ahead)
+                context, keep, send = project_part(bits, starts[part], columns, None, (place, queries, kv), weight, fetched[0])
             else:
                 held, token = lax.optimization_barrier((context, token))
                 keep, send = project_part(bits, starts[part], columns, held, None, weight, fetched.get(part, []))

time: 61.2 us -> 60.4 us (0.987)
  waiting for transfers between devices: 11.5 us -> 9.9 us
  starting transfers between devices: 24.5 us -> 25.2 us
    ppermute x20, waiting for transfers between devices: 11.5 us -> 9.9 us  [passed_across(): lax.ppermute(value, axis, [(source, source ^ mask) for source in range(la...]
    pallas_call x4, Pallas kernels: 11.6 us -> 10.6 us  [project_part(): pl.pallas_call(functools.partial(part_kernel, bits, start, with_attention...]
    pallas_call x5, Pallas kernels: 9.15 us -> 10.2 us  [fetch(): pl.pallas_call(functools.partial(fetch_kernel, start), in_specs=[SMEM, AN...]
    ppermute x20, starting transfers between devices: 24.5 us -> 25.2 us  [passed_across(): lax.ppermute(value, axis, [(source, source ^ mask) for source in range(la...]
  transfers between devices with their start and end apart: 20 -> 20, of which waited for: 10 -> 8; matrix products, arithmetic and copies ran while one was open for 2% -> 2% of each run, Pallas kernels for 32% -> 33%
where the time goes in v5:
time: 60.4 us; the launch traced here: 60 us
  starting transfers between devices  25.2 us (42%)
  Pallas kernels  22.4 us (37%)
  waiting for transfers between devices  9.9 us (16%)
  other arithmetic  1.56 us (3%)
    ppermute x20, starting transfers between devices, passed_across(): lax.ppermute(value, axis, [(source, source ^ mask) for source in range(la...  25.2 us
    pallas_call x4, Pallas kernels, project_part(): pl.pallas_call(functools.partial(part_kernel, bits, start, with_attention...  10.6 us
    pallas_call x5, Pallas kernels, fetch(): pl.pallas_call(functools.partial(fetch_kernel, start), in_specs=[SMEM, AN...  10.2 us
    ppermute x20, waiting for transfers between devices, passed_across(): lax.ppermute(value, axis, [(source, source ^ mask) for source in range(la...  9.9 us
    pallas_call x2, Pallas kernels, finish(): pl.pallas_call(functools.partial(finish_kernel, bounds, is_last), in_spec...  1.28 us
  transfers between devices with their start and end apart: 20, of which 8 were waited for; matrix products, arithmetic and copies ran while one was open for 2% of the time, Pallas kernels for 33%

profile of v5, /device:TPU:0, one launch (start us, length us, event | category | flops | bytes accessed | tf_op | source)
XLA Modules:
  0.0 60.0 jit_solution(8102468023539794981)
XLA Ops:
  0.8 3.0 %collective-permute-start = (bf16[4,1,8,256]{3,2,1,0:T(8,128)(2,1)S(1)}, bf16[4,1,8,256]{3,2,1,0:T(8,128)(2,1)S(1)}, u32[]{:S(2)}, u32[]{:S(2)}) collective-permute-start(bf16[4,1,8,256]{3,2,1,0:T(8,128)(2,1)S(1)} %get-tuple-element.131), channel_id=1, source_target_pairs={{0,2},{1,3},{2,0},{3,1},{4,6},{5,7},{6,4},{7,5},{8,10},{9,11},{10,... | collective-permute-start | bytes 49160 | tf_op jit(solution)/shard_map/ppermute | solution.py:230
  3.8 2.2 %shard_map.66.refs_4_ = bf16[4,1024,512]{2,1,0:T(8,128)(2,1)S(1)} custom-call(s32[1]{0:T(128)} %bitcast.place_ref.refs_0_, bf16[1024,16384]{1,0:T(8,128)(2,1)} %refs_1_.5), custom_call_target="tpu_custom_call" | custom-call | tf_op jit(solution)/shard_map/pallas_call | solution.py:147
  6.1 1.6 %collective-permute-start.1 = (bf16[2,2,8,256]{3,2,1,0:T(8,128)(2,1)S(1)}, bf16[2,2,8,256]{3,2,1,0:T(8,128)(2,1)S(1)}, u32[]{:S(2)}, u32[]{:S(2)}) collective-permute-start(bf16[2,2,8,256]{3,2,1,0:T(8,128)(2,1)S(1)} %get-tuple-element.129), channel_id=1, source_target_pairs={{0,4},{1,5},{2,6},{3,7},{4,0},{5,1},{6,2},{7,3},{8,12},{9,13},{10,... | collective-permute-start | bytes 49160 | tf_op jit(solution)/shard_map/ppermute | solution.py:230
  7.7 2.2 %shard_map.67.refs_5_ = bf16[4,1024,512]{2,1,0:T(8,128)(2,1)S(1)} custom-call(s32[1]{0:T(128)} %bitcast.place_ref.refs_0_, bf16[1024,16384]{1,0:T(8,128)(2,1)} %refs_1_.5), custom_call_target="tpu_custom_call" | custom-call | tf_op jit(solution)/shard_map/pallas_call | solution.py:147
  10.0 2.7 %collective-permute-start.2 = (bf16[1,4,8,256]{3,2,1,0:T(8,128)(2,1)S(1)}, bf16[1,4,8,256]{3,2,1,0:T(8,128)(2,1)S(1)}, u32[]{:S(2)}, u32[]{:S(2)}) collective-permute-start(bf16[1,4,8,256]{3,2,1,0:T(8,128)(2,1)S(1)} %get-tuple-element.127), channel_id=1, source_target_pairs={{0,8},{1,9},{2,10},{3,11},{4,12},{5,13},{6,14},{7,15},{8,0},{9,1},... | collective-permute-start | bytes 49160 | tf_op jit(solution)/shard_map/ppermute | solution.py:230
  12.7 1.9 %shard_map.68.refs_2_ = bf16[3,1024,512]{2,1,0:T(8,128)(2,1)S(1)} custom-call(s32[1]{0:T(128)} %bitcast.place_ref.refs_0_, bf16[1024,16384]{1,0:T(8,128)(2,1)} %refs_1_.5), custom_call_target="tpu_custom_call" | custom-call | tf_op jit(solution)/shard_map/pallas_call | solution.py:147
  16.0 1.8 %shard_map.69 = (bf16[128,1024]{1,0:T(8,128)(2,1)S(1)}, f32[64,4096]{1,0:T(8,128)S(1)}, bf16[64,4096]{1,0:T(8,128)(2,1)S(1)}) custom-call(s32[1]{0:T(128)} %bitcast.place_ref.refs_0_, bf16[128,1024]{1,0:T(8,128)(2,1)S(1)} %shard_map.64.refs_1_, bf16[128,256]{1,0:T(8,128)(2,1)S(1)} %maximum_bitcast_fusion.refs_2_, bf16[1024,16384]{1,0:T(8,128)(2,1)} %refs_1_.5, ...), custom_call_target="tpu_custom_call" | custom-call | tf_op jit(solution)/shard_map/pallas_call | solution.py:171
  18.0 1.9 %shard_map.70.refs_2_ = bf16[3,1024,512]{2,1,0:T(8,128)(2,1)S(1)} custom-call(s32[1]{0:T(128)} %bitcast.place_ref.refs_0_, bf16[1024,16384]{1,0:T(8,128)(2,1)} %refs_1_.5), custom_call_target="tpu_custom_call" | custom-call | tf_op jit(solution)/shard_map/pallas_call | solution.py:147
  20.1 1.5 %collective-permute-start.7 = (bf16[32,4096]{1,0:T(8,128)(2,1)S(1)}, bf16[32,4096]{1,0:T(8,128)(2,1)S(1)}, u32[]{:S(2)}, u32[]{:S(2)}) collective-permute-start(bf16[32,4096]{1,0:T(8,128)(2,1)S(1)} %slice.202), channel_id=1, source_target_pairs={{0,2},{1,3},{2,0},{3,1},{4,6},{5,7},{6,4},{7,5},{8,10},{9,11},{10,... | collective-permute-start | bytes 786440 | tf_op jit(solution)/shard_map/ppermute | solution.py:230
  21.6 2.9 %shard_map.71 = (f32[64,4096]{1,0:T(8,128)S(1)}, bf16[64,4096]{1,0:T(8,128)(2,1)S(1)}) custom-call(bf16[128,1024]{1,0:T(8,128)(2,1)S(1)} %get-tuple-element.97.refs_0_, bf16[1024,16384]{1,0:T(8,128)(2,1)} %refs_1_.5, bf16[3,1024,512]{2,1,0:T(8,128)(2,1)S(1)} %shard_map.68.refs_2_), custom_call_target="tpu_custom_call" | custom-call | tf_op jit(solution)/shard_map/pallas_call | solution.py:171
  24.7 3.6 %shard_map.72 = (f32[64,5120]{1,0:T(8,128)S(1)}, bf16[64,5120]{1,0:T(8,128)(2,1)S(1)}) custom-call(bf16[128,1024]{1,0:T(8,128)(2,1)S(1)} %get-tuple-element.97.refs_0_, bf16[1024,16384]{1,0:T(8,128)(2,1)} %refs_1_.5, bf16[3,1024,512]{2,1,0:T(8,128)(2,1)S(1)} %shard_map.70.refs_2_), custom_call_target="tpu_custom_call" | custom-call | tf_op jit(solution)/shard_map/pallas_call | solution.py:171
  28.9 1.6 %collective-permute-start.13 = (bf16[16,4096]{1,0:T(8,128)(2,1)S(1)}, bf16[16,4096]{1,0:T(8,128)(2,1)S(1)}, u32[]{:S(2)}, u32[]{:S(2)}) collective-permute-start(bf16[16,4096]{1,0:T(8,128)(2,1)S(1)} %slice.206), channel_id=1, source_target_pairs={{0,4},{1,5},{2,6},{3,7},{4,0},{5,1},{6,2},{7,3},{8,12},{9,13},{10,... | collective-permute-start | bytes 393224 | tf_op jit(solution)/shard_map/ppermute | solution.py:230
  30.6 1.5 %collective-permute-start.9 = (bf16[32,4096]{1,0:T(8,128)(2,1)S(1)}, bf16[32,4096]{1,0:T(8,128)(2,1)S(1)}, u32[]{:S(2)}, u32[]{:S(2)}) collective-permute-start(bf16[32,4096]{1,0:T(8,128)(2,1)S(1)} %slice.201), channel_id=1, source_target_pairs={{0,2},{1,3},{2,0},{3,1},{4,6},{5,7},{6,4},{7,5},{8,10},{9,11},{10,... | collective-permute-start | bytes 786440 | tf_op jit(solution)/shard_map/ppermute | solution.py:230
  33.0 1.9 %shard_map.73.refs_2_ = bf16[3,1024,512]{2,1,0:T(8,128)(2,1)S(1)} custom-call(s32[1]{0:T(128)} %bitcast.place_ref.refs_0_, bf16[1024,16384]{1,0:T(8,128)(2,1)} %refs_1_.5), custom_call_target="tpu_custom_call" | custom-call | tf_op jit(solution)/shard_map/pallas_call | solution.py:147
  34.9 2.3 %shard_map.74 = (f32[64,3072]{1,0:T(8,128)S(1)}, bf16[64,3072]{1,0:T(8,128)(2,1)S(1)}) custom-call(bf16[128,1024]{1,0:T(8,128)(2,1)S(1)} %get-tuple-element.97.refs_0_, bf16[1024,16384]{1,0:T(8,128)(2,1)} %refs_1_.5, bf16[3,1024,512]{2,1,0:T(8,128)(2,1)S(1)} %shard_map.73.refs_2_), custom_call_target="tpu_custom_call" | custom-call | tf_op jit(solution)/shard_map/pallas_call | solution.py:171
  37.3 1.4 %collective-permute-done.9 = bf16[32,4096]{1,0:T(8,128)(2,1)S(1)} collective-permute-done((bf16[32,4096]{1,0:T(8,128)(2,1)S(1)}, bf16[32,4096]{1,0:T(8,128)(2,1)S(1)}, u32[]{:S(2)}, u32[]{:S(2)}) %collective-permute-start.9) | collective-permute-done | bytes 262176 | tf_op jit(solution)/shard_map/ppermute | solution.py:230
  40.6 2.6 %collective-permute-start.16 = (bf16[8,4096]{1,0:T(8,128)(2,1)S(1)}, bf16[8,4096]{1,0:T(8,128)(2,1)S(1)}, u32[]{:S(2)}, u32[]{:S(2)}) collective-permute-start(bf16[8,4096]{1,0:T(8,128)(2,1)S(1)} %slice.210), channel_id=1, source_target_pairs={{0,8},{1,9},{2,10},{3,11},{4,12},{5,13},{6,14},{7,15},{8,0},{9,1},... | collective-permute-start | bytes 196616 | tf_op jit(solution)/shard_map/ppermute | solution.py:230
  43.3 1.7 %collective-permute-done.11 = bf16[16,4096]{1,0:T(8,128)(2,1)S(1)} collective-permute-done((bf16[16,4096]{1,0:T(8,128)(2,1)S(1)}, bf16[16,4096]{1,0:T(8,128)(2,1)S(1)}, u32[]{:S(2)}, u32[]{:S(2)}) %collective-permute-start.11) | collective-permute-done | bytes 131104 | tf_op jit(solution)/shard_map/ppermute | solution.py:230
  45.1 1.0 %collective-permute-start.17 = (bf16[16,5120]{1,0:T(8,128)(2,1)S(1)}, bf16[16,5120]{1,0:T(8,128)(2,1)S(1)}, u32[]{:S(2)}, u32[]{:S(2)}) collective-permute-start(bf16[16,5120]{1,0:T(8,128)(2,1)S(1)} %slice.204), channel_id=1, source_target_pairs={{0,2},{1,3},{2,0},{3,1},{4,6},{5,7},{6,4},{7,5},{8,10},{9,11},{10,... | collective-permute-start | bytes 491528 | tf_op jit(solution)/shard_map/ppermute | solution.py:230
  46.1 2.6 %collective-permute-start.15 = (bf16[8,4096]{1,0:T(8,128)(2,1)S(1)}, bf16[8,4096]{1,0:T(8,128)(2,1)S(1)}, u32[]{:S(2)}, u32[]{:S(2)}) collective-permute-start(bf16[8,4096]{1,0:T(8,128)(2,1)S(1)} %slice.209), channel_id=1, source_target_pairs={{0,8},{1,9},{2,10},{3,11},{4,12},{5,13},{6,14},{7,15},{8,0},{9,1},... | collective-permute-start | bytes 196616 | tf_op jit(solution)/shard_map/ppermute | solution.py:230
  48.7 1.2 %collective-permute-start.14 = (bf16[16,3072]{1,0:T(8,128)(2,1)S(1)}, bf16[16,3072]{1,0:T(8,128)(2,1)S(1)}, u32[]{:S(2)}, u32[]{:S(2)}) collective-permute-start(bf16[16,3072]{1,0:T(8,128)(2,1)S(1)} %slice.207), channel_id=1, source_target_pairs={{0,4},{1,5},{2,6},{3,7},{4,0},{5,1},{6,2},{7,3},{8,12},{9,13},{10,... | collective-permute-start | bytes 294920 | tf_op jit(solution)/shard_map/ppermute | solution.py:230
  50.6 2.7 %collective-permute-start.19 = (bf16[8,5120]{1,0:T(8,128)(2,1)S(1)}, bf16[8,5120]{1,0:T(8,128)(2,1)S(1)}, u32[]{:S(2)}, u32[]{:S(2)}) collective-permute-start(bf16[8,5120]{1,0:T(8,128)(2,1)S(1)} %slice.208), channel_id=1, source_target_pairs={{0,8},{1,9},{2,10},{3,11},{4,12},{5,13},{6,14},{7,15},{8,0},{9,1},... | collective-permute-start | bytes 245768 | tf_op jit(solution)/shard_map/ppermute | solution.py:230
  54.3 1.8 %collective-permute-done.19.refs_5_ = bf16[8,5120]{1,0:T(8,128)(2,1)S(1)} collective-permute-done((bf16[8,5120]{1,0:T(8,128)(2,1)S(1)}, bf16[8,5120]{1,0:T(8,128)(2,1)S(1)}, u32[]{:S(2)}, u32[]{:S(2)}) %collective-permute-start.19) | collective-permute-done | bytes 81952 | tf_op jit(solution)/shard_map/ppermute | solution.py:230
  56.5 2.6 %collective-permute-done.18.refs_1_ = bf16[8,3072]{1,0:T(8,128)(2,1)S(1)} collective-permute-done((bf16[8,3072]{1,0:T(8,128)(2,1)S(1)}, bf16[8,3072]{1,0:T(8,128)(2,1)S(1)}, u32[]{:S(2)}, u32[]{:S(2)}) %collective-permute-start.18) | collective-permute-done | bytes 49184 | tf_op jit(solution)/shard_map/ppermute | solution.py:230
  (89 shorter events, 9.3 us)
Async XLA Ops:
  0.8 5.3 %collective-permute-start = (bf16[4,1,8,256]{3,2,1,0:T(8,128)(2,1)S(1)}, bf16[4,1,8,256]{3,2,1,0:T(8,128)(2,1)S(1)}, u32[]{:S(2)}, u32[]{:S(2)}) collective-permute-start(bf16[4,1,8,256]{3,2,1,0:T(8,128)(2,1)S(1)} %get-tuple-element.131), channel_id=1, source_target_pairs={{0,2},{1,3},{2,0},{3,1},{4,6},{5,7},{6,4},{7,5},{8,10},{9,11},{10,... | collective-permute-start | bytes 49160 | tf_op jit(solution)/shard_map/ppermute | solution.py:230
  6.1 3.9 %collective-permute-start.1 = (bf16[2,2,8,256]{3,2,1,0:T(8,128)(2,1)S(1)}, bf16[2,2,8,256]{3,2,1,0:T(8,128)(2,1)S(1)}, u32[]{:S(2)}, u32[]{:S(2)}) collective-permute-start(bf16[2,2,8,256]{3,2,1,0:T(8,128)(2,1)S(1)} %get-tuple-element.129), channel_id=1, source_target_pairs={{0,4},{1,5},{2,6},{3,7},{4,0},{5,1},{6,2},{7,3},{8,12},{9,13},{10,... | collective-permute-start | bytes 49160 | tf_op jit(solution)/shard_map/ppermute | solution.py:230
  10.0 4.7 %copy-start.1 = (bf16[128,1024]{1,0:T(8,128)(2,1)S(1)}, bf16[128,1024]{1,0:T(8,128)(2,1)}, u32[]{:S(2)}) copy-start(bf16[128,1024]{1,0:T(8,128)(2,1)} %q_ref.1) | copy-start | bytes 786436
  10.0 4.7 %collective-permute-start.2 = (bf16[1,4,8,256]{3,2,1,0:T(8,128)(2,1)S(1)}, bf16[1,4,8,256]{3,2,1,0:T(8,128)(2,1)S(1)}, u32[]{:S(2)}, u32[]{:S(2)}) collective-permute-start(bf16[1,4,8,256]{3,2,1,0:T(8,128)(2,1)S(1)} %get-tuple-element.127), channel_id=1, source_target_pairs={{0,8},{1,9},{2,10},{3,11},{4,12},{5,13},{6,14},{7,15},{8,0},{9,1},... | collective-permute-start | bytes 49160 | tf_op jit(solution)/shard_map/ppermute | solution.py:230
  14.7 1.2 %collective-permute-start.3 = (bf16[8,8,256]{2,1,0:T(8,128)(2,1)S(1)}, bf16[8,8,256]{2,1,0:T(8,128)(2,1)S(1)}, u32[]{:S(2)}, u32[]{:S(2)}) collective-permute-start(bf16[8,8,256]{2,1,0:T(8,128)(2,1)S(1)} %maximum_bitcast_fusion.2), channel_id=1, source_target_pairs={{0,1},{1,0},{2,3},{3,2},{4,5},{5,4},{6,7},{7,6},{8,9},{9,8},{10,11... | collective-permute-start | bytes 98312 | tf_op jit(solution)/shard_map/ppermute | solution.py:230
  17.8 2.1 %collective-permute-start.4 = (bf16[64,4096]{1,0:T(8,128)(2,1)S(1)}, bf16[64,4096]{1,0:T(8,128)(2,1)S(1)}, u32[]{:S(2)}, u32[]{:S(2)}) collective-permute-start(bf16[64,4096]{1,0:T(8,128)(2,1)S(1)} %get-tuple-element.79), channel_id=1, source_target_pairs={{0,1},{1,0},{2,3},{3,2},{4,5},{5,4},{6,7},{7,6},{8,9},{9,8},{10,11... | collective-permute-start | bytes 1572872 | tf_op jit(solution)/shard_map/ppermute | solution.py:230
  20.1 4.5 %copy-start.3 = (f32[64,4096]{1,0:T(8,128)}, f32[64,4096]{1,0:T(8,128)S(1)}, u32[]{:S(2)}) copy-start(f32[64,4096]{1,0:T(8,128)S(1)} %convert_add_fusion.2) | copy-start | bytes 3145732
  20.1 8.7 %collective-permute-start.7 = (bf16[32,4096]{1,0:T(8,128)(2,1)S(1)}, bf16[32,4096]{1,0:T(8,128)(2,1)S(1)}, u32[]{:S(2)}, u32[]{:S(2)}) collective-permute-start(bf16[32,4096]{1,0:T(8,128)(2,1)S(1)} %slice.202), channel_id=1, source_target_pairs={{0,2},{1,3},{2,0},{3,1},{4,6},{5,7},{6,4},{7,5},{8,10},{9,11},{10,... | collective-permute-start | bytes 786440 | tf_op jit(solution)/shard_map/ppermute | solution.py:230
  24.6 5.9 %collective-permute-start.6 = (bf16[64,4096]{1,0:T(8,128)(2,1)S(1)}, bf16[64,4096]{1,0:T(8,128)(2,1)S(1)}, u32[]{:S(2)}, u32[]{:S(2)}) collective-permute-start(bf16[64,4096]{1,0:T(8,128)(2,1)S(1)} %get-tuple-element.85), channel_id=1, source_target_pairs={{0,1},{1,0},{2,3},{3,2},{4,5},{5,4},{6,7},{7,6},{8,9},{9,8},{10,11... | collective-permute-start | bytes 1572872 | tf_op jit(solution)/shard_map/ppermute | solution.py:230
  28.3 3.8 %collective-permute-start.5 = (bf16[64,5120]{1,0:T(8,128)(2,1)S(1)}, bf16[64,5120]{1,0:T(8,128)(2,1)S(1)}, u32[]{:S(2)}, u32[]{:S(2)}) collective-permute-start(bf16[64,5120]{1,0:T(8,128)(2,1)S(1)} %get-tuple-element.88), channel_id=1, source_target_pairs={{0,1},{1,0},{2,3},{3,2},{4,5},{5,4},{6,7},{7,6},{8,9},{9,8},{10,11... | collective-permute-start | bytes 1966088 | tf_op jit(solution)/shard_map/ppermute | solution.py:230
  28.9 10.7 %collective-permute-start.13 = (bf16[16,4096]{1,0:T(8,128)(2,1)S(1)}, bf16[16,4096]{1,0:T(8,128)(2,1)S(1)}, u32[]{:S(2)}, u32[]{:S(2)}) collective-permute-start(bf16[16,4096]{1,0:T(8,128)(2,1)S(1)} %slice.206), channel_id=1, source_target_pairs={{0,4},{1,5},{2,6},{3,7},{4,0},{5,1},{6,2},{7,3},{8,12},{9,13},{10,... | collective-permute-start | bytes 393224 | tf_op jit(solution)/shard_map/ppermute | solution.py:230
  30.6 8.1 %collective-permute-start.9 = (bf16[32,4096]{1,0:T(8,128)(2,1)S(1)}, bf16[32,4096]{1,0:T(8,128)(2,1)S(1)}, u32[]{:S(2)}, u32[]{:S(2)}) collective-permute-start(bf16[32,4096]{1,0:T(8,128)(2,1)S(1)} %slice.201), channel_id=1, source_target_pairs={{0,2},{1,3},{2,0},{3,1},{4,6},{5,7},{6,4},{7,5},{8,10},{9,11},{10,... | collective-permute-start | bytes 786440 | tf_op jit(solution)/shard_map/ppermute | solution.py:230
  32.4 10.8 %collective-permute-start.12 = (bf16[32,5120]{1,0:T(8,128)(2,1)S(1)}, bf16[32,5120]{1,0:T(8,128)(2,1)S(1)}, u32[]{:S(2)}, u32[]{:S(2)}) collective-permute-start(bf16[32,5120]{1,0:T(8,128)(2,1)S(1)} %bitcast.38), channel_id=1, source_target_pairs={{0,4},{1,5},{2,6},{3,7},{4,0},{5,1},{6,2},{7,3},{8,12},{9,13},{10,... | collective-permute-start | bytes 983048 | tf_op jit(solution)/shard_map/ppermute | solution.py:230
  37.2 2.2 %collective-permute-start.8 = (bf16[64,3072]{1,0:T(8,128)(2,1)S(1)}, bf16[64,3072]{1,0:T(8,128)(2,1)S(1)}, u32[]{:S(2)}, u32[]{:S(2)}) collective-permute-start(bf16[64,3072]{1,0:T(8,128)(2,1)S(1)} %get-tuple-element.99), channel_id=1, source_target_pairs={{0,1},{1,0},{2,3},{3,2},{4,5},{5,4},{6,7},{7,6},{8,9},{9,8},{10,11... | collective-permute-start | bytes 1179656 | tf_op jit(solution)/shard_map/ppermute | solution.py:230
  38.8 6.2 %collective-permute-start.11 = (bf16[16,4096]{1,0:T(8,128)(2,1)S(1)}, bf16[16,4096]{1,0:T(8,128)(2,1)S(1)}, u32[]{:S(2)}, u32[]{:S(2)}) collective-permute-start(bf16[16,4096]{1,0:T(8,128)(2,1)S(1)} %slice.205), channel_id=1, source_target_pairs={{0,4},{1,5},{2,6},{3,7},{4,0},{5,1},{6,2},{7,3},{8,12},{9,13},{10,... | collective-permute-start | bytes 393224 | tf_op jit(solution)/shard_map/ppermute | solution.py:230
  39.6 9.0 %collective-permute-start.10 = (bf16[32,3072]{1,0:T(8,128)(2,1)S(1)}, bf16[32,3072]{1,0:T(8,128)(2,1)S(1)}, u32[]{:S(2)}, u32[]{:S(2)}) collective-permute-start(bf16[32,3072]{1,0:T(8,128)(2,1)S(1)} %slice.203), channel_id=1, source_target_pairs={{0,2},{1,3},{2,0},{3,1},{4,6},{5,7},{6,4},{7,5},{8,10},{9,11},{10,... | collective-permute-start | bytes 589832 | tf_op jit(solution)/shard_map/ppermute | solution.py:230
  40.6 12.7 %collective-permute-start.16 = (bf16[8,4096]{1,0:T(8,128)(2,1)S(1)}, bf16[8,4096]{1,0:T(8,128)(2,1)S(1)}, u32[]{:S(2)}, u32[]{:S(2)}) collective-permute-start(bf16[8,4096]{1,0:T(8,128)(2,1)S(1)} %slice.210), channel_id=1, source_target_pairs={{0,8},{1,9},{2,10},{3,11},{4,12},{5,13},{6,14},{7,15},{8,0},{9,1},... | collective-permute-start | bytes 196616 | tf_op jit(solution)/shard_map/ppermute | solution.py:230
  43.3 12.8 %copy-start = (s32[8,16384]{1,0:T(8,128)S(1)}, s32[8,16384]{1,0:T(8,128)}, u32[]{:S(2)}) copy-start(s32[8,16384]{1,0:T(8,128)} %codes_ref.3) | copy-start | bytes 1572868
  43.3 12.8 %copy-start.2 = (s32[8,128]{1,0:T(8,128)S(1)}, s32[8,128]{1,0:T(8,128)}, u32[]{:S(2)}) copy-start(s32[8,128]{1,0:T(8,128)} %exponents_ref.3) | copy-start | bytes 12292
  45.1 5.4 %collective-permute-start.17 = (bf16[16,5120]{1,0:T(8,128)(2,1)S(1)}, bf16[16,5120]{1,0:T(8,128)(2,1)S(1)}, u32[]{:S(2)}, u32[]{:S(2)}) collective-permute-start(bf16[16,5120]{1,0:T(8,128)(2,1)S(1)} %slice.204), channel_id=1, source_target_pairs={{0,2},{1,3},{2,0},{3,1},{4,6},{5,7},{6,4},{7,5},{8,10},{9,11},{10,... | collective-permute-start | bytes 491528 | tf_op jit(solution)/shard_map/ppermute | solution.py:230
  46.1 7.2 %collective-permute-start.15 = (bf16[8,4096]{1,0:T(8,128)(2,1)S(1)}, bf16[8,4096]{1,0:T(8,128)(2,1)S(1)}, u32[]{:S(2)}, u32[]{:S(2)}) collective-permute-start(bf16[8,4096]{1,0:T(8,128)(2,1)S(1)} %slice.209), channel_id=1, source_target_pairs={{0,8},{1,9},{2,10},{3,11},{4,12},{5,13},{6,14},{7,15},{8,0},{9,1},... | collective-permute-start | bytes 196616 | tf_op jit(solution)/shard_map/ppermute | solution.py:230
  48.7 5.3 %collective-permute-start.14 = (bf16[16,3072]{1,0:T(8,128)(2,1)S(1)}, bf16[16,3072]{1,0:T(8,128)(2,1)S(1)}, u32[]{:S(2)}, u32[]{:S(2)}) collective-permute-start(bf16[16,3072]{1,0:T(8,128)(2,1)S(1)} %slice.207), channel_id=1, source_target_pairs={{0,4},{1,5},{2,6},{3,7},{4,0},{5,1},{6,2},{7,3},{8,12},{9,13},{10,... | collective-permute-start | bytes 294920 | tf_op jit(solution)/shard_map/ppermute | solution.py:230
  50.6 5.5 %collective-permute-start.19 = (bf16[8,5120]{1,0:T(8,128)(2,1)S(1)}, bf16[8,5120]{1,0:T(8,128)(2,1)S(1)}, u32[]{:S(2)}, u32[]{:S(2)}) collective-permute-start(bf16[8,5120]{1,0:T(8,128)(2,1)S(1)} %slice.208), channel_id=1, source_target_pairs={{0,8},{1,9},{2,10},{3,11},{4,12},{5,13},{6,14},{7,15},{8,0},{9,1},... | collective-permute-start | bytes 245768 | tf_op jit(solution)/shard_map/ppermute | solution.py:230
  54.1 5.1 %collective-permute-start.18 = (bf16[8,3072]{1,0:T(8,128)(2,1)S(1)}, bf16[8,3072]{1,0:T(8,128)(2,1)S(1)}, u32[]{:S(2)}, u32[]{:S(2)}) collective-permute-start(bf16[8,3072]{1,0:T(8,128)(2,1)S(1)} %slice.211), channel_id=1, source_target_pairs={{0,8},{1,9},{2,10},{3,11},{4,12},{5,13},{6,14},{7,15},{8,0},{9,1},... | collective-permute-start | bytes 147464 | tf_op jit(solution)/shard_map/ppermute | solution.py:230
  (5 other events, 15.5 us)

commit v6 on v5

--- a/solution.py
+++ b/solution.py
@@ -199,7 +199,7 @@
         blocks = width // HBLK
         rest = jnp.concatenate([summed[:, b * HBLK:(b + 1) * HBLK] for b in range(blocks)], axis=0)
         rotated = jnp.zeros_like(rest)
-        for _ in range(3):
+        for _ in range(2):
             piece = rest.astype(jnp.bfloat16)
             rotated = rotated + jnp.dot(piece, table, preferred_element_type=jnp.float32)
             rest = rest - piece.astype(jnp.float32)

time: 60.4 us -> 60.4 us (level)
  no operation moved by 1% of the time
where the time goes in v6:
time: 60.4 us; the launch traced here: 60 us
  starting transfers between devices  25.2 us (42%)
  Pallas kernels  22.3 us (37%)
  waiting for transfers between devices  9.94 us (16%)
  other arithmetic  1.56 us (3%)
    ppermute x20, starting transfers between devices, passed_across(): lax.ppermute(value, axis, [(source, source ^ mask) for source in range(la...  25.2 us
    pallas_call x4, Pallas kernels, project_part(): pl.pallas_call(functools.partial(part_kernel, bits, start, with_attention...  10.6 us
    pallas_call x5, Pallas kernels, fetch(): pl.pallas_call(functools.partial(fetch_kernel, start), in_specs=[SMEM, AN...  10.2 us
    ppermute x20, waiting for transfers between devices, passed_across(): lax.ppermute(value, axis, [(source, source ^ mask) for source in range(la...  9.94 us
    pallas_call x2, Pallas kernels, finish(): pl.pallas_call(functools.partial(finish_kernel, bounds, is_last), in_spec...  1.22 us
  transfers between devices with their start and end apart: 20, of which 8 were waited for; matrix products, arithmetic and copies ran while one was open for 2% of the time, Pallas kernels for 33%

profile of v6, /device:TPU:0, one launch (start us, length us, event | category | flops | bytes accessed | tf_op | source)
XLA Modules:
  0.0 60.0 jit_solution(12948427147602787624)
XLA Ops:
  0.8 3.0 %collective-permute-start = (bf16[4,1,8,256]{3,2,1,0:T(8,128)(2,1)S(1)}, bf16[4,1,8,256]{3,2,1,0:T(8,128)(2,1)S(1)}, u32[]{:S(2)}, u32[]{:S(2)}) collective-permute-start(bf16[4,1,8,256]{3,2,1,0:T(8,128)(2,1)S(1)} %get-tuple-element.131), channel_id=1, source_target_pairs={{0,2},{1,3},{2,0},{3,1},{4,6},{5,7},{6,4},{7,5},{8,10},{9,11},{10,... | collective-permute-start | bytes 49160 | tf_op jit(solution)/shard_map/ppermute | solution.py:230
  3.8 2.2 %shard_map.66.refs_4_ = bf16[4,1024,512]{2,1,0:T(8,128)(2,1)S(1)} custom-call(s32[1]{0:T(128)} %bitcast.place_ref.refs_0_, bf16[1024,16384]{1,0:T(8,128)(2,1)} %refs_1_.5), custom_call_target="tpu_custom_call" | custom-call | tf_op jit(solution)/shard_map/pallas_call | solution.py:147
  6.1 1.6 %collective-permute-start.1 = (bf16[2,2,8,256]{3,2,1,0:T(8,128)(2,1)S(1)}, bf16[2,2,8,256]{3,2,1,0:T(8,128)(2,1)S(1)}, u32[]{:S(2)}, u32[]{:S(2)}) collective-permute-start(bf16[2,2,8,256]{3,2,1,0:T(8,128)(2,1)S(1)} %get-tuple-element.129), channel_id=1, source_target_pairs={{0,4},{1,5},{2,6},{3,7},{4,0},{5,1},{6,2},{7,3},{8,12},{9,13},{10,... | collective-permute-start | bytes 49160 | tf_op jit(solution)/shard_map/ppermute | solution.py:230
  7.7 2.2 %shard_map.67.refs_5_ = bf16[4,1024,512]{2,1,0:T(8,128)(2,1)S(1)} custom-call(s32[1]{0:T(128)} %bitcast.place_ref.refs_0_, bf16[1024,16384]{1,0:T(8,128)(2,1)} %refs_1_.5), custom_call_target="tpu_custom_call" | custom-call | tf_op jit(solution)/shard_map/pallas_call | solution.py:147
  10.0 2.7 %collective-permute-start.2 = (bf16[1,4,8,256]{3,2,1,0:T(8,128)(2,1)S(1)}, bf16[1,4,8,256]{3,2,1,0:T(8,128)(2,1)S(1)}, u32[]{:S(2)}, u32[]{:S(2)}) collective-permute-start(bf16[1,4,8,256]{3,2,1,0:T(8,128)(2,1)S(1)} %get-tuple-element.127), channel_id=1, source_target_pairs={{0,8},{1,9},{2,10},{3,11},{4,12},{5,13},{6,14},{7,15},{8,0},{9,1},... | collective-permute-start | bytes 49160 | tf_op jit(solution)/shard_map/ppermute | solution.py:230
  12.7 1.9 %shard_map.68.refs_2_ = bf16[3,1024,512]{2,1,0:T(8,128)(2,1)S(1)} custom-call(s32[1]{0:T(128)} %bitcast.place_ref.refs_0_, bf16[1024,16384]{1,0:T(8,128)(2,1)} %refs_1_.5), custom_call_target="tpu_custom_call" | custom-call | tf_op jit(solution)/shard_map/pallas_call | solution.py:147
  16.0 1.8 %shard_map.69 = (bf16[128,1024]{1,0:T(8,128)(2,1)S(1)}, f32[64,4096]{1,0:T(8,128)S(1)}, bf16[64,4096]{1,0:T(8,128)(2,1)S(1)}) custom-call(s32[1]{0:T(128)} %bitcast.place_ref.refs_0_, bf16[128,1024]{1,0:T(8,128)(2,1)S(1)} %shard_map.64.refs_1_, bf16[128,256]{1,0:T(8,128)(2,1)S(1)} %maximum_bitcast_fusion.refs_2_, bf16[1024,16384]{1,0:T(8,128)(2,1)} %refs_1_.5, ...), custom_call_target="tpu_custom_call" | custom-call | tf_op jit(solution)/shard_map/pallas_call | solution.py:171
  18.0 1.9 %shard_map.70.refs_2_ = bf16[3,1024,512]{2,1,0:T(8,128)(2,1)S(1)} custom-call(s32[1]{0:T(128)} %bitcast.place_ref.refs_0_, bf16[1024,16384]{1,0:T(8,128)(2,1)} %refs_1_.5), custom_call_target="tpu_custom_call" | custom-call | tf_op jit(solution)/shard_map/pallas_call | solution.py:147
  20.1 1.5 %collective-permute-start.7 = (bf16[32,4096]{1,0:T(8,128)(2,1)S(1)}, bf16[32,4096]{1,0:T(8,128)(2,1)S(1)}, u32[]{:S(2)}, u32[]{:S(2)}) collective-permute-start(bf16[32,4096]{1,0:T(8,128)(2,1)S(1)} %slice.202), channel_id=1, source_target_pairs={{0,2},{1,3},{2,0},{3,1},{4,6},{5,7},{6,4},{7,5},{8,10},{9,11},{10,... | collective-permute-start | bytes 786440 | tf_op jit(solution)/shard_map/ppermute | solution.py:230
  21.6 2.9 %shard_map.71 = (f32[64,4096]{1,0:T(8,128)S(1)}, bf16[64,4096]{1,0:T(8,128)(2,1)S(1)}) custom-call(bf16[128,1024]{1,0:T(8,128)(2,1)S(1)} %get-tuple-element.97.refs_0_, bf16[1024,16384]{1,0:T(8,128)(2,1)} %refs_1_.5, bf16[3,1024,512]{2,1,0:T(8,128)(2,1)S(1)} %shard_map.68.refs_2_), custom_call_target="tpu_custom_call" | custom-call | tf_op jit(solution)/shard_map/pallas_call | solution.py:171
  24.7 3.6 %shard_map.72 = (f32[64,5120]{1,0:T(8,128)S(1)}, bf16[64,5120]{1,0:T(8,128)(2,1)S(1)}) custom-call(bf16[128,1024]{1,0:T(8,128)(2,1)S(1)} %get-tuple-element.97.refs_0_, bf16[1024,16384]{1,0:T(8,128)(2,1)} %refs_1_.5, bf16[3,1024,512]{2,1,0:T(8,128)(2,1)S(1)} %shard_map.70.refs_2_), custom_call_target="tpu_custom_call" | custom-call | tf_op jit(solution)/shard_map/pallas_call | solution.py:171
  28.9 1.6 %collective-permute-start.13 = (bf16[16,4096]{1,0:T(8,128)(2,1)S(1)}, bf16[16,4096]{1,0:T(8,128)(2,1)S(1)}, u32[]{:S(2)}, u32[]{:S(2)}) collective-permute-start(bf16[16,4096]{1,0:T(8,128)(2,1)S(1)} %slice.206), channel_id=1, source_target_pairs={{0,4},{1,5},{2,6},{3,7},{4,0},{5,1},{6,2},{7,3},{8,12},{9,13},{10,... | collective-permute-start | bytes 393224 | tf_op jit(solution)/shard_map/ppermute | solution.py:230
  30.6 1.5 %collective-permute-start.9 = (bf16[32,4096]{1,0:T(8,128)(2,1)S(1)}, bf16[32,4096]{1,0:T(8,128)(2,1)S(1)}, u32[]{:S(2)}, u32[]{:S(2)}) collective-permute-start(bf16[32,4096]{1,0:T(8,128)(2,1)S(1)} %slice.201), channel_id=1, source_target_pairs={{0,2},{1,3},{2,0},{3,1},{4,6},{5,7},{6,4},{7,5},{8,10},{9,11},{10,... | collective-permute-start | bytes 786440 | tf_op jit(solution)/shard_map/ppermute | solution.py:230
  33.0 1.9 %shard_map.73.refs_2_ = bf16[3,1024,512]{2,1,0:T(8,128)(2,1)S(1)} custom-call(s32[1]{0:T(128)} %bitcast.place_ref.refs_0_, bf16[1024,16384]{1,0:T(8,128)(2,1)} %refs_1_.5), custom_call_target="tpu_custom_call" | custom-call | tf_op jit(solution)/shard_map/pallas_call | solution.py:147
  34.9 2.3 %shard_map.74 = (f32[64,3072]{1,0:T(8,128)S(1)}, bf16[64,3072]{1,0:T(8,128)(2,1)S(1)}) custom-call(bf16[128,1024]{1,0:T(8,128)(2,1)S(1)} %get-tuple-element.97.refs_0_, bf16[1024,16384]{1,0:T(8,128)(2,1)} %refs_1_.5, bf16[3,1024,512]{2,1,0:T(8,128)(2,1)S(1)} %shard_map.73.refs_2_), custom_call_target="tpu_custom_call" | custom-call | tf_op jit(solution)/shard_map/pallas_call | solution.py:171
  37.3 1.4 %collective-permute-done.9 = bf16[32,4096]{1,0:T(8,128)(2,1)S(1)} collective-permute-done((bf16[32,4096]{1,0:T(8,128)(2,1)S(1)}, bf16[32,4096]{1,0:T(8,128)(2,1)S(1)}, u32[]{:S(2)}, u32[]{:S(2)}) %collective-permute-start.9) | collective-permute-done | bytes 262176 | tf_op jit(solution)/shard_map/ppermute | solution.py:230
  40.6 2.6 %collective-permute-start.16 = (bf16[8,4096]{1,0:T(8,128)(2,1)S(1)}, bf16[8,4096]{1,0:T(8,128)(2,1)S(1)}, u32[]{:S(2)}, u32[]{:S(2)}) collective-permute-start(bf16[8,4096]{1,0:T(8,128)(2,1)S(1)} %slice.210), channel_id=1, source_target_pairs={{0,8},{1,9},{2,10},{3,11},{4,12},{5,13},{6,14},{7,15},{8,0},{9,1},... | collective-permute-start | bytes 196616 | tf_op jit(solution)/shard_map/ppermute | solution.py:230
  43.3 1.7 %collective-permute-done.11 = bf16[16,4096]{1,0:T(8,128)(2,1)S(1)} collective-permute-done((bf16[16,4096]{1,0:T(8,128)(2,1)S(1)}, bf16[16,4096]{1,0:T(8,128)(2,1)S(1)}, u32[]{:S(2)}, u32[]{:S(2)}) %collective-permute-start.11) | collective-permute-done | bytes 131104 | tf_op jit(solution)/shard_map/ppermute | solution.py:230
  45.1 1.0 %collective-permute-start.17 = (bf16[16,5120]{1,0:T(8,128)(2,1)S(1)}, bf16[16,5120]{1,0:T(8,128)(2,1)S(1)}, u32[]{:S(2)}, u32[]{:S(2)}) collective-permute-start(bf16[16,5120]{1,0:T(8,128)(2,1)S(1)} %slice.204), channel_id=1, source_target_pairs={{0,2},{1,3},{2,0},{3,1},{4,6},{5,7},{6,4},{7,5},{8,10},{9,11},{10,... | collective-permute-start | bytes 491528 | tf_op jit(solution)/shard_map/ppermute | solution.py:230
  46.1 2.6 %collective-permute-start.15 = (bf16[8,4096]{1,0:T(8,128)(2,1)S(1)}, bf16[8,4096]{1,0:T(8,128)(2,1)S(1)}, u32[]{:S(2)}, u32[]{:S(2)}) collective-permute-start(bf16[8,4096]{1,0:T(8,128)(2,1)S(1)} %slice.209), channel_id=1, source_target_pairs={{0,8},{1,9},{2,10},{3,11},{4,12},{5,13},{6,14},{7,15},{8,0},{9,1},... | collective-permute-start | bytes 196616 | tf_op jit(solution)/shard_map/ppermute | solution.py:230
  48.7 1.2 %collective-permute-start.14 = (bf16[16,3072]{1,0:T(8,128)(2,1)S(1)}, bf16[16,3072]{1,0:T(8,128)(2,1)S(1)}, u32[]{:S(2)}, u32[]{:S(2)}) collective-permute-start(bf16[16,3072]{1,0:T(8,128)(2,1)S(1)} %slice.207), channel_id=1, source_target_pairs={{0,4},{1,5},{2,6},{3,7},{4,0},{5,1},{6,2},{7,3},{8,12},{9,13},{10,... | collective-permute-start | bytes 294920 | tf_op jit(solution)/shard_map/ppermute | solution.py:230
  50.6 2.7 %collective-permute-start.19 = (bf16[8,5120]{1,0:T(8,128)(2,1)S(1)}, bf16[8,5120]{1,0:T(8,128)(2,1)S(1)}, u32[]{:S(2)}, u32[]{:S(2)}) collective-permute-start(bf16[8,5120]{1,0:T(8,128)(2,1)S(1)} %slice.208), channel_id=1, source_target_pairs={{0,8},{1,9},{2,10},{3,11},{4,12},{5,13},{6,14},{7,15},{8,0},{9,1},... | collective-permute-start | bytes 245768 | tf_op jit(solution)/shard_map/ppermute | solution.py:230
  54.3 1.8 %collective-permute-done.19.refs_5_ = bf16[8,5120]{1,0:T(8,128)(2,1)S(1)} collective-permute-done((bf16[8,5120]{1,0:T(8,128)(2,1)S(1)}, bf16[8,5120]{1,0:T(8,128)(2,1)S(1)}, u32[]{:S(2)}, u32[]{:S(2)}) %collective-permute-start.19) | collective-permute-done | bytes 81952 | tf_op jit(solution)/shard_map/ppermute | solution.py:230
  56.4 2.7 %collective-permute-done.18.refs_1_ = bf16[8,3072]{1,0:T(8,128)(2,1)S(1)} collective-permute-done((bf16[8,3072]{1,0:T(8,128)(2,1)S(1)}, bf16[8,3072]{1,0:T(8,128)(2,1)S(1)}, u32[]{:S(2)}, u32[]{:S(2)}) %collective-permute-start.18) | collective-permute-done | bytes 49184 | tf_op jit(solution)/shard_map/ppermute | solution.py:230
  (89 shorter events, 9.3 us)
Async XLA Ops:
  0.8 5.3 %collective-permute-start = (bf16[4,1,8,256]{3,2,1,0:T(8,128)(2,1)S(1)}, bf16[4,1,8,256]{3,2,1,0:T(8,128)(2,1)S(1)}, u32[]{:S(2)}, u32[]{:S(2)}) collective-permute-start(bf16[4,1,8,256]{3,2,1,0:T(8,128)(2,1)S(1)} %get-tuple-element.131), channel_id=1, source_target_pairs={{0,2},{1,3},{2,0},{3,1},{4,6},{5,7},{6,4},{7,5},{8,10},{9,11},{10,... | collective-permute-start | bytes 49160 | tf_op jit(solution)/shard_map/ppermute | solution.py:230
  6.1 3.9 %collective-permute-start.1 = (bf16[2,2,8,256]{3,2,1,0:T(8,128)(2,1)S(1)}, bf16[2,2,8,256]{3,2,1,0:T(8,128)(2,1)S(1)}, u32[]{:S(2)}, u32[]{:S(2)}) collective-permute-start(bf16[2,2,8,256]{3,2,1,0:T(8,128)(2,1)S(1)} %get-tuple-element.129), channel_id=1, source_target_pairs={{0,4},{1,5},{2,6},{3,7},{4,0},{5,1},{6,2},{7,3},{8,12},{9,13},{10,... | collective-permute-start | bytes 49160 | tf_op jit(solution)/shard_map/ppermute | solution.py:230
  10.0 4.7 %copy-start.1 = (bf16[128,1024]{1,0:T(8,128)(2,1)S(1)}, bf16[128,1024]{1,0:T(8,128)(2,1)}, u32[]{:S(2)}) copy-start(bf16[128,1024]{1,0:T(8,128)(2,1)} %q_ref.1) | copy-start | bytes 786436
  10.0 4.7 %collective-permute-start.2 = (bf16[1,4,8,256]{3,2,1,0:T(8,128)(2,1)S(1)}, bf16[1,4,8,256]{3,2,1,0:T(8,128)(2,1)S(1)}, u32[]{:S(2)}, u32[]{:S(2)}) collective-permute-start(bf16[1,4,8,256]{3,2,1,0:T(8,128)(2,1)S(1)} %get-tuple-element.127), channel_id=1, source_target_pairs={{0,8},{1,9},{2,10},{3,11},{4,12},{5,13},{6,14},{7,15},{8,0},{9,1},... | collective-permute-start | bytes 49160 | tf_op jit(solution)/shard_map/ppermute | solution.py:230
  14.7 1.2 %collective-permute-start.3 = (bf16[8,8,256]{2,1,0:T(8,128)(2,1)S(1)}, bf16[8,8,256]{2,1,0:T(8,128)(2,1)S(1)}, u32[]{:S(2)}, u32[]{:S(2)}) collective-permute-start(bf16[8,8,256]{2,1,0:T(8,128)(2,1)S(1)} %maximum_bitcast_fusion.2), channel_id=1, source_target_pairs={{0,1},{1,0},{2,3},{3,2},{4,5},{5,4},{6,7},{7,6},{8,9},{9,8},{10,11... | collective-permute-start | bytes 98312 | tf_op jit(solution)/shard_map/ppermute | solution.py:230
  17.8 2.1 %collective-permute-start.4 = (bf16[64,4096]{1,0:T(8,128)(2,1)S(1)}, bf16[64,4096]{1,0:T(8,128)(2,1)S(1)}, u32[]{:S(2)}, u32[]{:S(2)}) collective-permute-start(bf16[64,4096]{1,0:T(8,128)(2,1)S(1)} %get-tuple-element.79), channel_id=1, source_target_pairs={{0,1},{1,0},{2,3},{3,2},{4,5},{5,4},{6,7},{7,6},{8,9},{9,8},{10,11... | collective-permute-start | bytes 1572872 | tf_op jit(solution)/shard_map/ppermute | solution.py:230
  20.1 4.5 %copy-start.3 = (f32[64,4096]{1,0:T(8,128)}, f32[64,4096]{1,0:T(8,128)S(1)}, u32[]{:S(2)}) copy-start(f32[64,4096]{1,0:T(8,128)S(1)} %convert_add_fusion.2) | copy-start | bytes 3145732
  20.1 8.7 %collective-permute-start.7 = (bf16[32,4096]{1,0:T(8,128)(2,1)S(1)}, bf16[32,4096]{1,0:T(8,128)(2,1)S(1)}, u32[]{:S(2)}, u32[]{:S(2)}) collective-permute-start(bf16[32,4096]{1,0:T(8,128)(2,1)S(1)} %slice.202), channel_id=1, source_target_pairs={{0,2},{1,3},{2,0},{3,1},{4,6},{5,7},{6,4},{7,5},{8,10},{9,11},{10,... | collective-permute-start | bytes 786440 | tf_op jit(solution)/shard_map/ppermute | solution.py:230
  24.6 5.9 %collective-permute-start.6 = (bf16[64,4096]{1,0:T(8,128)(2,1)S(1)}, bf16[64,4096]{1,0:T(8,128)(2,1)S(1)}, u32[]{:S(2)}, u32[]{:S(2)}) collective-permute-start(bf16[64,4096]{1,0:T(8,128)(2,1)S(1)} %get-tuple-element.85), channel_id=1, source_target_pairs={{0,1},{1,0},{2,3},{3,2},{4,5},{5,4},{6,7},{7,6},{8,9},{9,8},{10,11... | collective-permute-start | bytes 1572872 | tf_op jit(solution)/shard_map/ppermute | solution.py:230
  28.3 3.8 %collective-permute-start.5 = (bf16[64,5120]{1,0:T(8,128)(2,1)S(1)}, bf16[64,5120]{1,0:T(8,128)(2,1)S(1)}, u32[]{:S(2)}, u32[]{:S(2)}) collective-permute-start(bf16[64,5120]{1,0:T(8,128)(2,1)S(1)} %get-tuple-element.88), channel_id=1, source_target_pairs={{0,1},{1,0},{2,3},{3,2},{4,5},{5,4},{6,7},{7,6},{8,9},{9,8},{10,11... | collective-permute-start | bytes 1966088 | tf_op jit(solution)/shard_map/ppermute | solution.py:230
  28.9 10.7 %collective-permute-start.13 = (bf16[16,4096]{1,0:T(8,128)(2,1)S(1)}, bf16[16,4096]{1,0:T(8,128)(2,1)S(1)}, u32[]{:S(2)}, u32[]{:S(2)}) collective-permute-start(bf16[16,4096]{1,0:T(8,128)(2,1)S(1)} %slice.206), channel_id=1, source_target_pairs={{0,4},{1,5},{2,6},{3,7},{4,0},{5,1},{6,2},{7,3},{8,12},{9,13},{10,... | collective-permute-start | bytes 393224 | tf_op jit(solution)/shard_map/ppermute | solution.py:230
  30.6 8.1 %collective-permute-start.9 = (bf16[32,4096]{1,0:T(8,128)(2,1)S(1)}, bf16[32,4096]{1,0:T(8,128)(2,1)S(1)}, u32[]{:S(2)}, u32[]{:S(2)}) collective-permute-start(bf16[32,4096]{1,0:T(8,128)(2,1)S(1)} %slice.201), channel_id=1, source_target_pairs={{0,2},{1,3},{2,0},{3,1},{4,6},{5,7},{6,4},{7,5},{8,10},{9,11},{10,... | collective-permute-start | bytes 786440 | tf_op jit(solution)/shard_map/ppermute | solution.py:230
  32.4 10.8 %collective-permute-start.12 = (bf16[32,5120]{1,0:T(8,128)(2,1)S(1)}, bf16[32,5120]{1,0:T(8,128)(2,1)S(1)}, u32[]{:S(2)}, u32[]{:S(2)}) collective-permute-start(bf16[32,5120]{1,0:T(8,128)(2,1)S(1)} %bitcast.38), channel_id=1, source_target_pairs={{0,4},{1,5},{2,6},{3,7},{4,0},{5,1},{6,2},{7,3},{8,12},{9,13},{10,... | collective-permute-start | bytes 983048 | tf_op jit(solution)/shard_map/ppermute | solution.py:230
  37.2 2.2 %collective-permute-start.8 = (bf16[64,3072]{1,0:T(8,128)(2,1)S(1)}, bf16[64,3072]{1,0:T(8,128)(2,1)S(1)}, u32[]{:S(2)}, u32[]{:S(2)}) collective-permute-start(bf16[64,3072]{1,0:T(8,128)(2,1)S(1)} %get-tuple-element.99), channel_id=1, source_target_pairs={{0,1},{1,0},{2,3},{3,2},{4,5},{5,4},{6,7},{7,6},{8,9},{9,8},{10,11... | collective-permute-start | bytes 1179656 | tf_op jit(solution)/shard_map/ppermute | solution.py:230
  38.8 6.2 %collective-permute-start.11 = (bf16[16,4096]{1,0:T(8,128)(2,1)S(1)}, bf16[16,4096]{1,0:T(8,128)(2,1)S(1)}, u32[]{:S(2)}, u32[]{:S(2)}) collective-permute-start(bf16[16,4096]{1,0:T(8,128)(2,1)S(1)} %slice.205), channel_id=1, source_target_pairs={{0,4},{1,5},{2,6},{3,7},{4,0},{5,1},{6,2},{7,3},{8,12},{9,13},{10,... | collective-permute-start | bytes 393224 | tf_op jit(solution)/shard_map/ppermute | solution.py:230
  39.6 9.0 %collective-permute-start.10 = (bf16[32,3072]{1,0:T(8,128)(2,1)S(1)}, bf16[32,3072]{1,0:T(8,128)(2,1)S(1)}, u32[]{:S(2)}, u32[]{:S(2)}) collective-permute-start(bf16[32,3072]{1,0:T(8,128)(2,1)S(1)} %slice.203), channel_id=1, source_target_pairs={{0,2},{1,3},{2,0},{3,1},{4,6},{5,7},{6,4},{7,5},{8,10},{9,11},{10,... | collective-permute-start | bytes 589832 | tf_op jit(solution)/shard_map/ppermute | solution.py:230
  40.6 12.7 %collective-permute-start.16 = (bf16[8,4096]{1,0:T(8,128)(2,1)S(1)}, bf16[8,4096]{1,0:T(8,128)(2,1)S(1)}, u32[]{:S(2)}, u32[]{:S(2)}) collective-permute-start(bf16[8,4096]{1,0:T(8,128)(2,1)S(1)} %slice.210), channel_id=1, source_target_pairs={{0,8},{1,9},{2,10},{3,11},{4,12},{5,13},{6,14},{7,15},{8,0},{9,1},... | collective-permute-start | bytes 196616 | tf_op jit(solution)/shard_map/ppermute | solution.py:230
  43.3 12.8 %copy-start = (s32[8,16384]{1,0:T(8,128)S(1)}, s32[8,16384]{1,0:T(8,128)}, u32[]{:S(2)}) copy-start(s32[8,16384]{1,0:T(8,128)} %codes_ref.3) | copy-start | bytes 1572868
  43.3 12.8 %copy-start.2 = (s32[8,128]{1,0:T(8,128)S(1)}, s32[8,128]{1,0:T(8,128)}, u32[]{:S(2)}) copy-start(s32[8,128]{1,0:T(8,128)} %exponents_ref.3) | copy-start | bytes 12292
  45.1 5.4 %collective-permute-start.17 = (bf16[16,5120]{1,0:T(8,128)(2,1)S(1)}, bf16[16,5120]{1,0:T(8,128)(2,1)S(1)}, u32[]{:S(2)}, u32[]{:S(2)}) collective-permute-start(bf16[16,5120]{1,0:T(8,128)(2,1)S(1)} %slice.204), channel_id=1, source_target_pairs={{0,2},{1,3},{2,0},{3,1},{4,6},{5,7},{6,4},{7,5},{8,10},{9,11},{10,... | collective-permute-start | bytes 491528 | tf_op jit(solution)/shard_map/ppermute | solution.py:230
  46.1 7.2 %collective-permute-start.15 = (bf16[8,4096]{1,0:T(8,128)(2,1)S(1)}, bf16[8,4096]{1,0:T(8,128)(2,1)S(1)}, u32[]{:S(2)}, u32[]{:S(2)}) collective-permute-start(bf16[8,4096]{1,0:T(8,128)(2,1)S(1)} %slice.209), channel_id=1, source_target_pairs={{0,8},{1,9},{2,10},{3,11},{4,12},{5,13},{6,14},{7,15},{8,0},{9,1},... | collective-permute-start | bytes 196616 | tf_op jit(solution)/shard_map/ppermute | solution.py:230
  48.7 5.3 %collective-permute-start.14 = (bf16[16,3072]{1,0:T(8,128)(2,1)S(1)}, bf16[16,3072]{1,0:T(8,128)(2,1)S(1)}, u32[]{:S(2)}, u32[]{:S(2)}) collective-permute-start(bf16[16,3072]{1,0:T(8,128)(2,1)S(1)} %slice.207), channel_id=1, source_target_pairs={{0,4},{1,5},{2,6},{3,7},{4,0},{5,1},{6,2},{7,3},{8,12},{9,13},{10,... | collective-permute-start | bytes 294920 | tf_op jit(solution)/shard_map/ppermute | solution.py:230
  50.6 5.5 %collective-permute-start.19 = (bf16[8,5120]{1,0:T(8,128)(2,1)S(1)}, bf16[8,5120]{1,0:T(8,128)(2,1)S(1)}, u32[]{:S(2)}, u32[]{:S(2)}) collective-permute-start(bf16[8,5120]{1,0:T(8,128)(2,1)S(1)} %slice.208), channel_id=1, source_target_pairs={{0,8},{1,9},{2,10},{3,11},{4,12},{5,13},{6,14},{7,15},{8,0},{9,1},... | collective-permute-start | bytes 245768 | tf_op jit(solution)/shard_map/ppermute | solution.py:230
  54.1 5.1 %collective-permute-start.18 = (bf16[8,3072]{1,0:T(8,128)(2,1)S(1)}, bf16[8,3072]{1,0:T(8,128)(2,1)S(1)}, u32[]{:S(2)}, u32[]{:S(2)}) collective-permute-start(bf16[8,3072]{1,0:T(8,128)(2,1)S(1)} %slice.211), channel_id=1, source_target_pairs={{0,8},{1,9},{2,10},{3,11},{4,12},{5,13},{6,14},{7,15},{8,0},{9,1},... | collective-permute-start | bytes 147464 | tf_op jit(solution)/shard_map/ppermute | solution.py:230
  (5 other events, 15.5 us)
